TPU v7x, 256 devices: a whole 4x4x8 slice. The times are simulated.
256 devices in a mesh: section: 8 (over x_hi, y), seq: 32 (over z, x_lo, core).
Axes of the slice: x: 4 (x_hi: 2, x_lo: 2; x = x_hi * 2 + x_lo), y: 4, z: 8, core: 2. Of those that a mesh axis runs over, the one named last changes fastest.
Arguments:
- queries: bfloat16 [8, 256, 2688], P('section'), may hold values from -10 to 10
- keys: bfloat16 [8, 4096, 2688], P('section', 'seq'), may hold values from -10 to 10
- values: bfloat16 [8, 4096, 2688], P('section', 'seq'), may hold values from -6 to 6
- out_grad: bfloat16 [8, 256, 5280], P('section'), may hold values from -6 to 6
- w_out: bfloat16 [2688, 5280], P('seq'), may hold values from -0.125 to 0.125
- window_start: int32 [256], replicated, may hold values from 0 to 4095, as said below
Outputs:
- grad_queries: bfloat16 [8, 2688, 256], P('section', 'seq')
- grad_keys: bfloat16 [8, 4096, 2688], P('section', 'seq')
- grad_values: bfloat16 [8, 4096, 2688], P('section', 'seq')
- grad_w_out: bfloat16 [2688, 5280], P('seq', 'section')
Inputs may be any that keep to these rules, and one draw needn't show every extreme that they name: window_start[i] lies between 0 and the query's own position 3840 + i and never falls as i grows.
All inputs are finite; a program needn't handle non-finite values.
Results may differ from a plain program's by a relative error of at most 0.0088.
Values may be sent and summed in bfloat16 or wider, within the bound.
No kernel may reach another device: no remote copies, remote signals or barrier semaphores. Data moves between devices by JAX's collectives and lax.ppermute only.
A program may use at most 64 MiB of HBM per device.

v0:
```python
import jax
import jax.numpy as jnp
from jax import lax
from jax.sharding import PartitionSpec as P

HEADS = 28
HEAD_DIM = 96


NEG = -1e30


def combined_all(value, axis, join):
    pieces = jax.tree.map(lambda part: lax.all_gather(part, axis), value)
    head = jax.tree.map(lambda part: part[0], pieces)
    tail = jax.tree.map(lambda part: part[1:], pieces)
    so_far, _ = lax.scan(lambda so_far, slab: (join(so_far, slab), None), head, tail)
    return so_far


def combine_stats(first, second):
    top = jnp.maximum(first[0], second[0])
    total = first[1] * jnp.exp(first[0] - top) + second[1] * jnp.exp(second[0] - top)
    return (top, total)


def local(queries, keys, values, out_grad, w_out, window_start):
    seq_count = lax.axis_size("seq")
    place = lax.axis_index("seq")
    query = queries[0]
    key_rows = keys[0]
    value_rows = values[0]
    cotangent = out_grad[0]
    q_len = query.shape[0]
    kv_len = key_rows.shape[0]
    own_width = w_out.shape[0]
    width = HEADS * HEAD_DIM
    scale = HEAD_DIM ** (-0.5)
    qh = query.reshape(q_len, HEADS, HEAD_DIM)
    kh = key_rows.reshape(kv_len, HEADS, HEAD_DIM)
    vh = value_rows.reshape(kv_len, HEADS, HEAD_DIM)
    d_cols = lax.dot_general(
        w_out, cotangent, (((1,), (1,)), ((), ())), preferred_element_type=jnp.float32
    ).astype(jnp.bfloat16)
    d_full = lax.all_gather(d_cols, "seq", axis=0, tiled=True)
    scores = jnp.einsum("qhd,khd->hqk", qh, kh, preferred_element_type=jnp.float32) * scale
    key_pos = place * kv_len + jnp.arange(kv_len, dtype=jnp.int32)
    query_pos = kv_len * seq_count - q_len + jnp.arange(q_len, dtype=jnp.int32)
    visible = (key_pos[None, :] >= window_start[:, None]) & (key_pos[None, :] <= query_pos[:, None])
    scores = jnp.where(visible[None], scores, NEG)
    local_top = jnp.max(scores, axis=2)
    local_total = jnp.sum(jnp.exp(scores - local_top[..., None]), axis=2)
    top, total = combined_all((local_top, local_total), "seq", combine_stats)
    probs = jnp.exp(scores - top[..., None]) / total[..., None]
    probs_b = probs.astype(jnp.bfloat16)
    partial_value = jnp.einsum(
        "hqk,khd->hdq", probs_b, vh, preferred_element_type=jnp.float32
    ).reshape(width, q_len)
    dah = d_full.reshape(HEADS, HEAD_DIM, q_len)
    attended = lax.psum(partial_value, "seq").astype(jnp.bfloat16)
    dots = jnp.sum(
        dah.astype(jnp.float32) * attended.reshape(HEADS, HEAD_DIM, q_len).astype(jnp.float32),
        axis=1,
    )
    own_cols = lax.dynamic_slice_in_dim(attended, place * own_width, own_width, 0)
    weight_term = jnp.dot(own_cols, cotangent, preferred_element_type=jnp.float32)
    grad_weight = lax.psum_scatter(weight_term, "section", scatter_dimension=1, tiled=True).astype(
        jnp.bfloat16
    )
    dprobs = jnp.einsum("hdq,khd->hqk", dah, vh, preferred_element_type=jnp.float32)
    dscores_b = (probs * (dprobs - dots[..., None])).astype(jnp.bfloat16)
    grad_v = (
        jnp.einsum("hqk,hdq->khd", probs_b, dah, preferred_element_type=jnp.float32)
        .reshape(kv_len, width)
        .astype(jnp.bfloat16)
    )
    grad_k = (
        (scale * jnp.einsum("hqk,qhd->khd", dscores_b, qh, preferred_element_type=jnp.float32))
        .reshape(kv_len, width)
        .astype(jnp.bfloat16)
    )
    query_term = (
        scale * jnp.einsum("hqk,khd->hdq", dscores_b, kh, preferred_element_type=jnp.float32)
    ).reshape(width, q_len)
    grad_q = lax.psum_scatter(query_term, "seq", scatter_dimension=0, tiled=True).astype(
        jnp.bfloat16
    )
    return (grad_q[None], grad_k[None], grad_v[None], grad_weight)


def solution(mesh):
    return jax.shard_map(
        local,
        mesh=mesh,
        in_specs=(
            P("section", None, None),
            P("section", "seq", None),
            P("section", "seq", None),
            P("section", None, None),
            P("seq", None),
            P(),
        ),
        out_specs=(
            P("section", "seq", None),
            P("section", "seq", None),
            P("section", "seq", None),
            P("seq", "section"),
        ),
        check_vma=False,
    )
```

profile of v0, /device:TPU:6, one launch (start us, length us, event | category | flops | bytes accessed | tf_op | source)
XLA Modules:
  0.0 445.7 jit_solution(6057647331058708665)
XLA Ops:
  7.2 1.7 copy-done
  8.9 2.4 fusion.13
  11.4 2.6 copy.33
  13.9 1.4 copy.34
  15.5 2.2 fusion.3
  17.7 0.8 exponential_reduce_fusion
  18.5 37.3 %all-gather.3 = f32[32,28,256]{2,1,0:T(8,128)S(1)} all-gather(f32[1,28,256]{2,1,0:T(8,128)S(1)} %bitcast.79), channel_id=3, replica_groups=mesh['section'=8,'seq'=32] {'seq'}, dimensions={0}, use_global_device_ids=true | all-gather | bytes 946176 | tf_op jit(solution)/shard_map/all_gather | solution.py:14
  55.8 1.1 slice.27
  56.9 36.7 %all-gather.2 = f32[32,28,256]{2,1,0:T(8,128)S(1)} all-gather(f32[1,28,256]{2,1,0:T(8,128)S(1)} %bitcast.78), channel_id=2, replica_groups=mesh['section'=8,'seq'=32] {'seq'}, dimensions={0}, use_global_device_ids=true | all-gather | bytes 946176 | tf_op jit(solution)/shard_map/all_gather | solution.py:14
  93.6 1.1 slice.26
  94.7 25.7 %while.12 = (s32[]{:T(128)}, f32[28,256]{1,0:T(8,128)S(1)}, f32[28,256]{1,0:T(8,128)S(1)}, f32[31,28,256]{2,1,0:T(8,128)}, f32[31,28,256]{2,1,0:T(8,128)}, /*index=5*/s32[]{:T(128)}) while((s32[]{:T(128)}, f32[28,256]{1,0:T(8,128)S(1)}, f32[28,256]{1,0:T(8,128)S(1)}, f32[31,28,256]{2,1,0:T(8,128)}, f32[31,28,256]{2,1,0:T(8,128)}, ...), condition=%wide.region_3.4_spmd, body=%wide.region_2.3_spmd.sunk | while | flops 43010 | bytes 172105 | solution.py:17
  95.6 0.8 fusion.34
  96.4 0.8 fusion.34
  97.2 0.8 fusion.34
  98.1 0.8 fusion.34
  98.9 0.8 fusion.34
  99.7 0.8 fusion.34
  100.5 0.8 fusion.34
  101.4 0.8 fusion.34
  102.2 0.8 fusion.34
  103.0 0.8 fusion.34
  103.9 0.8 fusion.34
  104.7 0.8 fusion.34
  105.5 0.8 fusion.34
  106.4 0.8 fusion.34
  107.2 0.8 fusion.34
  108.0 0.8 fusion.34
  108.8 0.8 fusion.34
  109.7 0.8 fusion.34
  110.5 0.8 fusion.34
  120.5 2.2 copy.35
  122.7 5.0 %fusion.17 = f32[28,256,96]{1,2,0:T(8,128)} fusion(bf16[128,28,96]{0,2,1:T(8,128)(2,1)} %bitcast.75, f32[28,256,128]{1,2,0:T(8,128)} %copy-done.1, f32[28,256]{1,0:T(8,128)S(1)} %get-tuple-element.33, f32[28,256]{1,0:T(8,128)S(1)} %get-tuple-element.32, pred[256,128]{0,1:T(8,128)(4,1)S(1)} %compare_and_fusion), kind=kOutput, calls=%fused_computation.23 | convolution fusion | flops 180748288 | bytes 7200768 | tf_op jit(solution)/shard_map/hqk,khd->hdq/dot_general | solution.py:56
  127.7 126.9 %all-reduce.5 = bf16[2688,256]{1,0:T(8,128)(2,1)} all-reduce(f32[2688,256]{1,0:T(8,128)} %bitcast.73), channel_id=1, replica_groups=mesh['section'=8,'seq'=32] {'seq'}, use_global_device_ids=true, to_apply=%region_4.5 | all-reduce | flops 688128 | bytes 4128768 | tf_op jit(solution)/shard_map/psum | solution.py:60
  254.6 3.1 fusion.5
  260.2 81.6 %all-reduce.6 = bf16[84,5280]{1,0:T(8,128)(2,1)} all-reduce(f32[84,5280]{1,0:T(8,128)} %fusion.5), channel_id=5, replica_groups=mesh['section'=8,'seq'=32] {'section'}, use_global_device_ids=true, to_apply=%region_7.8.clone | all-reduce | flops 443520 | bytes 2661120
  341.8 1.7 dynamic-slice_convert_fusion
  343.5 3.3 reshape.110
  346.8 4.6 %convolution_convert_fusion = bf16[28,96,128]{2,1,0:T(8,128)(2,1)} fusion(bf16[28,96,256]{2,1,0:T(8,128)(2,1)} %reshape.110, f32[28,256,128]{1,2,0:T(8,128)} %copy-done.1, f32[28,256]{1,0:T(8,128)S(1)} %get-tuple-element.33, f32[28,256]{1,0:T(8,128)S(1)} %get-tuple-element.32, pred[256,128]{0,1:T(8,128)(4,1)S(1)} %compare_and_fusion), kind=kOutput, calls=%fused_computation.19 | convolution fusion | flops 181092352 | bytes 5824512 | tf_op jit(solution)/shard_map/hqk,hdq->khd/dot_general | solution.py:73
  352.5 1.3 multiply_convert_fusion
  353.8 1.2 copy-done.3
  355.1 2.1 convolution_multiply_fusion
  357.1 69.2 %fusion = f32[88,256]{1,0:T(8,128)S(1)} fusion(f32[2688,256]{1,0:T(8,128)} %bitcast.69), kind=kCustom, calls=%all-reduce-scatter | all-reduce-scatter fusion | flops 720897 | bytes 2843648
  426.9 1.9 collective-permute-start
  428.8 1.9 collective-permute-start.1
  430.8 2.6 fusion.9
  433.4 2.2 copy.42
  435.6 1.1 copy.41
  437.1 1.1 concatenate
  (46 shorter events, 13.9 us)
Async XLA Ops:
  7.2 1.8 copy-start
  7.2 336.3 %all-gather.7.cloned.1.call-start = ((), (), s32[]{:S(2)}) async-start(), calls=%async_computation | async-start | bytes 1486848 | tf_op jit(solution)/shard_map/all_gather | solution.py:45
  11.3 4.1 copy-start.7
  17.6 39.3 %copy-start.1 = (f32[28,256,128]{1,2,0:T(8,128)}, f32[28,256,128]{1,2,0:T(8,128)S(1)}, u32[]{:S(2)}) copy-start(f32[28,256,128]{1,2,0:T(8,128)S(1)} %get-tuple-element.59) | copy-start | bytes 11010052
  254.6 3.1 copy-start.8
  254.6 4.4 copy-start.9
  346.8 4.6 %copy-start.4 = (bf16[2688,256]{1,0:T(8,128)(2,1)S(1)}, bf16[2688,256]{1,0:T(8,128)(2,1)}, u32[]{:S(2)}) copy-start(bf16[2688,256]{1,0:T(8,128)(2,1)} %all-reduce.5) | copy-start | bytes 4128772
  346.8 4.6 %copy-start.5 = (bf16[28,96,256]{2,1,0:T(8,128)(2,1)S(1)}, bf16[28,96,256]{2,1,0:T(8,128)(2,1)}, u32[]{:S(2)}) copy-start(bf16[28,96,256]{2,1,0:T(8,128)(2,1)} %reshape.110) | copy-start | bytes 4128772
  346.8 5.1 %copy-start.2 = (f32[28,256,128]{1,2,0:T(8,128)S(1)}, f32[28,256,128]{1,2,0:T(8,128)}, u32[]{:S(2)}) copy-start(f32[28,256,128]{1,2,0:T(8,128)} %copy-done.1) | copy-start | bytes 11010052
  351.4 1.1 copy-start.6
  353.8 1.2 copy-start.3
  426.9 10.2 %collective-permute-start = (bf16[88,256]{1,0:T(8,128)(2,1)S(1)}, bf16[88,256]{1,0:T(8,128)(2,1)}, u32[]{:S(2)}, u32[]{:S(2)}) collective-permute-start(bf16[88,256]{1,0:T(8,128)(2,1)S(1)} %convert.9), channel_id=1, source_target_pairs={{0,1},{1,2},{2,3},{3,4},{4,5},{5,6},{6,7},{7,8},{8,9},{9,10},{10,1... | collective-permute-start | bytes 135176
  428.8 8.3 %collective-permute-start.1 = (bf16[36,256]{1,0:T(8,128)(2,1)}, bf16[36,256]{1,0:T(8,128)(2,1)S(1)}, u32[]{:S(2)}, u32[]{:S(2)}) collective-permute-start(bf16[36,256]{1,0:T(8,128)(2,1)} %slice.28), channel_id=1, source_target_pairs={{0,2},{1,3},{2,4},{3,5},{4,6},{5,7},{6,8},{7,9},{8,10},{9,11},{10,... | collective-permute-start | bytes 55304
Sparse Core Ops, SparseCore 0:
  11.5 66.6 all-gather.6
where the time goes:
time: 453 us; the launch traced here: 446 us
  blocking collectives  352 us (78%)
  other arithmetic  26.7 us (6%)
  local copies, waits for them, and re-layouts  23.7 us (5%)
  matrix products  23.3 us (5%)
  between operations  15.5 us (3%)
    unnamed x2, blocking collectives  151 us
    psum x1, blocking collectives, local(): attended = lax.psum(partial_value, 'seq').astype(jnp.bfloat16)  127 us
    all_gather x2, blocking collectives, combined_all(): pieces = jax.tree.map(lambda part: lax.all_gather(part, axis), value)  74 us
    add x31, other arithmetic, combine_stats(): first[1] * jnp.exp(first[0] - top) + second[1] * jnp.exp(second[0] - top)  25.3 us
    unnamed x29, local copies, waits for them, and re-layouts  15.9 us
  transfers between devices with their start and end apart: 3, of which 1 were waited for; matrix products, arithmetic and copies ran while one was open for 12% of the time, Pallas kernels for 0%

commit v1 on v0

v1 whole, which is shorter than its diff:
```python
import functools

import jax
import jax.numpy as jnp
from jax import lax
from jax.experimental import pallas as pl
from jax.experimental.pallas import tpu as pltpu
from jax.sharding import Mesh, PartitionSpec as P

HEADS = 28
HEAD_DIM = 96
GROUPS = 4
GROUP_HEADS = HEADS // GROUPS
GROUP_WIDTH = GROUP_HEADS * HEAD_DIM
BLOCK = 8
NEG = -(2.0**99)
SCALE = HEAD_DIM ** (-0.5)
BLOCK_AXES = ("zl", "x_lo", "core")
SEQ_AXES = ("zp",) + BLOCK_AXES
F32 = jnp.float32
BF16 = jnp.bfloat16
VMEM_LIMIT = 48 * 1024 * 1024
NT = (((1,), (1,)), ((), ()))
NN = (((1,), (0,)), ((), ()))
TN = (((0,), (0,)), ((), ()))


def mm(a, b, dims):
    return lax.dot_general(a, b, dims, preferred_element_type=F32)


def pack_kernel(place, k_ref, v_ref, q_ref, *outs):
    zp = place[0]
    kv_len = k_ref.shape[0]
    for g in range(GROUPS):
        cols = slice(g * GROUP_WIDTH, (g + 1) * GROUP_WIDTH)
        for s in range(GROUPS):

            @pl.when(lax.rem(zp + s, GROUPS) == g)
            def _():
                outs[s][:kv_len, :] = k_ref[:, cols]
                outs[s][kv_len:, :] = v_ref[:, cols]
                if s == 0:
                    outs[GROUPS][...] = q_ref[:, cols]


def unpack_kernel(place, s0, s1, s2, s3, gk_ref, gv_ref):
    zp = place[0]
    kv_len = gk_ref.shape[0]
    slots = (s0, s1, s2, s3)
    for g in range(GROUPS):
        cols = slice(g * GROUP_WIDTH, (g + 1) * GROUP_WIDTH)
        for s in range(GROUPS):

            @pl.when(lax.rem(zp + s, GROUPS) == g)
            def _():
                gk_ref[:, cols] = slots[s][:kv_len, :]
                gv_ref[:, cols] = slots[s][kv_len:, :]


def set_up(place, ws_ref, d_ref, bias, d_all):
    zp, member = place[0], place[1]
    q_len = ws_ref.shape[1]
    kv_len = bias.shape[0] // GROUPS
    context = kv_len * GROUPS * BLOCK
    rows = lax.broadcasted_iota(jnp.int32, (kv_len, q_len), 0)
    query_pos = context - q_len + lax.broadcasted_iota(jnp.int32, (kv_len, q_len), 1)
    for s in range(GROUPS):
        owner = lax.rem(zp + GROUPS - s, GROUPS) * BLOCK + member
        key_pos = owner * kv_len + rows
        visible = (key_pos >= ws_ref[...]) & (key_pos <= query_pos)
        bias[s * kv_len : (s + 1) * kv_len, :] = jnp.where(visible, 0.0, NEG)
    rows_each = d_ref.shape[1]
    for k in range(BLOCK):
        d_all[k * rows_each : (k + 1) * rows_each, :] = d_ref[k].astype(F32)


def head_cols(slots, lo, hi, cols):
    return jnp.concatenate([s[lo:hi, cols] for s in slots], axis=0)


def forward_kernel(place, ws_ref, q_ref, s0, s1, s2, s3, d_ref, out_ref, bias, d_all, att, payload):
    kv_len = s0.shape[0] // 2
    slots = (s0, s1, s2, s3)
    rows_each = d_ref.shape[1]
    set_up(place, ws_ref, d_ref, bias, d_all)
    payload[...] = jnp.zeros_like(payload)
    for h in range(GROUP_HEADS):
        cols = slice(h * HEAD_DIM, (h + 1) * HEAD_DIM)
        kh = head_cols(slots, 0, kv_len, cols)
        vh = head_cols(slots, kv_len, 2 * kv_len, cols)
        dh = d_all[cols, :].astype(BF16)
        scores = mm(kh, q_ref[:, cols], NT) * SCALE + bias[...]
        top = jnp.floor(jnp.max(scores, axis=0, keepdims=True) * 0.125) * 8.0
        expo = jnp.exp(scores - top)
        total = jnp.sum(expo, axis=0, keepdims=True)
        att[cols, :] = mm(vh, expo.astype(BF16), TN)
        dots = jnp.sum(expo * mm(vh, dh, NN), axis=0, keepdims=True)
        total_hi = total.astype(BF16).astype(F32)
        dots_hi = dots.astype(BF16).astype(F32)
        for n, row in enumerate((top, total_hi, total - total_hi, dots_hi, dots - dots_hi)):
            payload[0, 88 + 8 * n + h : 89 + 8 * n + h, :] = row
    for k in range(BLOCK):
        if k > 0:
            payload[k, 88:, :] = payload[0, 88:, :]
        payload[k, :rows_each, :] = att[k * rows_each : (k + 1) * rows_each, :]
    out_ref[...] = payload[...].astype(BF16)


def backward_kernel(
    place, ws_ref, q_ref, s0, s1, s2, s3, d_ref, ex_ref, o0, o1, o2, o3, gq_ref, att_ref, bias, d_all, gq, stats, weights
):
    kv_len = s0.shape[0] // 2
    slots = (s0, s1, s2, s3)
    outs = (o0, o1, o2, o3)
    rows_each, q_len = att_ref.shape
    member = place[1]
    set_up(place, ws_ref, d_ref, bias, d_all)
    parts = [ex_ref[j].astype(F32) for j in range(BLOCK)]
    top = functools.reduce(jnp.maximum, [p[88:96] for p in parts])
    scaled = [jnp.exp(p[88:96] - top) for p in parts]
    total = sum(w * (p[96:104] + p[104:112]) for w, p in zip(scaled, parts))
    total = jnp.where(total > 0.0, total, 1.0)
    inverse = 1.0 / total
    dots = sum(w * (p[112:120] + p[120:128]) for w, p in zip(scaled, parts)) * inverse
    stats[0] = top
    stats[1] = inverse
    stats[2] = dots
    weights[...] = jnp.zeros_like(weights)
    row = lax.broadcasted_iota(jnp.int32, (rows_each, q_len), 0)
    first = row < (HEAD_DIM - rows_each) * member
    attended = jnp.zeros((rows_each, q_len), F32)
    for j in range(BLOCK):
        weights[j, 8:16, :] = scaled[j] * inverse
        before = weights[j, pl.ds(member + 7, 1), :]
        after = weights[j, pl.ds(member + 8, 1), :]
        attended += jnp.where(first, before, after) * parts[j][:rows_each]
    att_ref[...] = attended.astype(BF16)
    for h in range(GROUP_HEADS):
        cols = slice(h * HEAD_DIM, (h + 1) * HEAD_DIM)
        kh = head_cols(slots, 0, kv_len, cols)
        vh = head_cols(slots, kv_len, 2 * kv_len, cols)
        qh = q_ref[:, cols]
        dh = d_all[cols, :].astype(BF16)
        scores = mm(kh, qh, NT) * SCALE + bias[...]
        probs = jnp.exp(scores - stats[0, h : h + 1, :]) * stats[1, h : h + 1, :]
        dscores = probs * (mm(vh, dh, NN) - stats[2, h : h + 1, :])
        probs = probs.astype(BF16)
        dscores = dscores.astype(BF16)
        gk = (mm(dscores, qh, NN) * SCALE).astype(BF16)
        gv = mm(probs, dh, NT).astype(BF16)
        for s in range(GROUPS):
            part = slice(s * kv_len, (s + 1) * kv_len)
            outs[s][:kv_len, cols] = gk[part]
            outs[s][kv_len:, cols] = gv[part]
        gq[cols, :] = mm(kh, dscores, TN) * SCALE
    for k in range(BLOCK):
        gq_ref[k] = gq[k * rows_each : (k + 1) * rows_each, :].astype(BF16)


def weight_kernel(att_ref, cot_ref, out_ref, full):
    pieces, _, width = out_ref.shape
    full[...] = mm(att_ref[...], cot_ref[...], NN)
    for s in range(pieces):
        out_ref[s] = full[:, s * width : (s + 1) * width].astype(BF16)


SMEM = pl.BlockSpec(memory_space=pltpu.SMEM)
WHOLE = pl.BlockSpec(memory_space=pltpu.VMEM)


def call(kernel, n_in, out_shapes, scratch=(), scalars=1, flops=0, nbytes=0):
    return pl.pallas_call(
        kernel,
        out_shape=out_shapes,
        in_specs=[SMEM] * scalars + [WHOLE] * n_in,
        out_specs=jax.tree.map(lambda _: WHOLE, out_shapes),
        scratch_shapes=list(scratch),
        compiler_params=pltpu.CompilerParams(vmem_limit_bytes=VMEM_LIMIT),
        cost_estimate=pl.CostEstimate(flops=flops, bytes_accessed=nbytes, transcendentals=0),
    )


def shift(by):
    return [(i, (i + by) % GROUPS) for i in range(GROUPS)]


def local(queries, keys, values, out_grad, w_out, window_start):
    query, key_rows, value_rows, cotangent = queries[0], keys[0], values[0], out_grad[0]
    q_len = query.shape[0]
    kv_len = key_rows.shape[0]
    rows_each, model = w_out.shape
    sections = lax.axis_size("section")
    member = lax.axis_index(BLOCK_AXES)
    place = jnp.stack([lax.axis_index("zp"), member]).astype(jnp.int32)
    starts = window_start.reshape(1, q_len)
    sds = jax.ShapeDtypeStruct
    slot = sds((2 * kv_len, GROUP_WIDTH), BF16)

    *send, q_own = call(pack_kernel, 3, [slot] * GROUPS + [sds((q_len, GROUP_WIDTH), BF16)], nbytes=4_000_000)(
        place, key_rows, value_rows, query
    )
    slots = [send[0]] + [lax.ppermute(send[s], "zp", shift(s)) for s in range(1, GROUPS)]

    d_own = lax.dot_general(w_out, cotangent, NT, preferred_element_type=F32).astype(BF16)
    d_group = lax.all_to_all(jnp.broadcast_to(d_own[None], (BLOCK, rows_each, q_len)), BLOCK_AXES, 0, 0)

    positions = GROUPS * kv_len
    common = [pltpu.VMEM((positions, q_len), F32), pltpu.VMEM((GROUP_WIDTH, q_len), F32), pltpu.VMEM((GROUP_WIDTH, q_len), F32)]
    payload = call(
        forward_kernel,
        7,
        sds((BLOCK, 128, q_len), BF16),
        common + [pltpu.VMEM((BLOCK, 128, q_len), F32)],
        flops=2_000_000_000,
        nbytes=2_000_000,
    )(place, starts, q_own, *slots, d_group)
    exchanged = lax.all_to_all(payload, BLOCK_AXES, 0, 0)

    *back, gq_parts, attended = call(
        backward_kernel,
        8,
        [slot] * GROUPS + [sds((BLOCK, rows_each, q_len), BF16), sds((rows_each, q_len), BF16)],
        common + [pltpu.VMEM((3, 8, q_len), F32), pltpu.VMEM((BLOCK, 24, q_len), F32)],
        flops=3_000_000_000,
        nbytes=4_000_000,
    )(place, starts, q_own, *slots, d_group, exchanged)

    back = [back[0]] + [lax.ppermute(back[s], "zp", shift(-s)) for s in range(1, GROUPS)]

    gq = lax.all_to_all(gq_parts, BLOCK_AXES, 0, 0)
    grad_q = jnp.sum(gq.astype(F32), axis=0).astype(BF16)

    width = model // sections
    weight_parts = call(
        weight_kernel,
        2,
        sds((sections, rows_each, width), BF16),
        [pltpu.VMEM((rows_each, model), F32)],
        scalars=0,
        flops=2 * rows_each * q_len * model,
        nbytes=4_000_000,
    )(attended, cotangent)
    weight_parts = lax.all_to_all(weight_parts, "section", 0, 0)
    grad_weight = jnp.sum(weight_parts.astype(F32), axis=0).astype(BF16)

    grad_k, grad_v = call(unpack_kernel, 4, [sds((kv_len, HEADS * HEAD_DIM), BF16)] * 2, nbytes=3_000_000)(place, *back)
    return grad_q[None], grad_k[None], grad_v[None], grad_weight


def solution(mesh):
    sections = mesh.shape["section"]
    fine = Mesh(mesh.devices.reshape(sections, GROUPS, 2, 2, 2), ("section",) + SEQ_AXES)
    return jax.shard_map(
        local,
        mesh=fine,
        in_specs=(
            P("section", None, None),
            P("section", SEQ_AXES, None),
            P("section", SEQ_AXES, None),
            P("section", None, None),
            P(SEQ_AXES, None),
            P(),
        ),
        out_specs=(
            P("section", SEQ_AXES, None),
            P("section", SEQ_AXES, None),
            P("section", SEQ_AXES, None),
            P(SEQ_AXES, "section"),
        ),
        check_vma=False,
    )
```

time: 453 us -> 146 us (0.32)
  the two profiles are of different devices: /device:TPU:6 before, /device:TPU:39 now
where the time goes in v1:
time: 146 us; the launch traced here: 145 us
  waiting for transfers between devices  64.9 us (44%)
  starting transfers between devices  32.5 us (22%)
  local copies, waits for them, and re-layouts  15 us (10%)
  blocking collectives  13.7 us (9%)
  Pallas kernels  12.8 us (9%)
  other arithmetic  2.84 us (2%)
  matrix products  2.33 us (2%)
    ppermute x3, waiting for transfers between devices, local(): lax.ppermute(back[s], 'zp', shift(-s))  34.7 us
    ppermute x3, waiting for transfers between devices, local(): lax.ppermute(send[s], 'zp', shift(s))  30.2 us
    unnamed x29, local copies, waits for them, and re-layouts  14.2 us
    all_to_all x1, blocking collectives, local(): exchanged = lax.all_to_all(payload, BLOCK_AXES, 0, 0)  13.7 us
    ppermute x3, starting transfers between devices, local(): lax.ppermute(send[s], 'zp', shift(s))  10.1 us
    all_to_all x1, starting transfers between devices, local(): weight_parts = lax.all_to_all(weight_parts, 'section', 0, 0)  6.88 us
    ppermute x3, starting transfers between devices, local(): lax.ppermute(back[s], 'zp', shift(-s))  5.81 us
    all_to_all x1, starting transfers between devices, local(): gq = lax.all_to_all(gq_parts, BLOCK_AXES, 0, 0)  5.19 us
  transfers between devices with their start and end apart: 9, of which 5 were waited for; matrix products, arithmetic and copies ran while one was open for 4% of the time, Pallas kernels for 3%

profile of v1, /device:TPU:39, one launch (start us, length us, event | category | flops | bytes accessed | tf_op | source)
XLA Modules:
  0.0 144.8 jit_solution(16502529270647663948)
XLA Ops:
  0.6 0.0 copy-start
  0.6 0.0 copy-start.3
  0.7 0.0 copy-start.2
  0.7 1.2 copy-done
  1.8 2.3 %fusion.2 = bf16[84,256]{1,0:T(8,128)(2,1)S(1)} fusion(bf16[84,5280]{1,0:T(8,128)(2,1)S(1)} %copy-done, bf16[1,256,5280]{1,2,0:T(8,128)(2,1)} %param.9), kind=kOutput, calls=%fused_computation.2 | convolution fusion | flops 227103744 | bytes 3633408 | tf_op jit(solution)/shard_map/dot_general | solution.py:205
  4.2 0.0 copy-start.13
  4.2 0.8 broadcast_in_dim.15
  5.0 4.5 %all-to-all-start = ((bf16[8,84,256]{2,1,0:T(8,128)(2,1)}), bf16[8,84,256]{2,1,0:T(8,128)(2,1)S(1)}, u32[]{:S(2)}, u32[]{:S(2)}) async-start(bf16[8,84,256]{2,1,0:T(8,128)(2,1)} %broadcast_in_dim.15), calls=%async_computation | async-start | bytes 720896 | tf_op jit(solution)/shard_map/all_to_all | solution.py:206
  9.5 0.1 pad_add_fusion.place
  9.5 0.0 copy-done.3
  9.5 0.0 copy-done.2
  9.6 1.1 copy-done.4
  10.6 1.2 shard_map.93
  11.8 0.0 copy-start.5
  11.8 0.7 copy-done.5
  12.6 0.7 copy-done.7
  13.3 3.1 %collective-permute-start = (bf16[256,672]{1,0:T(8,128)(2,1)S(1)}, bf16[256,672]{1,0:T(8,128)(2,1)S(1)}, u32[]{:S(2)}, u32[]{:S(2)}) collective-permute-start(bf16[256,672]{1,0:T(8,128)(2,1)S(1)} %get-tuple-element.19), channel_id=1, source_target_pairs={{0,8},{8,16},{16,24},{24,0},{1,9},{9,17},{17,25},{25,1},{2,10},{10... | collective-permute-start | bytes 1032200 | tf_op jit(solution)/shard_map/ppermute | solution.py:203
  16.4 4.7 %collective-permute-start.1 = (bf16[256,672]{1,0:T(8,128)(2,1)S(1)}, bf16[256,672]{1,0:T(8,128)(2,1)S(1)}, u32[]{:S(2)}, u32[]{:S(2)}) collective-permute-start(bf16[256,672]{1,0:T(8,128)(2,1)S(1)} %get-tuple-element.20), channel_id=1, source_target_pairs={{0,16},{8,24},{16,0},{24,8},{1,17},{9,25},{17,1},{25,9},{2,18},{10... | collective-permute-start | bytes 1032200 | tf_op jit(solution)/shard_map/ppermute | solution.py:203
  21.0 2.4 %collective-permute-start.2 = (bf16[256,672]{1,0:T(8,128)(2,1)S(1)}, bf16[256,672]{1,0:T(8,128)(2,1)S(1)}, u32[]{:S(2)}, u32[]{:S(2)}) collective-permute-start(bf16[256,672]{1,0:T(8,128)(2,1)S(1)} %get-tuple-element.21), channel_id=1, source_target_pairs={{0,24},{8,0},{16,8},{24,16},{1,25},{9,1},{17,9},{25,17},{2,26},{10... | collective-permute-start | bytes 1032200 | tf_op jit(solution)/shard_map/ppermute | solution.py:203
  23.4 24.8 %collective-permute-done.s1 = bf16[256,672]{1,0:T(8,128)(2,1)S(1)} collective-permute-done((bf16[256,672]{1,0:T(8,128)(2,1)S(1)}, bf16[256,672]{1,0:T(8,128)(2,1)S(1)}, u32[]{:S(2)}, u32[]{:S(2)}) %collective-permute-start) | collective-permute-done | bytes 344096 | tf_op jit(solution)/shard_map/ppermute | solution.py:203
  48.2 0.0 collective-permute-done.1.s2
  48.2 5.4 %collective-permute-done.2.s3 = bf16[256,672]{1,0:T(8,128)(2,1)S(1)} collective-permute-done((bf16[256,672]{1,0:T(8,128)(2,1)S(1)}, bf16[256,672]{1,0:T(8,128)(2,1)S(1)}, u32[]{:S(2)}, u32[]{:S(2)}) %collective-permute-start.2) | collective-permute-done | bytes 344096 | tf_op jit(solution)/shard_map/ppermute | solution.py:203
  53.6 0.0 all-to-all-done.d_ref
  53.6 0.0 copy-done.13
  53.6 0.0 copy-start.6
  53.6 1.1 copy-done.6
  54.8 1.0 copy-done.8
  55.8 3.5 %shard_map.94 = bf16[8,128,256]{2,1,0:T(8,128)(2,1)S(1)} custom-call(s32[2]{0:T(128)S(1)} %pad_add_fusion.place, s32[1,256]{1,0:T(1,128)S(1)} %bitcast.20, bf16[256,672]{1,0:T(8,128)(2,1)S(1)} %copy-done.8, bf16[256,672]{1,0:T(8,128)(2,1)S(1)} %copy-done.6, bf16[256,672]{1,0:T(8,128)(2,1)S(1)} %collective-permute-done.s1, ...), custom_call_target="tpu_custom_call" | custom-call | flops 2000000000 | bytes 2000000 | tf_op jit(solution)/shard_map/pallas_call | solution.py:210
  59.3 13.7 %all_to_all.20.ex_ref = bf16[8,128,256]{2,1,0:T(8,128)(2,1)S(1)} all-to-all(bf16[8,128,256]{2,1,0:T(8,128)(2,1)S(1)} %shard_map.94), channel_id=1, replica_groups=mesh['section'=8,'zp'=4,'zl'=2,'x_lo'=2,'core'=2] {'zl','x_lo','core'}, dimensions={0} | all-to-all | bytes 1048576 | tf_op jit(solution)/shard_map/all_to_all | solution.py:218
  73.0 1.0 copy-done.10
  74.0 1.0 copy-done.12
  75.0 4.2 %shard_map.95 = (bf16[256,672]{1,0:T(8,128)(2,1)S(1)}, bf16[256,672]{1,0:T(8,128)(2,1)S(1)}, bf16[256,672]{1,0:T(8,128)(2,1)S(1)}, bf16[256,672]{1,0:T(8,128)(2,...) custom-call(s32[2]{0:T(128)S(1)} %pad_add_fusion.place, s32[1,256]{1,0:T(1,128)S(1)} %bitcast.21, ...), custom_call_target="tpu_custom_call" | custom-call | flops 3000000000 | bytes 4000000 | tf_op jit(solution)/shard_map/pallas_call | solution.py:220
  79.3 5.2 %all-to-all-start.2 = ((bf16[8,84,256]{2,1,0:T(8,128)(2,1)}), bf16[8,84,256]{2,1,0:T(8,128)(2,1)S(1)}, u32[]{:S(2)}, u32[]{:S(2)}) async-start(bf16[8,84,256]{2,1,0:T(8,128)(2,1)} %get-tuple-element.22), calls=%async_computation.2 | async-start | bytes 720896 | tf_op jit(solution)/shard_map/all_to_all | solution.py:231
  84.4 4.6 %copy.10 = bf16[1,256,5280]{2,1,0:T(8,128)(2,1)} copy(bf16[1,256,5280]{1,2,0:T(8,128)(2,1)} %param.9) | data formatting | bytes 5406720 | tf_op args[3]
  89.0 1.8 %copy-done.1 = bf16[1,256,5280]{2,1,0:T(8,128)(2,1)S(1)} copy-done((bf16[1,256,5280]{2,1,0:T(8,128)(2,1)S(1)}, bf16[1,256,5280]{2,1,0:T(8,128)(2,1)}, u32[]{:S(2)}) %copy-start.1) | copy-done | bytes 2703384
  90.8 1.7 %shard_map.97 = bf16[8,84,660]{2,1,0:T(8,128)(2,1)} custom-call(bf16[84,256]{1,0:T(8,128)(2,1)S(1)} %get-tuple-element.29.att_ref, bf16[256,5280]{1,0:T(8,128)(2,1)S(1)} %bitcast.16), custom_call_target="tpu_custom_call" | custom-call | flops 227082240 | bytes 4000000 | tf_op jit(solution)/shard_map/pallas_call | solution.py:235
  92.4 0.0 all-to-all-done.2
  92.4 6.9 %all-to-all-start.3 = ((bf16[8,84,660]{2,1,0:T(8,128)(2,1)}), bf16[8,84,660]{2,1,0:T(8,128)(2,1)}, u32[]{:S(2)}, u32[]{:S(2)}) async-start(bf16[8,84,660]{2,1,0:T(8,128)(2,1)} %shard_map.97), calls=%async_computation.3 | async-start | bytes 2162688 | tf_op jit(solution)/shard_map/all_to_all | solution.py:244
  99.3 3.1 %collective-permute-start.3 = (bf16[256,672]{1,0:T(8,128)(2,1)S(1)}, bf16[256,672]{1,0:T(8,128)(2,1)S(1)}, u32[]{:S(2)}, u32[]{:S(2)}) collective-permute-start(bf16[256,672]{1,0:T(8,128)(2,1)S(1)} %get-tuple-element.24), channel_id=1, source_target_pairs={{0,24},{8,0},{16,8},{24,16},{1,25},{9,1},{17,9},{25,17},{2,26},{10... | collective-permute-start | bytes 1032200 | tf_op jit(solution)/shard_map/ppermute | solution.py:229
  102.5 0.9 collective-permute-start.4
  103.4 1.8 %collective-permute-start.5 = (bf16[256,672]{1,0:T(8,128)(2,1)S(1)}, bf16[256,672]{1,0:T(8,128)(2,1)S(1)}, u32[]{:S(2)}, u32[]{:S(2)}) collective-permute-start(bf16[256,672]{1,0:T(8,128)(2,1)S(1)} %get-tuple-element.26), channel_id=1, source_target_pairs={{0,8},{8,16},{16,24},{24,0},{1,9},{9,17},{17,25},{25,1},{2,10},{10... | collective-permute-start | bytes 1032200 | tf_op jit(solution)/shard_map/ppermute | solution.py:229
  105.1 13.2 %collective-permute-done.3.s1 = bf16[256,672]{1,0:T(8,128)(2,1)S(1)} collective-permute-done((bf16[256,672]{1,0:T(8,128)(2,1)S(1)}, bf16[256,672]{1,0:T(8,128)(2,1)S(1)}, u32[]{:S(2)}, u32[]{:S(2)}) %collective-permute-start.3) | collective-permute-done | bytes 344096 | tf_op jit(solution)/shard_map/ppermute | solution.py:229
  118.3 19.3 %collective-permute-done.4.s2 = bf16[256,672]{1,0:T(8,128)(2,1)S(1)} collective-permute-done((bf16[256,672]{1,0:T(8,128)(2,1)S(1)}, bf16[256,672]{1,0:T(8,128)(2,1)S(1)}, u32[]{:S(2)}, u32[]{:S(2)}) %collective-permute-start.4) | collective-permute-done | bytes 344096 | tf_op jit(solution)/shard_map/ppermute | solution.py:229
  137.6 2.2 %collective-permute-done.5.s3 = bf16[256,672]{1,0:T(8,128)(2,1)S(1)} collective-permute-done((bf16[256,672]{1,0:T(8,128)(2,1)S(1)}, bf16[256,672]{1,0:T(8,128)(2,1)S(1)}, u32[]{:S(2)}, u32[]{:S(2)}) %collective-permute-start.5) | collective-permute-done | bytes 344096 | tf_op jit(solution)/shard_map/ppermute | solution.py:229
  139.8 2.2 %shard_map.96 = (bf16[128,2688]{1,0:T(8,128)(2,1)}, bf16[128,2688]{1,0:T(8,128)(2,1)}) custom-call(s32[2]{0:T(128)S(1)} %pad_add_fusion.place, bf16[256,672]{1,0:T(8,128)(2,1)S(1)} %get-tuple-element.23.s0, bf16[256,672]{1,0:T(8,128)(2,1)S(1)} %collective-permute-done.3.s1, bf16[256,672]{1,0:T(8,128)(2,1)S(1)} %collective-permute-done.4.s2, ...), custom_call_target="tpu_custom_call" | custom-call | bytes 3000000 | tf_op jit(solution)/shard_map/pallas_call | solution.py:247
  142.1 0.7 reduce_sum.24
  142.7 0.0 all-to-all-done.3
  142.7 2.1 %reduce_sum.25 = bf16[84,660]{1,0:T(8,128)(2,1)} reduce(bf16[8,84,660]{2,1,0:T(8,128)(2,1)} %all-to-all-done.3, bf16[]{:T(256)} %constant.21.clone.1), dimensions={0}, to_apply=%region_1.0 | reduce | flops 388080 | bytes 997922 | tf_op jit(solution)/shard_map/reduce_sum | solution.py:245
  (10 shorter events, 0.0 us)
Async XLA Ops:
  0.6 1.2 copy-start
  0.6 8.9 %copy-start.3 = (bf16[1,128,2688]{2,1,0:T(8,128)(2,1)S(1)}, bf16[1,128,2688]{2,1,0:T(8,128)(2,1)}, u32[]{:S(2)}) copy-start(bf16[1,128,2688]{2,1,0:T(8,128)(2,1)} %param.7) | copy-start | bytes 2064388
  0.7 8.9 %copy-start.2 = (bf16[1,256,2688]{2,1,0:T(8,128)(2,1)S(1)}, bf16[1,256,2688]{2,1,0:T(8,128)(2,1)}, u32[]{:S(2)}) copy-start(bf16[1,256,2688]{2,1,0:T(8,128)(2,1)} %param.6) | copy-start | bytes 4128772
  4.2 49.5 %copy-start.13 = (s32[256]{0:T(256)S(1)}, s32[256]{0:T(256)}, u32[]{:S(2)}) copy-start(s32[256]{0:T(256)} %param.11) | copy-start | bytes 3076
  5.0 48.7 %all-to-all-start = ((bf16[8,84,256]{2,1,0:T(8,128)(2,1)}), bf16[8,84,256]{2,1,0:T(8,128)(2,1)S(1)}, u32[]{:S(2)}, u32[]{:S(2)}) async-start(bf16[8,84,256]{2,1,0:T(8,128)(2,1)} %broadcast_in_dim.15), calls=%async_computation | async-start | bytes 720896 | tf_op jit(solution)/shard_map/all_to_all | solution.py:206
  9.5 1.1 copy-start.4
  11.8 0.7 copy-start.5
  12.6 0.7 copy-start.7
  13.3 34.9 %collective-permute-start = (bf16[256,672]{1,0:T(8,128)(2,1)S(1)}, bf16[256,672]{1,0:T(8,128)(2,1)S(1)}, u32[]{:S(2)}, u32[]{:S(2)}) collective-permute-start(bf16[256,672]{1,0:T(8,128)(2,1)S(1)} %get-tuple-element.19), channel_id=1, source_target_pairs={{0,8},{8,16},{16,24},{24,0},{1,9},{9,17},{17,25},{25,1},{2,10},{10... | collective-permute-start | bytes 1032200 | tf_op jit(solution)/shard_map/ppermute | solution.py:203
  16.4 31.9 %collective-permute-start.1 = (bf16[256,672]{1,0:T(8,128)(2,1)S(1)}, bf16[256,672]{1,0:T(8,128)(2,1)S(1)}, u32[]{:S(2)}, u32[]{:S(2)}) collective-permute-start(bf16[256,672]{1,0:T(8,128)(2,1)S(1)} %get-tuple-element.20), channel_id=1, source_target_pairs={{0,16},{8,24},{16,0},{24,8},{1,17},{9,25},{17,1},{25,9},{2,18},{10... | collective-permute-start | bytes 1032200 | tf_op jit(solution)/shard_map/ppermute | solution.py:203
  21.0 32.6 %collective-permute-start.2 = (bf16[256,672]{1,0:T(8,128)(2,1)S(1)}, bf16[256,672]{1,0:T(8,128)(2,1)S(1)}, u32[]{:S(2)}, u32[]{:S(2)}) collective-permute-start(bf16[256,672]{1,0:T(8,128)(2,1)S(1)} %get-tuple-element.21), channel_id=1, source_target_pairs={{0,24},{8,0},{16,8},{24,16},{1,25},{9,1},{17,9},{25,17},{2,26},{10... | collective-permute-start | bytes 1032200 | tf_op jit(solution)/shard_map/ppermute | solution.py:203
  48.2 11.1 %copy-start.9 = (bf16[256,672]{1,0:T(8,128)(2,1)}, bf16[256,672]{1,0:T(8,128)(2,1)S(1)}, u32[]{:S(2)}) copy-start(bf16[256,672]{1,0:T(8,128)(2,1)S(1)} %collective-permute-done.1.s2) | copy-start | bytes 1032196
  53.6 5.7 %copy-start.11 = (bf16[256,672]{1,0:T(8,128)(2,1)}, bf16[256,672]{1,0:T(8,128)(2,1)S(1)}, u32[]{:S(2)}) copy-start(bf16[256,672]{1,0:T(8,128)(2,1)S(1)} %collective-permute-done.2.s3) | copy-start | bytes 1032196
  53.6 1.1 copy-start.6
  54.8 1.0 copy-start.8
  73.0 1.0 copy-start.10
  74.0 1.0 copy-start.12
  79.3 13.2 %all-to-all-start.2 = ((bf16[8,84,256]{2,1,0:T(8,128)(2,1)}), bf16[8,84,256]{2,1,0:T(8,128)(2,1)S(1)}, u32[]{:S(2)}, u32[]{:S(2)}) async-start(bf16[8,84,256]{2,1,0:T(8,128)(2,1)} %get-tuple-element.22), calls=%async_computation.2 | async-start | bytes 720896 | tf_op jit(solution)/shard_map/all_to_all | solution.py:231
  89.0 1.8 %copy-start.1 = (bf16[1,256,5280]{2,1,0:T(8,128)(2,1)S(1)}, bf16[1,256,5280]{2,1,0:T(8,128)(2,1)}, u32[]{:S(2)}) copy-start(bf16[1,256,5280]{2,1,0:T(8,128)(2,1)} %copy.10) | copy-start | bytes 8110084
  92.4 50.3 %all-to-all-start.3 = ((bf16[8,84,660]{2,1,0:T(8,128)(2,1)}), bf16[8,84,660]{2,1,0:T(8,128)(2,1)}, u32[]{:S(2)}, u32[]{:S(2)}) async-start(bf16[8,84,660]{2,1,0:T(8,128)(2,1)} %shard_map.97), calls=%async_computation.3 | async-start | bytes 2162688 | tf_op jit(solution)/shard_map/all_to_all | solution.py:244
  99.3 19.0 %collective-permute-start.3 = (bf16[256,672]{1,0:T(8,128)(2,1)S(1)}, bf16[256,672]{1,0:T(8,128)(2,1)S(1)}, u32[]{:S(2)}, u32[]{:S(2)}) collective-permute-start(bf16[256,672]{1,0:T(8,128)(2,1)S(1)} %get-tuple-element.24), channel_id=1, source_target_pairs={{0,24},{8,0},{16,8},{24,16},{1,25},{9,1},{17,9},{25,17},{2,26},{10... | collective-permute-start | bytes 1032200 | tf_op jit(solution)/shard_map/ppermute | solution.py:229
  102.5 35.2 %collective-permute-start.4 = (bf16[256,672]{1,0:T(8,128)(2,1)S(1)}, bf16[256,672]{1,0:T(8,128)(2,1)S(1)}, u32[]{:S(2)}, u32[]{:S(2)}) collective-permute-start(bf16[256,672]{1,0:T(8,128)(2,1)S(1)} %get-tuple-element.25), channel_id=1, source_target_pairs={{0,16},{8,24},{16,0},{24,8},{1,17},{9,25},{17,1},{25,9},{2,18},{10... | collective-permute-start | bytes 1032200 | tf_op jit(solution)/shard_map/ppermute | solution.py:229
  103.4 36.5 %collective-permute-start.5 = (bf16[256,672]{1,0:T(8,128)(2,1)S(1)}, bf16[256,672]{1,0:T(8,128)(2,1)S(1)}, u32[]{:S(2)}, u32[]{:S(2)}) collective-permute-start(bf16[256,672]{1,0:T(8,128)(2,1)S(1)} %get-tuple-element.26), channel_id=1, source_target_pairs={{0,8},{8,16},{16,24},{24,0},{1,9},{9,17},{17,25},{25,1},{2,10},{10... | collective-permute-start | bytes 1032200 | tf_op jit(solution)/shard_map/ppermute | solution.py:229

commit v2 on v1

v2 whole, which is shorter than its diff:
```python
import functools

import jax
import jax.numpy as jnp
from jax import lax
from jax.experimental import pallas as pl
from jax.experimental.pallas import tpu as pltpu
from jax.sharding import Mesh, PartitionSpec as P

HEADS = 28
HEAD_DIM = 96
GROUPS = 4
GROUP_HEADS = HEADS // GROUPS
GROUP_WIDTH = GROUP_HEADS * HEAD_DIM
PIECES = 8
NEG = -(2.0**99)
SCALE = HEAD_DIM ** (-0.5)
SEQ_AXES = ("zp", "zl", "x_lo", "core")
F32 = jnp.float32
BF16 = jnp.bfloat16
VMEM_LIMIT = 48 * 1024 * 1024
COST = dict(
    pack=1, join=1, forward=2, core=1, attended=1, backward=3, weight=2, add=30, unpack=10, add4=1, sum=10
)
NT = (((1,), (1,)), ((), ()))
NN = (((1,), (0,)), ((), ()))
TN = (((0,), (0,)), ((), ()))


def mm(a, b, dims):
    return lax.dot_general(a, b, dims, preferred_element_type=F32)


def pack_kernel(place, k_ref, v_ref, q_ref, *outs):
    chip = place[0]
    for g in range(GROUPS):
        cols = slice(g * GROUP_WIDTH, (g + 1) * GROUP_WIDTH)
        for s in range(GROUPS):

            @pl.when(lax.bitwise_xor(chip, s) == g)
            def _():
                outs[s][0] = k_ref[:, cols]
                outs[s][1] = v_ref[:, cols]
                if s == 0:
                    outs[GROUPS][...] = q_ref[:, cols]


def unpack_kernel(place, s0, s1, s2, s3, gk_ref, gv_ref):
    chip = place[0]
    slots = (s0, s1, s2, s3)
    for g in range(GROUPS):
        cols = slice(g * GROUP_WIDTH, (g + 1) * GROUP_WIDTH)
        for s in range(GROUPS):

            @pl.when(lax.bitwise_xor(chip, s) == g)
            def _():
                gk_ref[:, cols] = slots[s][0]
                gv_ref[:, cols] = slots[s][1]


def set_mask(place, ws_ref, bias):
    chip, pair, core = place[0], place[1], place[2]
    q_len = ws_ref.shape[1]
    kv_len = bias.shape[0] // GROUPS
    context = kv_len * GROUPS * PIECES
    rows = lax.broadcasted_iota(jnp.int32, (kv_len, q_len), 0)
    query_pos = context - q_len + lax.broadcasted_iota(jnp.int32, (kv_len, q_len), 1)
    for s in range(GROUPS):
        owner = pair * PIECES + 2 * lax.bitwise_xor(chip, s) + core
        key_pos = owner * kv_len + rows
        visible = (key_pos >= ws_ref[...]) & (key_pos <= query_pos)
        bias[s * kv_len : (s + 1) * kv_len, :] = jnp.where(visible, 0.0, NEG)


def join_kernel(place, m0, m1, m2, m3, theirs_ref, out_ref, pieces, rows):
    pair, core = place[1], place[2]
    rows_each = m0.shape[0]
    for j, mine in enumerate((m0, m1, m2, m3)):
        at = 2 * lax.bitwise_xor(pair, j)
        pieces[at + core] = mine[...].astype(F32)
        pieces[at + 1 - core] = theirs_ref[j].astype(F32)
    for k in range(PIECES):
        rows[k * rows_each : (k + 1) * rows_each, :] = pieces[k]
    out_ref[...] = rows[...].astype(BF16)


def head(h):
    return slice(h * HEAD_DIM, (h + 1) * HEAD_DIM)


def joined(slots, which, cols):
    return jnp.concatenate([s[which, :, cols] for s in slots], axis=0)


def halve(place, full, pieces, keep_ref, send_ref):
    core = place[2]
    rows_each = keep_ref.shape[1]
    for k in range(PIECES):
        pieces[k] = full[k * rows_each : (k + 1) * rows_each, :]
    for b in range(GROUPS):
        keep_ref[b] = pieces[2 * b + core]
        send_ref[b] = pieces[2 * b + 1 - core].astype(BF16)


def forward_kernel(place, ws_ref, q_ref, s0, s1, s2, s3, d_ref, keep_ref, send_ref, stats_ref, bias, att, pieces):
    slots = (s0, s1, s2, s3)
    set_mask(place, ws_ref, bias)
    stats_ref[...] = jnp.zeros_like(stats_ref)
    for h in range(GROUP_HEADS):
        kh = joined(slots, 0, head(h))
        vh = joined(slots, 1, head(h))
        scores = mm(kh, q_ref[:, head(h)], NT) * SCALE + bias[...]
        top = jnp.floor(jnp.max(scores, axis=0, keepdims=True) * 0.125) * 8.0
        expo = jnp.exp(scores - top)
        att[head(h), :] = mm(vh, expo.astype(BF16), TN)
        dots = jnp.sum(expo * mm(vh, d_ref[head(h), :], NN), axis=0, keepdims=True)
        stats_ref[0, h : h + 1, :] = top
        stats_ref[1, h : h + 1, :] = jnp.sum(expo, axis=0, keepdims=True)
        stats_ref[2, h : h + 1, :] = dots
    halve(place, att, pieces, keep_ref, send_ref)


def row_weights(spread, piece, rows_each):
    q_len = spread.shape[1]
    row = lax.broadcasted_iota(jnp.int32, (rows_each, q_len), 0)
    before = spread[pl.ds(piece + 7, 1), :]
    after = spread[pl.ds(piece + 8, 1), :]
    return jnp.where(row < (HEAD_DIM - rows_each) * piece, before, after)


def core_kernel(place, keep_ref, stats_ref, got_ref, got_stats_ref, o0, o1, o2, o3, spread, payload):
    pair, core = place[1], place[2]
    rows_each = keep_ref.shape[1]
    top = jnp.maximum(stats_ref[0], got_stats_ref[0])
    mine, other = jnp.exp(stats_ref[0] - top), jnp.exp(got_stats_ref[0] - top)
    total = mine * stats_ref[1] + other * got_stats_ref[1]
    dots = mine * stats_ref[2] + other * got_stats_ref[2]
    total_hi, dots_hi = total.astype(BF16).astype(F32), dots.astype(BF16).astype(F32)
    tail = jnp.concatenate([top, total_hi, total - total_hi, dots_hi, dots - dots_hi], axis=0)
    spread[...] = jnp.zeros_like(spread)
    spread[0, 8:16, :] = mine
    spread[1, 8:16, :] = other
    for b in range(GROUPS):
        piece = 2 * b + core
        payload[b, 80:88, :] = jnp.zeros_like(top)
        payload[b, :rows_each, :] = row_weights(spread.at[0], piece, rows_each) * keep_ref[b] + row_weights(
            spread.at[1], piece, rows_each
        ) * got_ref[b].astype(F32)
        payload[b, 88:, :] = tail
    for j, out in enumerate((o0, o1, o2, o3)):
        out[...] = payload[lax.bitwise_xor(pair, j)].astype(BF16)


def read_stats(parts):
    tops = [p[88:96, :].astype(F32) for p in parts]
    top = functools.reduce(jnp.maximum, tops)
    scaled = [jnp.exp(t - top) for t in tops]
    total = sum(w * (p[96:104].astype(F32) + p[104:112].astype(F32)) for w, p in zip(scaled, parts))
    inverse = 1.0 / jnp.where(total > 0.0, total, 1.0)
    dots = sum(w * (p[112:120].astype(F32) + p[120:128].astype(F32)) for w, p in zip(scaled, parts)) * inverse
    return top, inverse, dots, scaled


def attended_kernel(place, p0, p1, p2, p3, out_ref, spread):
    rows_each = out_ref.shape[0]
    parts = [p[...].astype(F32) for p in (p0, p1, p2, p3)]
    _, inverse, _, scaled = read_stats(parts)
    spread[...] = jnp.zeros_like(spread)
    total = jnp.zeros(out_ref.shape, F32)
    for j, part in enumerate(parts):
        spread[j, 8:16, :] = scaled[j] * inverse
        total += row_weights(spread.at[j], 2 * place[1] + place[2], rows_each) * part[:rows_each]
    out_ref[...] = total.astype(BF16)


def backward_kernel(
    place, ws_ref, q_ref, s0, s1, s2, s3, d_ref, p0, p1, p2, p3, o0, o1, o2, o3, keep_ref, send_ref, bias, gq, pieces, stats
):
    kv_len = s0.shape[1]
    slots = (s0, s1, s2, s3)
    set_mask(place, ws_ref, bias)
    stats[0], stats[1], stats[2], _ = read_stats([p[...].astype(F32) for p in (p0, p1, p2, p3)])
    for h in range(GROUP_HEADS):
        kh = joined(slots, 0, head(h))
        vh = joined(slots, 1, head(h))
        qh = q_ref[:, head(h)]
        dh = d_ref[head(h), :]
        scores = mm(kh, qh, NT) * SCALE + bias[...]
        probs = jnp.exp(scores - stats[0, h : h + 1, :]) * stats[1, h : h + 1, :]
        dscores = probs * (mm(vh, dh, NN) - stats[2, h : h + 1, :])
        probs = probs.astype(BF16)
        dscores = dscores.astype(BF16)
        gk = (mm(dscores, qh, NN) * SCALE).astype(BF16)
        gv = mm(probs, dh, NT).astype(BF16)
        for s, out in enumerate((o0, o1, o2, o3)):
            part = slice(s * kv_len, (s + 1) * kv_len)
            out[0, :, head(h)] = gk[part]
            out[1, :, head(h)] = gv[part]
        gq[head(h), :] = mm(kh, dscores, TN) * SCALE
    halve(place, gq, pieces, keep_ref, send_ref)


def add_kernel(place, keep_ref, got_ref, o0, o1, o2, o3, pieces):
    for b in range(GROUPS):
        pieces[b] = keep_ref[b] + got_ref[b].astype(F32)
    for j, out in enumerate((o0, o1, o2, o3)):
        out[...] = pieces[lax.bitwise_xor(place[1], j)].astype(BF16)


def weight_kernel(att_ref, cot_ref, out_ref, full):
    pieces, _, width = out_ref.shape
    full[...] = mm(att_ref[...], cot_ref[...], NT)
    for s in range(pieces):
        out_ref[s] = full[:, s * width : (s + 1) * width].astype(BF16)


def sum_kernel(x_ref, out_ref):
    out_ref[...] = sum(x_ref[j].astype(F32) for j in range(x_ref.shape[0])).astype(BF16)


def add4_kernel(x0, x1, x2, x3, out_ref):
    out_ref[...] = sum(x[...].astype(F32) for x in (x0, x1, x2, x3)).astype(BF16)


SMEM = pl.BlockSpec(memory_space=pltpu.SMEM)
WHOLE = pl.BlockSpec(memory_space=pltpu.VMEM)


def call(name, kernel, n_in, out_shapes, scratch=(), scalars=1, grid=(), in_blocks=None, out_blocks=None):
    return pl.pallas_call(
        kernel,
        out_shape=out_shapes,
        grid=grid,
        in_specs=[SMEM] * scalars + (in_blocks or [WHOLE] * n_in),
        out_specs=out_blocks or jax.tree.map(lambda _: WHOLE, out_shapes),
        scratch_shapes=list(scratch),
        compiler_params=pltpu.CompilerParams(vmem_limit_bytes=VMEM_LIMIT),
        cost_estimate=pl.CostEstimate(flops=int(COST[name] * 1e9), bytes_accessed=0, transcendentals=0),
        name=name,
    )


def rows_block(shape, dim):
    block = tuple(n // 4 if d == dim else n for d, n in enumerate(shape))
    return pl.BlockSpec(block, lambda i: tuple(i if d == dim else 0 for d in range(len(shape))))


ALL = [(a, b) for a in range(GROUPS) for b in range(GROUPS)]


def swap_chip(x, s):
    return lax.ppermute(x, ("zl", "x_lo"), [(i, i ^ s) for i in range(GROUPS)])


def swap_pair(x, j):
    return lax.ppermute(x, "zp", [(i, i ^ j) for i in range(GROUPS)])


def swap_core(x):
    return lax.ppermute(x, "core", [(0, 1), (1, 0)])


def to_holder(x, j):
    return lax.ppermute(x, ("zp", "zl", "x_lo"), [(a * GROUPS + b, (b ^ j) * GROUPS + a) for a, b in ALL])


def to_owner(x, j):
    return lax.ppermute(x, ("zp", "zl", "x_lo"), [((b ^ j) * GROUPS + a, a * GROUPS + b) for a, b in ALL])


def local(queries, keys, values, out_grad, w_out, window_start):
    query, key_rows, value_rows, cotangent = queries[0], keys[0], values[0], out_grad[0].T
    q_len = query.shape[0]
    kv_len, width = key_rows.shape
    rows_each, model = w_out.shape
    sections = lax.axis_size("section")
    place = jnp.stack([lax.axis_index(("zl", "x_lo")), lax.axis_index("zp"), lax.axis_index("core")]).astype(jnp.int32)
    starts = window_start.reshape(1, q_len)
    sds = jax.ShapeDtypeStruct
    four = range(GROUPS)
    slots4 = [sds((2, kv_len, GROUP_WIDTH), BF16)] * GROUPS
    halves = [sds((GROUPS, rows_each, q_len), F32), sds((GROUPS, rows_each, q_len), BF16)]
    bias = pltpu.VMEM((GROUPS * kv_len, q_len), F32)
    features = pltpu.VMEM((GROUP_WIDTH, q_len), F32)
    pieces = pltpu.VMEM((PIECES, rows_each, q_len), F32)

    cut = [rows_block((2, kv_len, GROUP_WIDTH), 1)] * GROUPS
    *send, q_own = call(
        "pack",
        pack_kernel,
        3,
        slots4 + [sds((q_len, GROUP_WIDTH), BF16)],
        grid=(4,),
        in_blocks=[rows_block(x.shape, 0) for x in (key_rows, value_rows, query)],
        out_blocks=cut + [rows_block((q_len, GROUP_WIDTH), 0)],
    )(place, key_rows, value_rows, query)
    w_out, send = lax.optimization_barrier((w_out, send))
    slots = [send[0]] + [swap_chip(send[s], s) for s in range(1, GROUPS)]
    d_own = lax.dot_general(w_out, cotangent, NN, preferred_element_type=F32).astype(BF16)
    mine = [to_holder(d_own, j) for j in four]
    theirs = swap_core(jnp.stack(mine))
    d_group = call("join", join_kernel, 5, sds((GROUP_WIDTH, q_len), BF16), [pieces, features])(place, *mine, theirs)

    keep, half, stats = call(
        "forward", forward_kernel, 7, halves + [sds((3, 8, q_len), F32)], [bias, features, pieces]
    )(place, starts, q_own, *slots, d_group)
    parts = call(
        "core",
        core_kernel,
        4,
        [sds((128, q_len), BF16)] * GROUPS,
        [pltpu.VMEM((2, 24, q_len), F32), pltpu.VMEM((GROUPS, 128, q_len), F32)],
    )(place, keep, stats, swap_core(half), swap_core(stats))
    parts = [parts[0]] + [swap_pair(parts[j], j) for j in range(1, GROUPS)]
    attended = call(
        "attended", attended_kernel, 4, sds((rows_each, q_len), BF16), [pltpu.VMEM((GROUPS, 24, q_len), F32)]
    )(place, *parts)
    attended, parts = lax.optimization_barrier((attended, parts))
    attended = to_owner(attended, 0)

    *back, keep, half = call(
        "backward", backward_kernel, 11, slots4 + halves, [bias, features, pieces, pltpu.VMEM((3, 8, q_len), F32)]
    )(place, starts, q_own, *slots, d_group, *parts)
    attended, keep = lax.optimization_barrier((attended, keep))
    back = [back[0]] + [swap_chip(back[s], s) for s in range(1, GROUPS)]

    part = model // sections
    gw = call(
        "weight", weight_kernel, 2, sds((sections, rows_each, part), BF16), [pltpu.VMEM((rows_each, model), F32)], scalars=0
    )(attended, cotangent)
    gw = lax.all_to_all(gw, "section", 0, 0)

    gq = call("add", add_kernel, 2, [sds((rows_each, q_len), BF16)] * GROUPS, [pltpu.VMEM((GROUPS, rows_each, q_len), F32)])(
        place, keep, swap_core(half)
    )
    gq = [to_owner(gq[j], j) for j in four]

    grad_weight = call("sum", sum_kernel, 1, sds((rows_each, part), BF16), scalars=0)(gw)
    grad_weight, back = lax.optimization_barrier((grad_weight, back))
    grad_k, grad_v = call(
        "unpack",
        unpack_kernel,
        4,
        [sds((kv_len, width), BF16)] * 2,
        grid=(4,),
        in_blocks=cut,
        out_blocks=[rows_block((kv_len, width), 0)] * 2,
    )(place, *back)
    grad_q = call("add4", add4_kernel, 4, sds((rows_each, q_len), BF16), scalars=0)(*gq)
    return grad_q[None], grad_k[None], grad_v[None], grad_weight


def solution(mesh):
    sections = mesh.shape["section"]
    fine = Mesh(mesh.devices.reshape(sections, GROUPS, 2, 2, 2), ("section",) + SEQ_AXES)
    return jax.shard_map(
        local,
        mesh=fine,
        in_specs=(
            P("section", None, None),
            P("section", SEQ_AXES, None),
            P("section", SEQ_AXES, None),
            P("section", None, None),
            P(SEQ_AXES, None),
            P(),
        ),
        out_specs=(
            P("section", SEQ_AXES, None),
            P("section", SEQ_AXES, None),
            P("section", SEQ_AXES, None),
            P(SEQ_AXES, "section"),
        ),
        check_vma=False,
    )
```

time: 146 us -> 119 us (0.82)
  the two profiles are of different devices: /device:TPU:39 before, /device:TPU:6 now
where the time goes in v2:
time: 119 us; the launch traced here: 117 us
  starting transfers between devices  54.9 us (46%)
  waiting for transfers between devices  35.1 us (29%)
  Pallas kernels  19.7 us (17%)
  local copies, waits for them, and re-layouts  6.17 us (5%)
    ppermute x6, waiting for transfers between devices, swap_chip(): return lax.ppermute(x, ('zl', 'x_lo'), [(i, i ^ s) for i in range(GROUPS)])  23 us
    ppermute x5, starting transfers between devices, to_owner(): lax.ppermute(x, ('zp', 'zl', 'x_lo'), [((b ^ j) * GROUPS + a, a * GROUPS...  16.3 us
    ppermute x4, starting transfers between devices, to_holder(): lax.ppermute(x, ('zp', 'zl', 'x_lo'), [(a * GROUPS + b, (b ^ j) * GROUPS...  14.2 us
    ppermute x6, starting transfers between devices, swap_chip(): return lax.ppermute(x, ('zl', 'x_lo'), [(i, i ^ s) for i in range(GROUPS)])  9.71 us
    all_to_all x1, starting transfers between devices, local(): gw = lax.all_to_all(gw, 'section', 0, 0)  7.43 us
    ppermute x3, starting transfers between devices, swap_pair(): return lax.ppermute(x, 'zp', [(i, i ^ j) for i in range(GROUPS)])  6.61 us
    unnamed x20, local copies, waits for them, and re-layouts  6.17 us
    ppermute x3, waiting for transfers between devices, swap_pair(): return lax.ppermute(x, 'zp', [(i, i ^ j) for i in range(GROUPS)])  5.59 us
  transfers between devices with their start and end apart: 23, of which 13 were waited for; matrix products, arithmetic and copies ran while one was open for 0% of the time, Pallas kernels for 7%

profile of v2, /device:TPU:6, one launch (start us, length us, event | category | flops | bytes accessed | tf_op | source)
XLA Modules:
  0.0 117.4 jit_solution(7143715325882271648)
XLA Ops:
  0.7 1.5 %copy-done.2 = bf16[1,256,2688]{2,1,0:T(8,128)(2,1)S(1)} copy-done((bf16[1,256,2688]{2,1,0:T(8,128)(2,1)S(1)}, bf16[1,256,2688]{2,1,0:T(8,128)(2,1)}, u32[]{:S(2)}) %copy-start.2) | copy-done | bytes 1376280
  2.2 1.1 copy-done.3
  3.3 1.1 copy-done.4
  4.4 2.2 %pack.1 = (bf16[2,128,672]{2,1,0:T(8,128)(2,1)S(1)}, bf16[2,128,672]{2,1,0:T(8,128)(2,1)S(1)}, bf16[2,128,672]{2,1,0:T(8,128)(2,1)S(1)}, bf16[2,128,672]{2,1,0:T(8,128)(2,1)S(1)}, bf16[256,672]{1,0:T(8,128)(2,1)S(1)}) custom-call(s32[3]{0:T(128)S(1)} %pad_add_fusion.place, bf16[128,2688]{1,0:T(8,128)(2,1)S(1)} %bitcast.28, bf16[128,2688]{1,0:T(8,128)(2,1)S(1)} %bitcast.29, ...), custom_call_target="tpu_custom_call" | custom-call | flops 1000000000 | tf_op jit(solution)/shard_map/pack/pallas_call | solution.py:288
  6.7 0.6 fusion.2
  7.3 5.4 %collective-permute-start.3 = (bf16[84,256]{1,0:T(8,128)(2,1)S(1)}, bf16[84,256]{1,0:T(8,128)(2,1)S(1)}, u32[]{:S(2)}, u32[]{:S(2)}) collective-permute-start(bf16[84,256]{1,0:T(8,128)(2,1)S(1)} %fusion.2), channel_id=1, source_target_pairs={{0,0},{2,8},{4,16},{6,24},{8,2},{10,10},{12,18},{14,26},{16,4},{18... | collective-permute-start | bytes 129032 | tf_op jit(solution)/shard_map/ppermute | solution.py:264
  12.7 8.8 %collective-permute-start.5 = (bf16[84,256]{1,0:T(8,128)(2,1)S(1)}, bf16[84,256]{1,0:T(8,128)(2,1)S(1)}, u32[]{:S(2)}, u32[]{:S(2)}) collective-permute-start(bf16[84,256]{1,0:T(8,128)(2,1)S(1)} %fusion.2), channel_id=1, source_target_pairs={{0,16},{2,24},{4,0},{6,8},{8,18},{10,26},{12,2},{14,10},{16,20},{1... | collective-permute-start | bytes 129032 | tf_op jit(solution)/shard_map/ppermute | solution.py:264
  21.5 0.6 collective-permute-start
  22.1 2.2 %collective-permute-start.1 = (bf16[2,128,672]{2,1,0:T(8,128)(2,1)S(1)}, bf16[2,128,672]{2,1,0:T(8,128)(2,1)S(1)}, u32[]{:S(2)}, u32[]{:S(2)}) collective-permute-start(bf16[2,128,672]{2,1,0:T(8,128)(2,1)S(1)} %get-tuple-element.52), channel_id=1, source_target_pairs={{0,4},{2,6},{4,0},{6,2},{1,5},{3,7},{5,1},{7,3},{8,12},{10,14},{12... | collective-permute-start | bytes 1032200 | tf_op jit(solution)/shard_map/ppermute | solution.py:252
  24.3 3.1 %collective-permute-start.2 = (bf16[2,128,672]{2,1,0:T(8,128)(2,1)S(1)}, bf16[2,128,672]{2,1,0:T(8,128)(2,1)S(1)}, u32[]{:S(2)}, u32[]{:S(2)}) collective-permute-start(bf16[2,128,672]{2,1,0:T(8,128)(2,1)S(1)} %get-tuple-element.53), channel_id=1, source_target_pairs={{0,6},{2,4},{4,2},{6,0},{1,7},{3,5},{5,3},{7,1},{8,14},{10,12},{12... | collective-permute-start | bytes 1032200 | tf_op jit(solution)/shard_map/ppermute | solution.py:252
  27.4 0.7 collective-permute-done.6.m3
  28.1 0.1 collective-permute-start.7
  28.2 1.4 %collective-permute-done.7.theirs_ref = bf16[4,84,256]{2,1,0:T(8,128)(2,1)S(1)} collective-permute-done((bf16[4,84,256]{2,1,0:T(8,128)(2,1)S(1)}, bf16[4,84,256]{2,1,0:T(8,128)(2,1)S(1)}, u32[]{:S(2)}, u32[]{:S(2)}) %collective-permute-start.7) | collective-permute-done | bytes 172064 | tf_op jit(solution)/shard_map/ppermute | solution.py:260
  29.6 0.6 join.1.d_ref
  30.3 2.4 %collective-permute-done.s1 = bf16[2,128,672]{2,1,0:T(8,128)(2,1)S(1)} collective-permute-done((bf16[2,128,672]{2,1,0:T(8,128)(2,1)S(1)}, bf16[2,128,672]{2,1,0:T(8,128)(2,1)S(1)}, u32[]{:S(2)}, u32[]{:S(2)}) %collective-permute-start) | collective-permute-done | bytes 344096 | tf_op jit(solution)/shard_map/ppermute | solution.py:252
  32.6 2.1 %collective-permute-done.1.s2 = bf16[2,128,672]{2,1,0:T(8,128)(2,1)S(1)} collective-permute-done((bf16[2,128,672]{2,1,0:T(8,128)(2,1)S(1)}, bf16[2,128,672]{2,1,0:T(8,128)(2,1)S(1)}, u32[]{:S(2)}, u32[]{:S(2)}) %collective-permute-start.1) | collective-permute-done | bytes 344096 | tf_op jit(solution)/shard_map/ppermute | solution.py:252
  34.8 6.3 %collective-permute-done.2.s3 = bf16[2,128,672]{2,1,0:T(8,128)(2,1)S(1)} collective-permute-done((bf16[2,128,672]{2,1,0:T(8,128)(2,1)S(1)}, bf16[2,128,672]{2,1,0:T(8,128)(2,1)S(1)}, u32[]{:S(2)}, u32[]{:S(2)}) %collective-permute-start.2) | collective-permute-done | bytes 344096 | tf_op jit(solution)/shard_map/ppermute | solution.py:252
  41.1 3.5 %forward.1 = (f32[4,84,256]{2,1,0:T(8,128)S(1)}, bf16[4,84,256]{2,1,0:T(8,128)(2,1)S(1)}, f32[3,8,256]{2,1,0:T(8,128)S(1)}) custom-call(s32[3]{0:T(128)S(1)} %pad_add_fusion.place, s32[1,256]{1,0:T(1,128)S(1)} %bitcast.30, bf16[256,672]{1,0:T(8,128)(2,1)S(1)} %get-tuple-element.45.q_ref, bf16[2,128,672]{2,1,0:T(8,128)(2,1)S(1)} %get-tuple-element.50.s0, ...), custom_call_target="tpu_custom_call" | custom-call | flops 2000000000 | tf_op jit(solution)/shard_map/forward/pallas_call | solution.py:304
  44.7 0.1 collective-permute-start.8
  44.8 0.5 collective-permute-start.9
  45.3 0.9 collective-permute-done.9.got_stats_ref
  46.2 0.7 core.1
  46.9 2.9 %collective-permute-start.10 = (bf16[128,256]{1,0:T(8,128)(2,1)S(1)}, bf16[128,256]{1,0:T(8,128)(2,1)S(1)}, u32[]{:S(2)}, u32[]{:S(2)}) collective-permute-start(bf16[128,256]{1,0:T(8,128)(2,1)S(1)} %get-tuple-element.59), channel_id=1, source_target_pairs={{0,8},{8,0},{16,24},{24,16},{1,9},{9,1},{17,25},{25,17},{2,10},{10... | collective-permute-start | bytes 196616 | tf_op jit(solution)/shard_map/ppermute | solution.py:256
  49.8 1.7 %collective-permute-start.11 = (bf16[128,256]{1,0:T(8,128)(2,1)S(1)}, bf16[128,256]{1,0:T(8,128)(2,1)S(1)}, u32[]{:S(2)}, u32[]{:S(2)}) collective-permute-start(bf16[128,256]{1,0:T(8,128)(2,1)S(1)} %get-tuple-element.60), channel_id=1, source_target_pairs={{0,16},{8,24},{16,0},{24,8},{1,17},{9,25},{17,1},{25,9},{2,18},{10... | collective-permute-start | bytes 196616 | tf_op jit(solution)/shard_map/ppermute | solution.py:256
  51.5 2.0 %collective-permute-start.12 = (bf16[128,256]{1,0:T(8,128)(2,1)S(1)}, bf16[128,256]{1,0:T(8,128)(2,1)S(1)}, u32[]{:S(2)}, u32[]{:S(2)}) collective-permute-start(bf16[128,256]{1,0:T(8,128)(2,1)S(1)} %get-tuple-element.61), channel_id=1, source_target_pairs={{0,24},{8,16},{16,8},{24,0},{1,25},{9,17},{17,9},{25,1},{2,26},{10... | collective-permute-start | bytes 196616 | tf_op jit(solution)/shard_map/ppermute | solution.py:256
  53.5 0.3 collective-permute-done.10.p1
  53.8 4.8 %collective-permute-done.11.p2 = bf16[128,256]{1,0:T(8,128)(2,1)S(1)} collective-permute-done((bf16[128,256]{1,0:T(8,128)(2,1)S(1)}, bf16[128,256]{1,0:T(8,128)(2,1)S(1)}, u32[]{:S(2)}, u32[]{:S(2)}) %collective-permute-start.11) | collective-permute-done | bytes 65568 | tf_op jit(solution)/shard_map/ppermute | solution.py:256
  58.6 0.5 collective-permute-done.12.p3
  59.1 0.6 attended.1
  59.7 6.5 %collective-permute-start.13 = (bf16[84,256]{1,0:T(8,128)(2,1)S(1)}, bf16[84,256]{1,0:T(8,128)(2,1)S(1)}, u32[]{:S(2)}, u32[]{:S(2)}) collective-permute-start(bf16[84,256]{1,0:T(8,128)(2,1)S(1)} %attended.1), channel_id=1, source_target_pairs={{0,0},{8,2},{16,4},{24,6},{2,8},{10,10},{18,12},{26,14},{4,16},{12... | collective-permute-start | bytes 129032 | tf_op jit(solution)/shard_map/ppermute | solution.py:268
  66.2 3.4 %backward.1 = (bf16[2,128,672]{2,1,0:T(8,128)(2,1)S(1)}, bf16[2,128,672]{2,1,0:T(8,128)(2,1)S(1)}, bf16[2,128,672]{2,1,0:T(8,128)(2,1)S(1)}, bf16[2,128,672]{2,1...) custom-call(s32[3]{0:T(128)S(1)} %pad_add_fusion.place, s32[1,256]{1,0:T(1,128)S(1)} %bitcast.31, ...), custom_call_target="tpu_custom_call" | custom-call | flops 3000000000 | tf_op jit(solution)/shard_map/backward/pallas_call | solution.py:321
  69.6 0.7 copy-done.6
  70.4 0.7 copy-done.8
  71.1 2.0 %weight.1 = bf16[8,84,660]{2,1,0:T(8,128)(2,1)} custom-call(bf16[84,256]{1,0:T(8,128)(2,1)S(1)} %collective-permute-done.13.att_ref, bf16[5280,256]{1,0:T(8,128)(2,1)S(1)} %bitcast.22), custom_call_target="tpu_custom_call" | custom-call | flops 2000000000 | tf_op jit(solution)/shard_map/weight/pallas_call | solution.py:328
  73.2 7.4 %all-to-all-start = ((bf16[8,84,660]{2,1,0:T(8,128)(2,1)}), bf16[8,84,660]{2,1,0:T(8,128)(2,1)S(1)}, u32[]{:S(2)}, u32[]{:S(2)}) async-start(bf16[8,84,660]{2,1,0:T(8,128)(2,1)} %weight.1), calls=%async_computation | async-start | bytes 2162688 | tf_op jit(solution)/shard_map/all_to_all | solution.py:331
  80.6 1.0 copy-done.9
  81.6 1.0 add.9
  82.6 2.6 %collective-permute-start.15 = (bf16[84,256]{1,0:T(8,128)(2,1)S(1)}, bf16[84,256]{1,0:T(8,128)(2,1)S(1)}, u32[]{:S(2)}, u32[]{:S(2)}) collective-permute-start(bf16[84,256]{1,0:T(8,128)(2,1)S(1)} %get-tuple-element.70), channel_id=1, source_target_pairs={{0,0},{8,2},{16,4},{24,6},{2,8},{10,10},{18,12},{26,14},{4,16},{12... | collective-permute-start | bytes 129032 | tf_op jit(solution)/shard_map/ppermute | solution.py:268
  85.3 4.9 %collective-permute-start.17 = (bf16[84,256]{1,0:T(8,128)(2,1)S(1)}, bf16[84,256]{1,0:T(8,128)(2,1)S(1)}, u32[]{:S(2)}, u32[]{:S(2)}) collective-permute-start(bf16[84,256]{1,0:T(8,128)(2,1)S(1)} %get-tuple-element.72), channel_id=1, source_target_pairs={{16,0},{24,2},{0,4},{8,6},{18,8},{26,10},{2,12},{10,14},{20,16},{2... | collective-permute-start | bytes 129032 | tf_op jit(solution)/shard_map/ppermute | solution.py:268
  90.2 2.2 %collective-permute-start.18 = (bf16[84,256]{1,0:T(8,128)(2,1)S(1)}, bf16[84,256]{1,0:T(8,128)(2,1)S(1)}, u32[]{:S(2)}, u32[]{:S(2)}) collective-permute-start(bf16[84,256]{1,0:T(8,128)(2,1)S(1)} %get-tuple-element.73), channel_id=1, source_target_pairs={{24,0},{16,2},{8,4},{0,6},{26,8},{18,10},{10,12},{2,14},{28,16},{2... | collective-permute-start | bytes 129032 | tf_op jit(solution)/shard_map/ppermute | solution.py:268
  92.4 3.8 %collective-permute-start.20 = (bf16[2,128,672]{2,1,0:T(8,128)(2,1)S(1)}, bf16[2,128,672]{2,1,0:T(8,128)(2,1)}, u32[]{:S(2)}, u32[]{:S(2)}) collective-permute-start(bf16[2,128,672]{2,1,0:T(8,128)(2,1)S(1)} %get-tuple-element.77), channel_id=1, source_target_pairs={{0,4},{2,6},{4,0},{6,2},{1,5},{3,7},{5,1},{7,3},{8,12},{10,14},{12... | collective-permute-start | bytes 1032200 | tf_op jit(solution)/shard_map/ppermute | solution.py:252
  96.2 3.4 %collective-permute-done.18.x3 = bf16[84,256]{1,0:T(8,128)(2,1)S(1)} collective-permute-done((bf16[84,256]{1,0:T(8,128)(2,1)S(1)}, bf16[84,256]{1,0:T(8,128)(2,1)S(1)}, u32[]{:S(2)}, u32[]{:S(2)}) %collective-permute-start.18) | collective-permute-done | bytes 43040 | tf_op jit(solution)/shard_map/ppermute | solution.py:268
  99.6 0.6 add4.1
  100.2 0.8 sum.1
  101.0 3.2 %collective-permute-done.19.s1 = bf16[2,128,672]{2,1,0:T(8,128)(2,1)} collective-permute-done((bf16[2,128,672]{2,1,0:T(8,128)(2,1)S(1)}, bf16[2,128,672]{2,1,0:T(8,128)(2,1)}, u32[]{:S(2)}, u32[]{:S(2)}) %collective-permute-start.19) | collective-permute-done | bytes 344096 | tf_op jit(solution)/shard_map/ppermute | solution.py:252
  104.2 2.2 %collective-permute-done.20.s2 = bf16[2,128,672]{2,1,0:T(8,128)(2,1)} collective-permute-done((bf16[2,128,672]{2,1,0:T(8,128)(2,1)S(1)}, bf16[2,128,672]{2,1,0:T(8,128)(2,1)}, u32[]{:S(2)}, u32[]{:S(2)}) %collective-permute-start.20) | collective-permute-done | bytes 344096 | tf_op jit(solution)/shard_map/ppermute | solution.py:252
  106.4 6.8 %collective-permute-done.21.s3 = bf16[2,128,672]{2,1,0:T(8,128)(2,1)} collective-permute-done((bf16[2,128,672]{2,1,0:T(8,128)(2,1)S(1)}, bf16[2,128,672]{2,1,0:T(8,128)(2,1)}, u32[]{:S(2)}, u32[]{:S(2)}) %collective-permute-start.21) | collective-permute-done | bytes 344096 | tf_op jit(solution)/shard_map/ppermute | solution.py:252
  113.2 4.2 %unpack.1 = (bf16[128,2688]{1,0:T(8,128)(2,1)}, bf16[128,2688]{1,0:T(8,128)(2,1)}) custom-call(s32[3]{0:T(128)S(1)} %pad_add_fusion.place, bf16[2,128,672]{2,1,0:T(8,128)(2,1)S(1)} %copy-done.7, bf16[2,128,672]{2,1,0:T(8,128)(2,1)} %collective-permute-done.19.s1, bf16[2,128,672]{2,1,0:T(8,128)(2,1)} %collective-permute-done.20.s2, ...), custom_call_target="tpu_custom_call" | custom-call | flops 10000000000 | tf_op jit(solution)/shard_map/unpack/pallas_call | solution.py:340
  (32 shorter events, 0.3 us)
Async XLA Ops:
  0.6 6.0 %copy-start = (bf16[84,5280]{1,0:T(8,128)(2,1)S(1)}, bf16[84,5280]{1,0:T(8,128)(2,1)}, u32[]{:S(2)}) copy-start(bf16[84,5280]{1,0:T(8,128)(2,1)} %param.10) | copy-start | bytes 2661124
  0.7 6.0 %copy-start.1 = (bf16[1,256,5280]{1,2,0:T(8,128)(2,1)S(1)}, bf16[1,256,5280]{1,2,0:T(8,128)(2,1)}, u32[]{:S(2)}) copy-start(bf16[1,256,5280]{1,2,0:T(8,128)(2,1)} %param.9) | copy-start | bytes 8110084
  0.7 1.5 %copy-start.2 = (bf16[1,256,2688]{2,1,0:T(8,128)(2,1)S(1)}, bf16[1,256,2688]{2,1,0:T(8,128)(2,1)}, u32[]{:S(2)}) copy-start(bf16[1,256,2688]{2,1,0:T(8,128)(2,1)} %param.6) | copy-start | bytes 4128772
  2.2 1.1 copy-start.3
  3.3 1.1 copy-start.4
  7.2 33.9 %copy-start.5 = (s32[256]{0:T(256)S(1)}, s32[256]{0:T(256)}, u32[]{:S(2)}) copy-start(s32[256]{0:T(256)} %param.11) | copy-start | bytes 3076
  7.3 14.8 %collective-permute-start.3 = (bf16[84,256]{1,0:T(8,128)(2,1)S(1)}, bf16[84,256]{1,0:T(8,128)(2,1)S(1)}, u32[]{:S(2)}, u32[]{:S(2)}) collective-permute-start(bf16[84,256]{1,0:T(8,128)(2,1)S(1)} %fusion.2), channel_id=1, source_target_pairs={{0,0},{2,8},{4,16},{6,24},{8,2},{10,10},{12,18},{14,26},{16,4},{18... | collective-permute-start | bytes 129032 | tf_op jit(solution)/shard_map/ppermute | solution.py:264
  12.6 11.6 %collective-permute-start.4 = (bf16[84,256]{1,0:T(8,128)(2,1)S(1)}, bf16[84,256]{1,0:T(8,128)(2,1)S(1)}, u32[]{:S(2)}, u32[]{:S(2)}) collective-permute-start(bf16[84,256]{1,0:T(8,128)(2,1)S(1)} %fusion.2), channel_id=1, source_target_pairs={{0,8},{2,0},{4,24},{6,16},{8,10},{10,2},{12,26},{14,18},{16,12},{1... | collective-permute-start | bytes 129032 | tf_op jit(solution)/shard_map/ppermute | solution.py:264
  12.7 14.6 %collective-permute-start.5 = (bf16[84,256]{1,0:T(8,128)(2,1)S(1)}, bf16[84,256]{1,0:T(8,128)(2,1)S(1)}, u32[]{:S(2)}, u32[]{:S(2)}) collective-permute-start(bf16[84,256]{1,0:T(8,128)(2,1)S(1)} %fusion.2), channel_id=1, source_target_pairs={{0,16},{2,24},{4,0},{6,8},{8,18},{10,26},{12,2},{14,10},{16,20},{1... | collective-permute-start | bytes 129032 | tf_op jit(solution)/shard_map/ppermute | solution.py:264
  21.5 6.6 %collective-permute-start.6 = (bf16[84,256]{1,0:T(8,128)(2,1)S(1)}, bf16[84,256]{1,0:T(8,128)(2,1)S(1)}, u32[]{:S(2)}, u32[]{:S(2)}) collective-permute-start(bf16[84,256]{1,0:T(8,128)(2,1)S(1)} %fusion.2), channel_id=1, source_target_pairs={{0,24},{2,16},{4,8},{6,0},{8,26},{10,18},{12,10},{14,2},{16,28},{1... | collective-permute-start | bytes 129032 | tf_op jit(solution)/shard_map/ppermute | solution.py:264
  21.5 11.1 %collective-permute-start = (bf16[2,128,672]{2,1,0:T(8,128)(2,1)S(1)}, bf16[2,128,672]{2,1,0:T(8,128)(2,1)S(1)}, u32[]{:S(2)}, u32[]{:S(2)}) collective-permute-start(bf16[2,128,672]{2,1,0:T(8,128)(2,1)S(1)} %get-tuple-element.51), channel_id=1, source_target_pairs={{0,2},{2,0},{4,6},{6,4},{1,3},{3,1},{5,7},{7,5},{8,10},{10,8},{12,... | collective-permute-start | bytes 1032200 | tf_op jit(solution)/shard_map/ppermute | solution.py:252
  22.1 12.7 %collective-permute-start.1 = (bf16[2,128,672]{2,1,0:T(8,128)(2,1)S(1)}, bf16[2,128,672]{2,1,0:T(8,128)(2,1)S(1)}, u32[]{:S(2)}, u32[]{:S(2)}) collective-permute-start(bf16[2,128,672]{2,1,0:T(8,128)(2,1)S(1)} %get-tuple-element.52), channel_id=1, source_target_pairs={{0,4},{2,6},{4,0},{6,2},{1,5},{3,7},{5,1},{7,3},{8,12},{10,14},{12... | collective-permute-start | bytes 1032200 | tf_op jit(solution)/shard_map/ppermute | solution.py:252
  24.3 16.8 %collective-permute-start.2 = (bf16[2,128,672]{2,1,0:T(8,128)(2,1)S(1)}, bf16[2,128,672]{2,1,0:T(8,128)(2,1)S(1)}, u32[]{:S(2)}, u32[]{:S(2)}) collective-permute-start(bf16[2,128,672]{2,1,0:T(8,128)(2,1)S(1)} %get-tuple-element.53), channel_id=1, source_target_pairs={{0,6},{2,4},{4,2},{6,0},{1,7},{3,5},{5,3},{7,1},{8,14},{10,12},{12... | collective-permute-start | bytes 1032200 | tf_op jit(solution)/shard_map/ppermute | solution.py:252
  28.1 1.5 %collective-permute-start.7 = (bf16[4,84,256]{2,1,0:T(8,128)(2,1)S(1)}, bf16[4,84,256]{2,1,0:T(8,128)(2,1)S(1)}, u32[]{:S(2)}, u32[]{:S(2)}) collective-permute-start(bf16[4,84,256]{2,1,0:T(8,128)(2,1)S(1)} %pad_maximum_fusion), channel_id=1, source_target_pairs={{0,1},{1,0},{2,3},{3,2},{4,5},{5,4},{6,7},{7,6},{8,9},{9,8},{10,11... | collective-permute-start | bytes 516104 | tf_op jit(solution)/shard_map/ppermute | solution.py:260
  44.7 1.5 %collective-permute-start.8 = (bf16[4,84,256]{2,1,0:T(8,128)(2,1)S(1)}, bf16[4,84,256]{2,1,0:T(8,128)(2,1)S(1)}, u32[]{:S(2)}, u32[]{:S(2)}) collective-permute-start(bf16[4,84,256]{2,1,0:T(8,128)(2,1)S(1)} %get-tuple-element.57), channel_id=1, source_target_pairs={{0,1},{1,0},{2,3},{3,2},{4,5},{5,4},{6,7},{7,6},{8,9},{9,8},{10,11... | collective-permute-start | bytes 516104 | tf_op jit(solution)/shard_map/ppermute | solution.py:260
  44.8 1.4 %collective-permute-start.9 = (f32[3,8,256]{2,1,0:T(8,128)S(1)}, f32[3,8,256]{2,1,0:T(8,128)S(1)}, u32[]{:S(2)}, u32[]{:S(2)}) collective-permute-start(f32[3,8,256]{2,1,0:T(8,128)S(1)} %get-tuple-element.56.stats_ref), channel_id=1, source_target_pairs={{0,1},{1,0},{2,3},{3,2},{4,5},{5,4},{6,7},{7,6},{8,9},{9,8},{10,11... | collective-permute-start | bytes 73736 | tf_op jit(solution)/shard_map/ppermute | solution.py:260
  46.9 7.0 %collective-permute-start.10 = (bf16[128,256]{1,0:T(8,128)(2,1)S(1)}, bf16[128,256]{1,0:T(8,128)(2,1)S(1)}, u32[]{:S(2)}, u32[]{:S(2)}) collective-permute-start(bf16[128,256]{1,0:T(8,128)(2,1)S(1)} %get-tuple-element.59), channel_id=1, source_target_pairs={{0,8},{8,0},{16,24},{24,16},{1,9},{9,1},{17,25},{25,17},{2,10},{10... | collective-permute-start | bytes 196616 | tf_op jit(solution)/shard_map/ppermute | solution.py:256
  49.8 8.8 %collective-permute-start.11 = (bf16[128,256]{1,0:T(8,128)(2,1)S(1)}, bf16[128,256]{1,0:T(8,128)(2,1)S(1)}, u32[]{:S(2)}, u32[]{:S(2)}) collective-permute-start(bf16[128,256]{1,0:T(8,128)(2,1)S(1)} %get-tuple-element.60), channel_id=1, source_target_pairs={{0,16},{8,24},{16,0},{24,8},{1,17},{9,25},{17,1},{25,9},{2,18},{10... | collective-permute-start | bytes 196616 | tf_op jit(solution)/shard_map/ppermute | solution.py:256
  51.5 7.6 %collective-permute-start.12 = (bf16[128,256]{1,0:T(8,128)(2,1)S(1)}, bf16[128,256]{1,0:T(8,128)(2,1)S(1)}, u32[]{:S(2)}, u32[]{:S(2)}) collective-permute-start(bf16[128,256]{1,0:T(8,128)(2,1)S(1)} %get-tuple-element.61), channel_id=1, source_target_pairs={{0,24},{8,16},{16,8},{24,0},{1,25},{9,17},{17,9},{25,1},{2,26},{10... | collective-permute-start | bytes 196616 | tf_op jit(solution)/shard_map/ppermute | solution.py:256
  59.7 11.4 %collective-permute-start.13 = (bf16[84,256]{1,0:T(8,128)(2,1)S(1)}, bf16[84,256]{1,0:T(8,128)(2,1)S(1)}, u32[]{:S(2)}, u32[]{:S(2)}) collective-permute-start(bf16[84,256]{1,0:T(8,128)(2,1)S(1)} %attended.1), channel_id=1, source_target_pairs={{0,0},{8,2},{16,4},{24,6},{2,8},{10,10},{18,12},{26,14},{4,16},{12... | collective-permute-start | bytes 129032 | tf_op jit(solution)/shard_map/ppermute | solution.py:268
  69.6 0.7 copy-start.6
  70.4 0.7 copy-start.8
  71.1 9.5 %collective-permute-start.14 = (bf16[4,84,256]{2,1,0:T(8,128)(2,1)S(1)}, bf16[4,84,256]{2,1,0:T(8,128)(2,1)}, u32[]{:S(2)}, u32[]{:S(2)}) collective-permute-start(bf16[4,84,256]{2,1,0:T(8,128)(2,1)S(1)} %get-tuple-element.69), channel_id=1, source_target_pairs={{0,1},{1,0},{2,3},{3,2},{4,5},{5,4},{6,7},{7,6},{8,9},{9,8},{10,11... | collective-permute-start | bytes 516104 | tf_op jit(solution)/shard_map/ppermute | solution.py:260
  73.2 27.1 %all-to-all-start = ((bf16[8,84,660]{2,1,0:T(8,128)(2,1)}), bf16[8,84,660]{2,1,0:T(8,128)(2,1)S(1)}, u32[]{:S(2)}, u32[]{:S(2)}) async-start(bf16[8,84,660]{2,1,0:T(8,128)(2,1)} %weight.1), calls=%async_computation | async-start | bytes 2162688 | tf_op jit(solution)/shard_map/all_to_all | solution.py:331
  80.6 1.0 copy-start.9
  82.6 9.8 %collective-permute-start.15 = (bf16[84,256]{1,0:T(8,128)(2,1)S(1)}, bf16[84,256]{1,0:T(8,128)(2,1)S(1)}, u32[]{:S(2)}, u32[]{:S(2)}) collective-permute-start(bf16[84,256]{1,0:T(8,128)(2,1)S(1)} %get-tuple-element.70), channel_id=1, source_target_pairs={{0,0},{8,2},{16,4},{24,6},{2,8},{10,10},{18,12},{26,14},{4,16},{12... | collective-permute-start | bytes 129032 | tf_op jit(solution)/shard_map/ppermute | solution.py:268
  85.2 11.0 %collective-permute-start.16 = (bf16[84,256]{1,0:T(8,128)(2,1)S(1)}, bf16[84,256]{1,0:T(8,128)(2,1)S(1)}, u32[]{:S(2)}, u32[]{:S(2)}) collective-permute-start(bf16[84,256]{1,0:T(8,128)(2,1)S(1)} %get-tuple-element.71), channel_id=1, source_target_pairs={{8,0},{0,2},{24,4},{16,6},{10,8},{2,10},{26,12},{18,14},{12,16},{4... | collective-permute-start | bytes 129032 | tf_op jit(solution)/shard_map/ppermute | solution.py:268
  85.3 10.9 %collective-permute-start.17 = (bf16[84,256]{1,0:T(8,128)(2,1)S(1)}, bf16[84,256]{1,0:T(8,128)(2,1)S(1)}, u32[]{:S(2)}, u32[]{:S(2)}) collective-permute-start(bf16[84,256]{1,0:T(8,128)(2,1)S(1)} %get-tuple-element.72), channel_id=1, source_target_pairs={{16,0},{24,2},{0,4},{8,6},{18,8},{26,10},{2,12},{10,14},{20,16},{2... | collective-permute-start | bytes 129032 | tf_op jit(solution)/shard_map/ppermute | solution.py:268
  90.2 9.4 %collective-permute-start.18 = (bf16[84,256]{1,0:T(8,128)(2,1)S(1)}, bf16[84,256]{1,0:T(8,128)(2,1)S(1)}, u32[]{:S(2)}, u32[]{:S(2)}) collective-permute-start(bf16[84,256]{1,0:T(8,128)(2,1)S(1)} %get-tuple-element.73), channel_id=1, source_target_pairs={{24,0},{16,2},{8,4},{0,6},{26,8},{18,10},{10,12},{2,14},{28,16},{2... | collective-permute-start | bytes 129032 | tf_op jit(solution)/shard_map/ppermute | solution.py:268
  92.3 11.9 %collective-permute-start.19 = (bf16[2,128,672]{2,1,0:T(8,128)(2,1)S(1)}, bf16[2,128,672]{2,1,0:T(8,128)(2,1)}, u32[]{:S(2)}, u32[]{:S(2)}) collective-permute-start(bf16[2,128,672]{2,1,0:T(8,128)(2,1)S(1)} %get-tuple-element.76), channel_id=1, source_target_pairs={{0,2},{2,0},{4,6},{6,4},{1,3},{3,1},{5,7},{7,5},{8,10},{10,8},{12,... | collective-permute-start | bytes 1032200 | tf_op jit(solution)/shard_map/ppermute | solution.py:252
  92.4 14.1 %collective-permute-start.20 = (bf16[2,128,672]{2,1,0:T(8,128)(2,1)S(1)}, bf16[2,128,672]{2,1,0:T(8,128)(2,1)}, u32[]{:S(2)}, u32[]{:S(2)}) collective-permute-start(bf16[2,128,672]{2,1,0:T(8,128)(2,1)S(1)} %get-tuple-element.77), channel_id=1, source_target_pairs={{0,4},{2,6},{4,0},{6,2},{1,5},{3,7},{5,1},{7,3},{8,12},{10,14},{12... | collective-permute-start | bytes 1032200 | tf_op jit(solution)/shard_map/ppermute | solution.py:252
  96.2 17.0 %collective-permute-start.21 = (bf16[2,128,672]{2,1,0:T(8,128)(2,1)S(1)}, bf16[2,128,672]{2,1,0:T(8,128)(2,1)}, u32[]{:S(2)}, u32[]{:S(2)}) collective-permute-start(bf16[2,128,672]{2,1,0:T(8,128)(2,1)S(1)} %get-tuple-element.78), channel_id=1, source_target_pairs={{0,6},{2,4},{4,2},{6,0},{1,7},{3,5},{5,3},{7,1},{8,14},{10,12},{12... | collective-permute-start | bytes 1032200 | tf_op jit(solution)/shard_map/ppermute | solution.py:252
  100.2 13.0 %copy-start.7 = (bf16[2,128,672]{2,1,0:T(8,128)(2,1)S(1)}, bf16[2,128,672]{2,1,0:T(8,128)(2,1)}, u32[]{:S(2)}) copy-start(bf16[2,128,672]{2,1,0:T(8,128)(2,1)} %copy-done.6) | copy-start | bytes 1032196

commit v3 on v2

v3 whole, which is shorter than its diff:
```python
import functools

import jax
import jax.numpy as jnp
from jax import lax
from jax.experimental import pallas as pl
from jax.experimental.pallas import tpu as pltpu
from jax.sharding import Mesh, PartitionSpec as P

HEADS = 28
HEAD_DIM = 96
GROUPS = 4
GROUP_HEADS = HEADS // GROUPS
GROUP_WIDTH = GROUP_HEADS * HEAD_DIM
PIECES = 8
NEG = -(2.0**99)
ATT, CENTRED, PLAIN, STATS = 0, 88, 176, 264
SCALE = HEAD_DIM ** (-0.5)
SECTION_AXES = ("x_hi", "y")
SEQ_AXES = ("zp", "zl", "x_lo", "core")
F32 = jnp.float32
BF16 = jnp.bfloat16
VMEM_LIMIT = 48 * 1024 * 1024
SMALL_LIMIT = 16 * 1024 * 1024
COST = dict(
    pack=1, join=1, forward=2, core=1, finish=1, backward=3, weight=2, unpack=10, sum_y=0, sum=0
)
NT = (((1,), (1,)), ((), ()))
NN = (((1,), (0,)), ((), ()))
TN = (((0,), (0,)), ((), ()))


def mm(a, b, dims):
    return lax.dot_general(a, b, dims, preferred_element_type=F32)


def pack_kernel(place, k_hbm, v_hbm, q_hbm, o0, o1, o2, o3, q_ref, k_all, v_all, q_all, sems):
    chip = place[0]
    copies = [
        pltpu.make_async_copy(src, dst, sems.at[n]) for n, (src, dst) in enumerate(((k_hbm, k_all), (v_hbm, v_all), (q_hbm, q_all)))
    ]
    for copy in copies:
        copy.start()
    for n, copy in enumerate(copies):
        copy.wait()
        for g in range(GROUPS):
            cols = slice(g * GROUP_WIDTH, (g + 1) * GROUP_WIDTH)
            for s, out in enumerate((o0, o1, o2, o3)):
                if n < 2:

                    @pl.when(lax.bitwise_xor(chip, s) == g)
                    def _():
                        out[n] = (k_all, v_all)[n][:, cols]

            if n == 2:

                @pl.when(chip == g)
                def _():
                    q_ref[...] = q_all[:, cols]


def unpack_kernel(place, s0, s1, s2, s3, gk_ref, gv_ref, all_k, all_v, sems):
    chip = place[0]
    slots = (s0, s1, s2, s3)
    copies = []
    for n, (rows, out) in enumerate(((all_k, gk_ref), (all_v, gv_ref))):
        for g in range(GROUPS):
            cols = slice(g * GROUP_WIDTH, (g + 1) * GROUP_WIDTH)
            for s in range(GROUPS):

                @pl.when(lax.bitwise_xor(chip, s) == g)
                def _():
                    rows[:, cols] = slots[s][n]

        copies.append(pltpu.make_async_copy(rows, out, sems.at[n]))
        copies[-1].start()
    for copy in copies:
        copy.wait()


def set_mask(place, ws_ref, bias):
    chip, pair, half = place[0], place[1], place[2]
    q_len = ws_ref.shape[1]
    kv_len = bias.shape[0] // GROUPS
    context = kv_len * GROUPS * PIECES
    rows = lax.broadcasted_iota(jnp.int32, (kv_len, q_len), 0)
    query_pos = context - q_len + lax.broadcasted_iota(jnp.int32, (kv_len, q_len), 1)
    for s in range(GROUPS):
        owner = pair * PIECES + 2 * lax.bitwise_xor(chip, s) + half
        key_pos = owner * kv_len + rows
        visible = (key_pos >= ws_ref[...]) & (key_pos <= query_pos)
        bias[s * kv_len : (s + 1) * kv_len, :] = jnp.where(visible, 0.0, NEG)


def join_kernel(place, m0, m1, m2, m3, theirs_ref, out_ref, pieces, rows):
    pair, half = place[1], place[2]
    rows_each = m0.shape[0]
    for j, mine in enumerate((m0, m1, m2, m3)):
        at = lax.bitwise_xor(pair, j)
        pieces[2 * at + half] = mine[...].astype(F32)
        pieces[2 * at + 1 - half] = theirs_ref[j].astype(F32)
    for k in range(PIECES):
        rows[k * rows_each : (k + 1) * rows_each, :] = pieces[k]
    out_ref[...] = rows[...].astype(BF16)


def head(h):
    return slice(h * HEAD_DIM, (h + 1) * HEAD_DIM)


def joined(slots, which, cols):
    return jnp.concatenate([s[which, :, cols] for s in slots], axis=0)


def halve(place, full, pieces, at, keep_ref, send_ref):
    half = place[2]
    rows_each = pieces.shape[1]
    for k in range(PIECES):
        pieces[k] = full[k * rows_each : (k + 1) * rows_each, :]
    for b in range(GROUPS):
        keep_ref[at * GROUPS + b] = pieces[2 * b + half]
        send_ref[at * GROUPS + b] = pieces[2 * b + 1 - half].astype(BF16)


def forward_kernel(
    place, ws_ref, q_ref, s0, s1, s2, s3, d_ref, keep_ref, send_ref, stats_ref, bias, att, centred, plain, pieces
):
    slots = (s0, s1, s2, s3)
    set_mask(place, ws_ref, bias)
    stats_ref[...] = jnp.zeros_like(stats_ref)
    for h in range(GROUP_HEADS):
        kh = joined(slots, 0, head(h))
        vh = joined(slots, 1, head(h))
        scores = mm(kh, q_ref[:, head(h)], NT) * SCALE + bias[...]
        top = jnp.floor(jnp.max(scores, axis=0, keepdims=True) * 0.125) * 8.0
        expo = jnp.exp(scores - top)
        total = jnp.sum(expo, axis=0, keepdims=True)
        dprobs = mm(vh, d_ref[head(h), :], NN)
        dots = jnp.sum(expo * dprobs, axis=0, keepdims=True) / total
        expo_b = expo.astype(BF16)
        att[head(h), :] = mm(vh, expo_b, TN)
        plain[head(h), :] = mm(kh, expo_b, TN)
        centred[head(h), :] = mm(kh, (expo * (dprobs - dots)).astype(BF16), TN)
        stats_ref[0, h : h + 1, :] = top
        stats_ref[1, h : h + 1, :] = total
        stats_ref[2, h : h + 1, :] = dots
    for at, full in enumerate((att, centred, plain)):
        halve(place, full, pieces, at, keep_ref, send_ref)


def row_weights(spread, piece, rows_each):
    q_len = spread.shape[1]
    row = lax.broadcasted_iota(jnp.int32, (rows_each, q_len), 0)
    before = spread[pl.ds(piece + 7, 1), :]
    after = spread[pl.ds(piece + 8, 1), :]
    return jnp.where(row < (HEAD_DIM - rows_each) * piece, before, after)


def merged(stats):
    top = functools.reduce(jnp.maximum, [s[0] for s in stats])
    weights = [jnp.exp(s[0] - top) for s in stats]
    total = sum(w * s[1] for w, s in zip(weights, stats))
    total = jnp.where(total > 0.0, total, 1.0)
    dots = sum(w * s[1] * s[2] for w, s in zip(weights, stats)) / total
    return top, total, dots, weights, [dots - s[2] for s in stats]


def core_kernel(place, keep_ref, stats_ref, got_ref, got_stats_ref, o0, o1, o2, o3, spread, payload):
    pair, half = place[1], place[2]
    rows_each = keep_ref.shape[1]
    top, total, dots, weights, shifts = merged([[r[n] for n in range(3)] for r in (stats_ref, got_stats_ref)])
    total_hi, dots_hi = total.astype(BF16).astype(F32), dots.astype(BF16).astype(F32)
    tail = jnp.concatenate([top, total_hi, total - total_hi, dots_hi, dots - dots_hi], axis=0)
    spread[...] = jnp.zeros_like(spread)
    for n in range(2):
        spread[n, 8:16, :] = weights[n]
        spread[2 + n, 8:16, :] = weights[n] * shifts[n]
    payload[...] = jnp.zeros_like(payload)
    for b in range(GROUPS):
        w0, w1, c0, c1 = [row_weights(spread.at[n], 2 * b + half, rows_each) for n in range(4)]
        plain0, plain1 = keep_ref[2 * GROUPS + b], got_ref[2 * GROUPS + b].astype(F32)
        payload[b, ATT : ATT + rows_each, :] = w0 * keep_ref[b] + w1 * got_ref[b].astype(F32)
        payload[b, CENTRED : CENTRED + rows_each, :] = (
            w0 * keep_ref[GROUPS + b] + w1 * got_ref[GROUPS + b].astype(F32) - c0 * plain0 - c1 * plain1
        )
        payload[b, PLAIN : PLAIN + rows_each, :] = w0 * plain0 + w1 * plain1
        payload[b, STATS:, :] = tail
    for j, out in enumerate((o0, o1, o2, o3)):
        out[...] = payload[lax.bitwise_xor(pair, j)].astype(BF16)


def read_stats(parts):
    tails = [p[STATS:, :].astype(F32) for p in parts]
    return merged([[t[0:8], t[8:16] + t[16:24], t[24:32] + t[32:40]] for t in tails])


def finish_kernel(place, p0, p1, p2, p3, out_ref, spread):
    rows_each = out_ref.shape[1]
    parts = (p0, p1, p2, p3)
    _, total, _, weights, shifts = read_stats(parts)
    spread[...] = jnp.zeros_like(spread)
    att = jnp.zeros(out_ref.shape[1:], F32)
    grad = jnp.zeros(out_ref.shape[1:], F32)
    for n, part in enumerate(parts):
        spread[0, 8:16, :] = weights[n] / total
        spread[1, 8:16, :] = weights[n] / total * shifts[n]
        w, c = [row_weights(spread.at[m], 2 * place[1] + place[2], rows_each) for m in range(2)]
        rows = part[...].astype(F32)
        att += w * rows[ATT : ATT + rows_each]
        grad += w * rows[CENTRED : CENTRED + rows_each] - c * rows[PLAIN : PLAIN + rows_each]
    out_ref[0] = att.astype(BF16)
    out_ref[1] = (grad * SCALE).astype(BF16)


def backward_kernel(place, ws_ref, q_ref, s0, s1, s2, s3, d_ref, p0, p1, p2, p3, o0, o1, o2, o3, bias, stats):
    kv_len = s0.shape[1]
    slots = (s0, s1, s2, s3)
    set_mask(place, ws_ref, bias)
    top, total, dots, _, _ = read_stats((p0, p1, p2, p3))
    stats[0], stats[1], stats[2] = top, 1.0 / total, dots
    for h in range(GROUP_HEADS):
        kh = joined(slots, 0, head(h))
        vh = joined(slots, 1, head(h))
        qh = q_ref[:, head(h)]
        dh = d_ref[head(h), :]
        scores = mm(kh, qh, NT) * SCALE + bias[...]
        probs = jnp.exp(scores - stats[0, h : h + 1, :]) * stats[1, h : h + 1, :]
        dscores = (probs * (mm(vh, dh, NN) - stats[2, h : h + 1, :])).astype(BF16)
        gk = (mm(dscores, qh, NN) * SCALE).astype(BF16)
        gv = mm(probs.astype(BF16), dh, NT).astype(BF16)
        for s, out in enumerate((o0, o1, o2, o3)):
            part = slice(s * kv_len, (s + 1) * kv_len)
            out[0, :, head(h)] = gk[part]
            out[1, :, head(h)] = gv[part]


def weight_kernel(rows_ref, cot_ref, out_ref, gq_ref, full):
    pieces, _, width = out_ref.shape
    full[...] = mm(rows_ref[0], cot_ref[...], NT)
    gq_ref[...] = rows_ref[1]
    for s in range(pieces):
        x_hi, y = divmod(s, pieces // 2)
        out_ref[2 * y + x_hi] = full[:, s * width : (s + 1) * width].astype(BF16)


def sum_y_kernel(place, x_ref, keep_ref, send_ref):
    x_hi = place[3]
    half = x_ref.shape[0] // 2
    keep_ref[...] = sum(x_ref[2 * y + x_hi].astype(F32) for y in range(half))
    send_ref[...] = sum(x_ref[2 * y + 1 - x_hi].astype(F32) for y in range(half)).astype(BF16)


def sum_kernel(keep_ref, got_ref, out_ref):
    out_ref[...] = (keep_ref[...] + got_ref[...].astype(F32)).astype(BF16)


SMEM = pl.BlockSpec(memory_space=pltpu.SMEM)
ANY = pl.BlockSpec(memory_space=pl.ANY)
WHOLE = pl.BlockSpec(memory_space=pltpu.VMEM)


def call(name, kernel, n_in, out_shapes, scratch=(), scalars=1, in_blocks=None, out_blocks=None, limit=VMEM_LIMIT):
    return pl.pallas_call(
        kernel,
        out_shape=out_shapes,
        in_specs=[SMEM] * scalars + (in_blocks or [WHOLE] * n_in),
        out_specs=out_blocks or jax.tree.map(lambda _: WHOLE, out_shapes),
        scratch_shapes=list(scratch),
        compiler_params=pltpu.CompilerParams(vmem_limit_bytes=limit),
        cost_estimate=pl.CostEstimate(flops=int(COST[name] * 1e9), bytes_accessed=0, transcendentals=0),
        name=name,
    )


def swap_chip(x, s):
    return lax.ppermute(x, ("zl", "x_lo"), [(i, i ^ s) for i in range(GROUPS)])


def swap_pair(x, j):
    return lax.ppermute(x, "zp", [(i, i ^ j) for i in range(GROUPS)])


def swap_half(x):
    return lax.ppermute(x, "core", [(0, 1), (1, 0)])


def trade(x, j=0):
    return lax.ppermute(x, ("zp", "zl", "x_lo"), [(a * GROUPS + b, (b ^ j) * GROUPS + a) for a in range(GROUPS) for b in range(GROUPS)])


def local(queries, keys, values, out_grad, w_out, window_start):
    query, key_rows, value_rows, cotangent = queries[0], keys[0], values[0], out_grad[0].T
    q_len = query.shape[0]
    kv_len, width = key_rows.shape
    rows_each, model = w_out.shape
    sections = lax.axis_size(SECTION_AXES)
    place = jnp.stack([lax.axis_index(("zl", "x_lo")), lax.axis_index("zp"), lax.axis_index("core"), lax.axis_index("x_hi")]).astype(jnp.int32)
    starts = window_start.reshape(1, q_len)
    sds = jax.ShapeDtypeStruct
    slots4 = [sds((2, kv_len, GROUP_WIDTH), BF16)] * GROUPS
    bias = pltpu.VMEM((GROUPS * kv_len, q_len), F32)
    features = pltpu.VMEM((GROUP_WIDTH, q_len), F32)
    pieces = pltpu.VMEM((PIECES, rows_each, q_len), F32)

    whole = pltpu.VMEM((kv_len, width), BF16)
    *send, q_own = call(
        "pack",
        pack_kernel,
        3,
        slots4 + [sds((q_len, GROUP_WIDTH), BF16)],
        [whole, whole, pltpu.VMEM((q_len, width), BF16), pltpu.SemaphoreType.DMA((3,))],
        in_blocks=[ANY] * 3,
        limit=60 * 1024 * 1024,
    )(place, key_rows, value_rows, query)
    w_out, send = lax.optimization_barrier((w_out, send))
    slots = [send[0]] + [swap_chip(send[s], s) for s in range(1, GROUPS)]
    d_own = lax.dot_general(w_out, cotangent, NN, preferred_element_type=F32).astype(BF16)
    mine = [trade(d_own, j) for j in range(GROUPS)]
    theirs = swap_half(jnp.stack(mine))
    d_group = call("join", join_kernel, 5, sds((GROUP_WIDTH, q_len), BF16), [pieces, features])(place, *mine, theirs)

    keep, half, stats = call(
        "forward",
        forward_kernel,
        7,
        [sds((3 * GROUPS, rows_each, q_len), F32), sds((3 * GROUPS, rows_each, q_len), BF16), sds((3, 8, q_len), F32)],
        [bias, features, features, features, pieces],
    )(place, starts, q_own, *slots, d_group)
    parts = call(
        "core",
        core_kernel,
        4,
        [sds((STATS + 40, q_len), BF16)] * GROUPS,
        [pltpu.VMEM((4, 24, q_len), F32), pltpu.VMEM((GROUPS, STATS + 40, q_len), F32)],
    )(place, keep, stats, swap_half(half), swap_half(stats))
    parts = [parts[0]] + [swap_pair(parts[j], j) for j in range(1, GROUPS)]
    rows = call("finish", finish_kernel, 4, sds((2, rows_each, q_len), BF16), [pltpu.VMEM((2, 24, q_len), F32)])(place, *parts)
    rows, parts = lax.optimization_barrier((rows, parts))
    rows = trade(rows)

    back = call("backward", backward_kernel, 11, slots4, [bias, pltpu.VMEM((3, 8, q_len), F32)])(
        place, starts, q_own, *slots, d_group, *parts
    )
    rows, back = lax.optimization_barrier((rows, back))
    back = [back[0]] + [swap_chip(back[s], s) for s in range(1, GROUPS)]

    part = model // sections
    gw, grad_q = call(
        "weight",
        weight_kernel,
        2,
        [sds((sections, rows_each, part), BF16), sds((rows_each, q_len), BF16)],
        [pltpu.VMEM((rows_each, model), F32)],
        scalars=0,
        limit=SMALL_LIMIT,
    )(rows, cotangent)
    gw = lax.all_to_all(gw, "y", 0, 0, tiled=True)
    grad_k, grad_v = call(
        "unpack",
        unpack_kernel,
        4,
        [sds((kv_len, width), BF16)] * 2,
        [whole, whole, pltpu.SemaphoreType.DMA((2,))],
        out_blocks=[ANY] * 2,
    )(place, *back)
    gw, grad_k = lax.optimization_barrier((gw, grad_k))
    keep, half = call("sum_y", sum_y_kernel, 1, [sds((rows_each, part), F32), sds((rows_each, part), BF16)], limit=SMALL_LIMIT)(place, gw)
    half = lax.ppermute(half, "x_hi", [(0, 1), (1, 0)])
    grad_weight = call("sum", sum_kernel, 2, sds((rows_each, part), BF16), scalars=0, limit=SMALL_LIMIT)(keep, half)
    return grad_q[None], grad_k[None], grad_v[None], grad_weight


def solution(mesh):
    fine = Mesh(mesh.devices.reshape(2, mesh.shape["section"] // 2, GROUPS, 2, 2, 2), SECTION_AXES + SEQ_AXES)
    return jax.shard_map(
        local,
        mesh=fine,
        in_specs=(
            P(SECTION_AXES, None, None),
            P(SECTION_AXES, SEQ_AXES, None),
            P(SECTION_AXES, SEQ_AXES, None),
            P(SECTION_AXES, None, None),
            P(SEQ_AXES, None),
            P(),
        ),
        out_specs=(
            P(SECTION_AXES, SEQ_AXES, None),
            P(SECTION_AXES, SEQ_AXES, None),
            P(SECTION_AXES, SEQ_AXES, None),
            P(SEQ_AXES, SECTION_AXES),
        ),
        check_vma=False,
    )
```

time: 119 us -> 112 us (0.941); the launches traced: 117 us -> 112 us
  starting transfers between devices: 54.9 us -> 41.2 us
  waiting for transfers between devices: 35.1 us -> 45.7 us
  local copies, waits for them, and re-layouts: 6.17 us -> 2.03 us
    ppermute x13 -> x9, starting transfers between devices: 31.2 us -> 21 us  [the longest x5 18.8 us: trade(): lax.ppermute(x, ('zp', 'zl', 'x_lo'), [(a * GROUPS + b, (b ^ j) * GROUPS...]
    ppermute x3, waiting for transfers between devices: 5.59 us -> 13.1 us  [swap_pair(): return lax.ppermute(x, 'zp', [(i, i ^ j) for i in range(GROUPS)])]
    unnamed x20 -> x24, local copies, waits for them, and re-layouts: 6.17 us -> 2.03 us
    all_to_all x1, starting transfers between devices: 7.43 us -> 4.47 us  [local(): gw = lax.all_to_all(gw, 'y', 0, 0, tiled=True)]
    pallas_call x1, Pallas kernels: 2.21 us -> 4.18 us  [local(): call('pack', pack_kernel, 3, slots4 + [sds((q_len, GROUP_WIDTH), BF16)],...]
    ppermute x13 -> x9, waiting for transfers between devices: 6.47 us -> 8.15 us  [the longest x1 5.16 us: local(): half = lax.ppermute(half, 'x_hi', [(0, 1), (1, 0)])]
    pallas_call x9 -> x8, Pallas kernels: 16.9 us -> 16 us  [the longest x1 4.51 us: local(): call('forward', forward_kernel, 7, [sds((3 * GROUPS, rows_each, q_len), F...]
  transfers between devices with their start and end apart: 23 -> 19, of which waited for: 13 -> 13; matrix products, arithmetic and copies ran while one was open for 0% -> 0% of each run, Pallas kernels for 7% -> 8%
where the time goes in v3:
time: 112 us
  waiting for transfers between devices  45.7 us (41%)
  starting transfers between devices  41.2 us (37%)
  Pallas kernels  20.8 us (19%)
  local copies, waits for them, and re-layouts  2.03 us (2%)
    ppermute x6, waiting for transfers between devices, swap_chip(): return lax.ppermute(x, ('zl', 'x_lo'), [(i, i ^ s) for i in range(GROUPS)])  24 us
    ppermute x5, starting transfers between devices, trade(): lax.ppermute(x, ('zp', 'zl', 'x_lo'), [(a * GROUPS + b, (b ^ j) * GROUPS...  18.8 us
    ppermute x3, waiting for transfers between devices, swap_pair(): return lax.ppermute(x, 'zp', [(i, i ^ j) for i in range(GROUPS)])  13.1 us
    ppermute x6, starting transfers between devices, swap_chip(): return lax.ppermute(x, ('zl', 'x_lo'), [(i, i ^ s) for i in range(GROUPS)])  9.14 us
    ppermute x3, starting transfers between devices, swap_pair(): return lax.ppermute(x, 'zp', [(i, i ^ j) for i in range(GROUPS)])  6.58 us
    ppermute x1, waiting for transfers between devices, local(): half = lax.ppermute(half, 'x_hi', [(0, 1), (1, 0)])  5.16 us
    pallas_call x1, Pallas kernels, local(): call('forward', forward_kernel, 7, [sds((3 * GROUPS, rows_each, q_len), F...  4.51 us
    all_to_all x1, starting transfers between devices, local(): gw = lax.all_to_all(gw, 'y', 0, 0, tiled=True)  4.47 us
  transfers between devices with their start and end apart: 19, of which 13 were waited for; matrix products, arithmetic and copies ran while one was open for 0% of the time, Pallas kernels for 8%

profile of v3, /device:TPU:6, one launch (start us, length us, event | category | flops | bytes accessed | tf_op | source)
XLA Modules:
  0.0 111.7 jit_solution(7828171892465696704)
XLA Ops:
  0.6 0.0 copy-start
  0.7 0.6 pad_add_fusion.place
  1.3 4.2 %pack.1 = (bf16[2,128,672]{2,1,0:T(8,128)(2,1)}, bf16[2,128,672]{2,1,0:T(8,128)(2,1)}, bf16[2,128,672]{2,1,0:T(8,128)(2,1)}, bf16[2,128,672]{2,1,0:T(8,128)(2,1)}, bf16[256,672]{1,0:T(8,128)(2,1)}) custom-call(s32[4]{0:T(128)} %pad_add_fusion.place, bf16[128,2688]{1,0:T(8,128)(2,1)} %bitcast.31, bf16[128,2688]{1,0:T(8,128)(2,1)} %bitcast.32, ...), custom_call_target="tpu_custom_call" | custom-call | flops 1000000000 | tf_op jit(solution)/shard_map/pack/pallas_call | solution.py:306
  5.4 0.0 copy-start.11
  5.5 0.6 fusion.2
  6.1 0.0 copy-start.4
  6.1 0.0 copy-start.5
  6.1 7.4 %collective-permute-start.6 = (bf16[84,256]{1,0:T(8,128)(2,1)S(1)}, bf16[84,256]{1,0:T(8,128)(2,1)S(1)}, u32[]{:S(2)}, u32[]{:S(2)}) collective-permute-start(bf16[84,256]{1,0:T(8,128)(2,1)S(1)} %fusion.2), channel_id=1, source_target_pairs={{0,24},{2,16},{4,8},{6,0},{8,26},{10,18},{12,10},{14,2},{16,28},{1... | collective-permute-start | bytes 129032 | tf_op jit(solution)/shard_map/ppermute | solution.py:288
  13.5 0.9 collective-permute-start.5
  14.4 1.7 %collective-permute-start.4 = (bf16[84,256]{1,0:T(8,128)(2,1)S(1)}, bf16[84,256]{1,0:T(8,128)(2,1)S(1)}, u32[]{:S(2)}, u32[]{:S(2)}) collective-permute-start(bf16[84,256]{1,0:T(8,128)(2,1)S(1)} %fusion.2), channel_id=1, source_target_pairs={{0,8},{2,0},{4,24},{6,16},{8,10},{10,2},{12,26},{14,18},{16,12},{1... | collective-permute-start | bytes 129032 | tf_op jit(solution)/shard_map/ppermute | solution.py:288
  16.2 3.1 %collective-permute-start.3 = (bf16[84,256]{1,0:T(8,128)(2,1)S(1)}, bf16[84,256]{1,0:T(8,128)(2,1)S(1)}, u32[]{:S(2)}, u32[]{:S(2)}) collective-permute-start(bf16[84,256]{1,0:T(8,128)(2,1)S(1)} %fusion.2), channel_id=1, source_target_pairs={{0,0},{2,8},{4,16},{6,24},{8,2},{10,10},{12,18},{14,26},{16,4},{18... | collective-permute-start | bytes 129032 | tf_op jit(solution)/shard_map/ppermute | solution.py:288
  19.2 0.1 collective-permute-start
  19.4 4.7 %collective-permute-start.1 = (bf16[2,128,672]{2,1,0:T(8,128)(2,1)S(1)}, bf16[2,128,672]{2,1,0:T(8,128)(2,1)S(1)}, u32[]{:S(2)}, u32[]{:S(2)}) collective-permute-start(bf16[2,128,672]{2,1,0:T(8,128)(2,1)S(1)} %copy-done.10), channel_id=1, source_target_pairs={{0,4},{2,6},{4,0},{6,2},{1,5},{3,7},{5,1},{7,3},{8,12},{10,14},{12... | collective-permute-start | bytes 1032200 | tf_op jit(solution)/shard_map/ppermute | solution.py:276
  24.1 0.1 collective-permute-done.3.m0
  24.2 0.1 collective-permute-start.7
  24.3 1.4 %collective-permute-done.7.theirs_ref = bf16[4,84,256]{2,1,0:T(8,128)(2,1)S(1)} collective-permute-done((bf16[4,84,256]{2,1,0:T(8,128)(2,1)S(1)}, bf16[4,84,256]{2,1,0:T(8,128)(2,1)S(1)}, u32[]{:S(2)}, u32[]{:S(2)}) %collective-permute-start.7) | collective-permute-done | bytes 172064 | tf_op jit(solution)/shard_map/ppermute | solution.py:284
  25.7 0.6 join.1.d_ref
  26.4 3.6 %collective-permute-done.s1 = bf16[2,128,672]{2,1,0:T(8,128)(2,1)S(1)} collective-permute-done((bf16[2,128,672]{2,1,0:T(8,128)(2,1)S(1)}, bf16[2,128,672]{2,1,0:T(8,128)(2,1)S(1)}, u32[]{:S(2)}, u32[]{:S(2)}) %collective-permute-start) | collective-permute-done | bytes 344096 | tf_op jit(solution)/shard_map/ppermute | solution.py:276
  30.0 4.1 %collective-permute-done.1.s2 = bf16[2,128,672]{2,1,0:T(8,128)(2,1)S(1)} collective-permute-done((bf16[2,128,672]{2,1,0:T(8,128)(2,1)S(1)}, bf16[2,128,672]{2,1,0:T(8,128)(2,1)S(1)}, u32[]{:S(2)}, u32[]{:S(2)}) %collective-permute-start.1) | collective-permute-done | bytes 344096 | tf_op jit(solution)/shard_map/ppermute | solution.py:276
  34.1 6.4 %collective-permute-done.2.s3 = bf16[2,128,672]{2,1,0:T(8,128)(2,1)S(1)} collective-permute-done((bf16[2,128,672]{2,1,0:T(8,128)(2,1)S(1)}, bf16[2,128,672]{2,1,0:T(8,128)(2,1)S(1)}, u32[]{:S(2)}, u32[]{:S(2)}) %collective-permute-start.2) | collective-permute-done | bytes 344096 | tf_op jit(solution)/shard_map/ppermute | solution.py:276
  40.5 4.5 %forward.1 = (f32[12,84,256]{2,1,0:T(8,128)S(1)}, bf16[12,84,256]{2,1,0:T(8,128)(2,1)S(1)}, f32[3,8,256]{2,1,0:T(8,128)S(1)}) custom-call(s32[4]{0:T(128)S(1)} %copy-done.3, s32[1,256]{1,0:T(1,128)S(1)} %bitcast.28, bf16[256,672]{1,0:T(8,128)(2,1)S(1)} %copy-done.6, bf16[2,128,672]{2,1,0:T(8,128)(2,1)S(1)} %copy-done.5, ...), custom_call_target="tpu_custom_call" | custom-call | flops 2000000000 | tf_op jit(solution)/shard_map/forward/pallas_call | solution.py:322
  45.1 0.1 collective-permute-start.8
  45.2 0.5 collective-permute-start.9
  45.7 1.5 %collective-permute-done.9.got_stats_ref = f32[3,8,256]{2,1,0:T(8,128)S(1)} collective-permute-done((f32[3,8,256]{2,1,0:T(8,128)S(1)}, f32[3,8,256]{2,1,0:T(8,128)S(1)}, u32[]{:S(2)}, u32[]{:S(2)}) %collective-permute-start.9) | collective-permute-done | bytes 24608 | tf_op jit(solution)/shard_map/ppermute | solution.py:284
  47.1 1.0 core.1
  48.1 2.0 %collective-permute-start.10 = (bf16[304,256]{1,0:T(8,128)(2,1)S(1)}, bf16[304,256]{1,0:T(8,128)(2,1)S(1)}, u32[]{:S(2)}, u32[]{:S(2)}) collective-permute-start(bf16[304,256]{1,0:T(8,128)(2,1)S(1)} %get-tuple-element.57), channel_id=1, source_target_pairs={{0,8},{8,0},{16,24},{24,16},{1,9},{9,1},{17,25},{25,17},{2,10},{10... | collective-permute-start | bytes 466952 | tf_op jit(solution)/shard_map/ppermute | solution.py:280
  50.1 2.2 %collective-permute-start.11 = (bf16[304,256]{1,0:T(8,128)(2,1)S(1)}, bf16[304,256]{1,0:T(8,128)(2,1)S(1)}, u32[]{:S(2)}, u32[]{:S(2)}) collective-permute-start(bf16[304,256]{1,0:T(8,128)(2,1)S(1)} %get-tuple-element.58), channel_id=1, source_target_pairs={{0,16},{8,24},{16,0},{24,8},{1,17},{9,25},{17,1},{25,9},{2,18},{10... | collective-permute-start | bytes 466952 | tf_op jit(solution)/shard_map/ppermute | solution.py:280
  52.3 2.4 %collective-permute-start.12 = (bf16[304,256]{1,0:T(8,128)(2,1)S(1)}, bf16[304,256]{1,0:T(8,128)(2,1)S(1)}, u32[]{:S(2)}, u32[]{:S(2)}) collective-permute-start(bf16[304,256]{1,0:T(8,128)(2,1)S(1)} %get-tuple-element.59), channel_id=1, source_target_pairs={{0,24},{8,16},{16,8},{24,0},{1,25},{9,17},{17,9},{25,1},{2,26},{10... | collective-permute-start | bytes 466952 | tf_op jit(solution)/shard_map/ppermute | solution.py:280
  54.7 8.0 %collective-permute-done.10.p1 = bf16[304,256]{1,0:T(8,128)(2,1)S(1)} collective-permute-done((bf16[304,256]{1,0:T(8,128)(2,1)S(1)}, bf16[304,256]{1,0:T(8,128)(2,1)S(1)}, u32[]{:S(2)}, u32[]{:S(2)}) %collective-permute-start.10) | collective-permute-done | bytes 155680 | tf_op jit(solution)/shard_map/ppermute | solution.py:280
  62.7 0.6 collective-permute-done.11.p2
  63.2 4.5 %collective-permute-done.12.p3 = bf16[304,256]{1,0:T(8,128)(2,1)S(1)} collective-permute-done((bf16[304,256]{1,0:T(8,128)(2,1)S(1)}, bf16[304,256]{1,0:T(8,128)(2,1)S(1)}, u32[]{:S(2)}, u32[]{:S(2)}) %collective-permute-start.12) | collective-permute-done | bytes 155680 | tf_op jit(solution)/shard_map/ppermute | solution.py:280
  67.8 0.7 finish.1
  68.5 5.7 %collective-permute-start.13 = (bf16[2,84,256]{2,1,0:T(8,128)(2,1)S(1)}, bf16[2,84,256]{2,1,0:T(8,128)(2,1)S(1)}, u32[]{:S(2)}, u32[]{:S(2)}) collective-permute-start(bf16[2,84,256]{2,1,0:T(8,128)(2,1)S(1)} %finish.1), channel_id=1, source_target_pairs={{0,0},{2,8},{4,16},{6,24},{8,2},{10,10},{12,18},{14,26},{16,4},{18... | collective-permute-start | bytes 258056 | tf_op jit(solution)/shard_map/ppermute | solution.py:288
  74.3 3.9 %backward.1 = (bf16[2,128,672]{2,1,0:T(8,128)(2,1)S(1)}, bf16[2,128,672]{2,1,0:T(8,128)(2,1)}, bf16[2,128,672]{2,1,0:T(8,128)(2,1)}, bf16[2,128,672]{2,1,0:T(8,128)(2,1)S(1)}) custom-call(s32[4]{0:T(128)S(1)} %copy-done.3, s32[1,256]{1,0:T(1,128)S(1)} %bitcast.29, bf16[256,672]{1,0:T(8,128)(2,1)S(1)} %copy-done.6, bf16[2,128,672]{2,1,0:T(8,128)(2,1)S(1)} %copy-done.5, ...), custom_call_target="tpu_custom_call" | custom-call | flops 3000000000 | tf_op jit(solution)/shard_map/backward/pallas_call | solution.py:341
  78.2 3.4 %collective-permute-start.15 = (bf16[2,128,672]{2,1,0:T(8,128)(2,1)}, bf16[2,128,672]{2,1,0:T(8,128)(2,1)}, u32[]{:S(2)}, u32[]{:S(2)}) collective-permute-start(bf16[2,128,672]{2,1,0:T(8,128)(2,1)} %get-tuple-element.74), channel_id=1, source_target_pairs={{0,4},{2,6},{4,0},{6,2},{1,5},{3,7},{5,1},{7,3},{8,12},{10,14},{12... | collective-permute-start | bytes 1032200 | tf_op jit(solution)/shard_map/ppermute | solution.py:276
  81.5 1.0 collective-permute-start.16
  82.5 1.6 %weight.1 = (bf16[8,84,660]{2,1,0:T(8,128)(2,1)S(1)}, bf16[84,256]{1,0:T(8,128)(2,1)}) custom-call(bf16[2,84,256]{2,1,0:T(8,128)(2,1)S(1)} %collective-permute-done.13.rows_ref, bf16[5280,256]{1,0:T(8,128)(2,1)S(1)} %bitcast.23), custom_call_target="tpu_custom_call" | custom-call | flops 2000000000 | tf_op jit(solution)/shard_map/weight/pallas_call | solution.py:348
  84.1 1.0 copy-done.2
  85.1 4.5 %all-to-all-start = ((bf16[8,84,660]{2,1,0:T(8,128)(2,1)}), bf16[8,84,660]{2,1,0:T(8,128)(2,1)S(1)}, u32[]{:S(2)}, u32[]{:S(2)}) async-start(bf16[8,84,660]{2,1,0:T(8,128)(2,1)} %copy-done.2), calls=%async_computation | async-start | bytes 2162688 | tf_op jit(solution)/shard_map/all_to_all | solution.py:357
  89.5 2.3 %collective-permute-done.15.s2 = bf16[2,128,672]{2,1,0:T(8,128)(2,1)} collective-permute-done((bf16[2,128,672]{2,1,0:T(8,128)(2,1)}, bf16[2,128,672]{2,1,0:T(8,128)(2,1)}, u32[]{:S(2)}, u32[]{:S(2)}) %collective-permute-start.15) | collective-permute-done | bytes 344096 | tf_op jit(solution)/shard_map/ppermute | solution.py:276
  91.9 7.5 %collective-permute-done.16.s3 = bf16[2,128,672]{2,1,0:T(8,128)(2,1)} collective-permute-done((bf16[2,128,672]{2,1,0:T(8,128)(2,1)S(1)}, bf16[2,128,672]{2,1,0:T(8,128)(2,1)}, u32[]{:S(2)}, u32[]{:S(2)}) %collective-permute-start.16) | collective-permute-done | bytes 344096 | tf_op jit(solution)/shard_map/ppermute | solution.py:276
  99.4 1.0 copy-done.8
  100.4 2.9 %unpack.1 = (bf16[128,2688]{1,0:T(8,128)(2,1)}, bf16[128,2688]{1,0:T(8,128)(2,1)}) custom-call(s32[4]{0:T(128)S(1)} %copy-done.3, bf16[2,128,672]{2,1,0:T(8,128)(2,1)S(1)} %copy-done.8, bf16[2,128,672]{2,1,0:T(8,128)(2,1)} %collective-permute-done.14.s1, bf16[2,128,672]{2,1,0:T(8,128)(2,1)} %collective-permute-done.15.s2, ...), custom_call_target="tpu_custom_call" | custom-call | flops 10000000000 | tf_op jit(solution)/shard_map/unpack/pallas_call | solution.py:358
  103.3 0.4 all-to-all-done.x_ref
  103.8 0.7 sum_y.1
  104.4 1.4 %collective-permute-start.17 = (bf16[84,660]{1,0:T(8,128)(2,1)S(1)}, bf16[84,660]{1,0:T(8,128)(2,1)S(1)}, u32[]{:S(2)}, u32[]{:S(2)}) collective-permute-start(bf16[84,660]{1,0:T(8,128)(2,1)S(1)} %get-tuple-element.81), channel_id=1, source_target_pairs={{0,128},{128,0},{1,129},{129,1},{2,130},{130,2},{3,131},{131,3},{4... | collective-permute-start | bytes 332648 | tf_op jit(solution)/shard_map/ppermute | solution.py:368
  105.9 5.2 %collective-permute-done.17.got_ref = bf16[84,660]{1,0:T(8,128)(2,1)S(1)} collective-permute-done((bf16[84,660]{1,0:T(8,128)(2,1)S(1)}, bf16[84,660]{1,0:T(8,128)(2,1)S(1)}, u32[]{:S(2)}, u32[]{:S(2)}) %collective-permute-start.17) | collective-permute-done | bytes 110912 | tf_op jit(solution)/shard_map/ppermute | solution.py:368
  111.0 0.7 sum.1
  (27 shorter events, 0.1 us)
Async XLA Ops:
  0.6 4.9 %copy-start = (bf16[84,5280]{1,0:T(8,128)(2,1)S(1)}, bf16[84,5280]{1,0:T(8,128)(2,1)}, u32[]{:S(2)}) copy-start(bf16[84,5280]{1,0:T(8,128)(2,1)} %param.10) | copy-start | bytes 2661124
  0.7 4.8 %copy-start.1 = (bf16[1,256,5280]{1,2,0:T(8,128)(2,1)S(1)}, bf16[1,256,5280]{1,2,0:T(8,128)(2,1)}, u32[]{:S(2)}) copy-start(bf16[1,256,5280]{1,2,0:T(8,128)(2,1)} %param.9) | copy-start | bytes 8110084
  5.4 13.8 %copy-start.11 = (bf16[2,128,672]{2,1,0:T(8,128)(2,1)S(1)}, bf16[2,128,672]{2,1,0:T(8,128)(2,1)}, u32[]{:S(2)}) copy-start(bf16[2,128,672]{2,1,0:T(8,128)(2,1)} %get-tuple-element.49) | copy-start | bytes 1032196
  5.5 13.9 %copy-start.10 = (bf16[2,128,672]{2,1,0:T(8,128)(2,1)S(1)}, bf16[2,128,672]{2,1,0:T(8,128)(2,1)}, u32[]{:S(2)}) copy-start(bf16[2,128,672]{2,1,0:T(8,128)(2,1)} %get-tuple-element.50) | copy-start | bytes 1032196
  5.5 18.6 %copy-start.9 = (bf16[2,128,672]{2,1,0:T(8,128)(2,1)S(1)}, bf16[2,128,672]{2,1,0:T(8,128)(2,1)}, u32[]{:S(2)}) copy-start(bf16[2,128,672]{2,1,0:T(8,128)(2,1)} %get-tuple-element.51) | copy-start | bytes 1032196
  5.5 20.3 %copy-start.3 = (s32[4]{0:T(128)S(1)}, s32[4]{0:T(128)}, u32[]{:S(2)}) copy-start(s32[4]{0:T(128)} %pad_add_fusion.place) | copy-start | bytes 52
  6.1 34.5 %copy-start.4 = (s32[256]{0:T(256)S(1)}, s32[256]{0:T(256)}, u32[]{:S(2)}) copy-start(s32[256]{0:T(256)} %param.11) | copy-start | bytes 3076
  6.1 34.4 %copy-start.5 = (bf16[2,128,672]{2,1,0:T(8,128)(2,1)S(1)}, bf16[2,128,672]{2,1,0:T(8,128)(2,1)}, u32[]{:S(2)}) copy-start(bf16[2,128,672]{2,1,0:T(8,128)(2,1)} %get-tuple-element.48.s0) | copy-start | bytes 1032196
  6.1 34.4 %copy-start.6 = (bf16[256,672]{1,0:T(8,128)(2,1)S(1)}, bf16[256,672]{1,0:T(8,128)(2,1)}, u32[]{:S(2)}) copy-start(bf16[256,672]{1,0:T(8,128)(2,1)} %get-tuple-element.43.q_ref) | copy-start | bytes 1032196
  6.1 13.2 %collective-permute-start.6 = (bf16[84,256]{1,0:T(8,128)(2,1)S(1)}, bf16[84,256]{1,0:T(8,128)(2,1)S(1)}, u32[]{:S(2)}, u32[]{:S(2)}) collective-permute-start(bf16[84,256]{1,0:T(8,128)(2,1)S(1)} %fusion.2), channel_id=1, source_target_pairs={{0,24},{2,16},{4,8},{6,0},{8,26},{10,18},{12,10},{14,2},{16,28},{1... | collective-permute-start | bytes 129032 | tf_op jit(solution)/shard_map/ppermute | solution.py:288
  13.5 10.5 %collective-permute-start.5 = (bf16[84,256]{1,0:T(8,128)(2,1)S(1)}, bf16[84,256]{1,0:T(8,128)(2,1)S(1)}, u32[]{:S(2)}, u32[]{:S(2)}) collective-permute-start(bf16[84,256]{1,0:T(8,128)(2,1)S(1)} %fusion.2), channel_id=1, source_target_pairs={{0,16},{2,24},{4,0},{6,8},{8,18},{10,26},{12,2},{14,10},{16,20},{1... | collective-permute-start | bytes 129032 | tf_op jit(solution)/shard_map/ppermute | solution.py:288
  14.4 9.7 %collective-permute-start.4 = (bf16[84,256]{1,0:T(8,128)(2,1)S(1)}, bf16[84,256]{1,0:T(8,128)(2,1)S(1)}, u32[]{:S(2)}, u32[]{:S(2)}) collective-permute-start(bf16[84,256]{1,0:T(8,128)(2,1)S(1)} %fusion.2), channel_id=1, source_target_pairs={{0,8},{2,0},{4,24},{6,16},{8,10},{10,2},{12,26},{14,18},{16,12},{1... | collective-permute-start | bytes 129032 | tf_op jit(solution)/shard_map/ppermute | solution.py:288
  16.2 8.0 %collective-permute-start.3 = (bf16[84,256]{1,0:T(8,128)(2,1)S(1)}, bf16[84,256]{1,0:T(8,128)(2,1)S(1)}, u32[]{:S(2)}, u32[]{:S(2)}) collective-permute-start(bf16[84,256]{1,0:T(8,128)(2,1)S(1)} %fusion.2), channel_id=1, source_target_pairs={{0,0},{2,8},{4,16},{6,24},{8,2},{10,10},{12,18},{14,26},{16,4},{18... | collective-permute-start | bytes 129032 | tf_op jit(solution)/shard_map/ppermute | solution.py:288
  19.2 10.8 %collective-permute-start = (bf16[2,128,672]{2,1,0:T(8,128)(2,1)S(1)}, bf16[2,128,672]{2,1,0:T(8,128)(2,1)S(1)}, u32[]{:S(2)}, u32[]{:S(2)}) collective-permute-start(bf16[2,128,672]{2,1,0:T(8,128)(2,1)S(1)} %copy-done.11), channel_id=1, source_target_pairs={{0,2},{2,0},{4,6},{6,4},{1,3},{3,1},{5,7},{7,5},{8,10},{10,8},{12,... | collective-permute-start | bytes 1032200 | tf_op jit(solution)/shard_map/ppermute | solution.py:276
  19.4 14.7 %collective-permute-start.1 = (bf16[2,128,672]{2,1,0:T(8,128)(2,1)S(1)}, bf16[2,128,672]{2,1,0:T(8,128)(2,1)S(1)}, u32[]{:S(2)}, u32[]{:S(2)}) collective-permute-start(bf16[2,128,672]{2,1,0:T(8,128)(2,1)S(1)} %copy-done.10), channel_id=1, source_target_pairs={{0,4},{2,6},{4,0},{6,2},{1,5},{3,7},{5,1},{7,3},{8,12},{10,14},{12... | collective-permute-start | bytes 1032200 | tf_op jit(solution)/shard_map/ppermute | solution.py:276
  24.1 16.5 %collective-permute-start.2 = (bf16[2,128,672]{2,1,0:T(8,128)(2,1)S(1)}, bf16[2,128,672]{2,1,0:T(8,128)(2,1)S(1)}, u32[]{:S(2)}, u32[]{:S(2)}) collective-permute-start(bf16[2,128,672]{2,1,0:T(8,128)(2,1)S(1)} %copy-done.9), channel_id=1, source_target_pairs={{0,6},{2,4},{4,2},{6,0},{1,7},{3,5},{5,3},{7,1},{8,14},{10,12},{12... | collective-permute-start | bytes 1032200 | tf_op jit(solution)/shard_map/ppermute | solution.py:276
  24.2 1.5 %collective-permute-start.7 = (bf16[4,84,256]{2,1,0:T(8,128)(2,1)S(1)}, bf16[4,84,256]{2,1,0:T(8,128)(2,1)S(1)}, u32[]{:S(2)}, u32[]{:S(2)}) collective-permute-start(bf16[4,84,256]{2,1,0:T(8,128)(2,1)S(1)} %pad_maximum_fusion), channel_id=1, source_target_pairs={{0,1},{1,0},{2,3},{3,2},{4,5},{5,4},{6,7},{7,6},{8,9},{9,8},{10,11... | collective-permute-start | bytes 516104 | tf_op jit(solution)/shard_map/ppermute | solution.py:284
  45.1 2.1 %collective-permute-start.8 = (bf16[12,84,256]{2,1,0:T(8,128)(2,1)S(1)}, bf16[12,84,256]{2,1,0:T(8,128)(2,1)S(1)}, u32[]{:S(2)}, u32[]{:S(2)}) collective-permute-start(bf16[12,84,256]{2,1,0:T(8,128)(2,1)S(1)} %get-tuple-element.55), channel_id=1, source_target_pairs={{0,1},{1,0},{2,3},{3,2},{4,5},{5,4},{6,7},{7,6},{8,9},{9,8},{10,11... | collective-permute-start | bytes 1548296 | tf_op jit(solution)/shard_map/ppermute | solution.py:284
  45.2 2.0 %collective-permute-start.9 = (f32[3,8,256]{2,1,0:T(8,128)S(1)}, f32[3,8,256]{2,1,0:T(8,128)S(1)}, u32[]{:S(2)}, u32[]{:S(2)}) collective-permute-start(f32[3,8,256]{2,1,0:T(8,128)S(1)} %get-tuple-element.54.stats_ref), channel_id=1, source_target_pairs={{0,1},{1,0},{2,3},{3,2},{4,5},{5,4},{6,7},{7,6},{8,9},{9,8},{10,11... | collective-permute-start | bytes 73736 | tf_op jit(solution)/shard_map/ppermute | solution.py:284
  48.1 14.5 %collective-permute-start.10 = (bf16[304,256]{1,0:T(8,128)(2,1)S(1)}, bf16[304,256]{1,0:T(8,128)(2,1)S(1)}, u32[]{:S(2)}, u32[]{:S(2)}) collective-permute-start(bf16[304,256]{1,0:T(8,128)(2,1)S(1)} %get-tuple-element.57), channel_id=1, source_target_pairs={{0,8},{8,0},{16,24},{24,16},{1,9},{9,1},{17,25},{25,17},{2,10},{10... | collective-permute-start | bytes 466952 | tf_op jit(solution)/shard_map/ppermute | solution.py:280
  50.1 13.1 %collective-permute-start.11 = (bf16[304,256]{1,0:T(8,128)(2,1)S(1)}, bf16[304,256]{1,0:T(8,128)(2,1)S(1)}, u32[]{:S(2)}, u32[]{:S(2)}) collective-permute-start(bf16[304,256]{1,0:T(8,128)(2,1)S(1)} %get-tuple-element.58), channel_id=1, source_target_pairs={{0,16},{8,24},{16,0},{24,8},{1,17},{9,25},{17,1},{25,9},{2,18},{10... | collective-permute-start | bytes 466952 | tf_op jit(solution)/shard_map/ppermute | solution.py:280
  52.3 15.5 %collective-permute-start.12 = (bf16[304,256]{1,0:T(8,128)(2,1)S(1)}, bf16[304,256]{1,0:T(8,128)(2,1)S(1)}, u32[]{:S(2)}, u32[]{:S(2)}) collective-permute-start(bf16[304,256]{1,0:T(8,128)(2,1)S(1)} %get-tuple-element.59), channel_id=1, source_target_pairs={{0,24},{8,16},{16,8},{24,0},{1,25},{9,17},{17,9},{25,1},{2,26},{10... | collective-permute-start | bytes 466952 | tf_op jit(solution)/shard_map/ppermute | solution.py:280
  68.5 9.6 %collective-permute-start.13 = (bf16[2,84,256]{2,1,0:T(8,128)(2,1)S(1)}, bf16[2,84,256]{2,1,0:T(8,128)(2,1)S(1)}, u32[]{:S(2)}, u32[]{:S(2)}) collective-permute-start(bf16[2,84,256]{2,1,0:T(8,128)(2,1)S(1)} %finish.1), channel_id=1, source_target_pairs={{0,0},{2,8},{4,16},{6,24},{8,2},{10,10},{12,18},{14,26},{16,4},{18... | collective-permute-start | bytes 258056 | tf_op jit(solution)/shard_map/ppermute | solution.py:288
  78.1 5.9 %copy-start.7 = (bf16[2,128,672]{2,1,0:T(8,128)(2,1)}, bf16[2,128,672]{2,1,0:T(8,128)(2,1)S(1)}, u32[]{:S(2)}) copy-start(bf16[2,128,672]{2,1,0:T(8,128)(2,1)S(1)} %get-tuple-element.72.s0) | copy-start | bytes 1032196
  78.1 11.4 %collective-permute-start.14 = (bf16[2,128,672]{2,1,0:T(8,128)(2,1)}, bf16[2,128,672]{2,1,0:T(8,128)(2,1)}, u32[]{:S(2)}, u32[]{:S(2)}) collective-permute-start(bf16[2,128,672]{2,1,0:T(8,128)(2,1)} %get-tuple-element.73), channel_id=1, source_target_pairs={{0,2},{2,0},{4,6},{6,4},{1,3},{3,1},{5,7},{7,5},{8,10},{10,8},{12,... | collective-permute-start | bytes 1032200 | tf_op jit(solution)/shard_map/ppermute | solution.py:276
  78.2 13.7 %collective-permute-start.15 = (bf16[2,128,672]{2,1,0:T(8,128)(2,1)}, bf16[2,128,672]{2,1,0:T(8,128)(2,1)}, u32[]{:S(2)}, u32[]{:S(2)}) collective-permute-start(bf16[2,128,672]{2,1,0:T(8,128)(2,1)} %get-tuple-element.74), channel_id=1, source_target_pairs={{0,4},{2,6},{4,0},{6,2},{1,5},{3,7},{5,1},{7,3},{8,12},{10,14},{12... | collective-permute-start | bytes 1032200 | tf_op jit(solution)/shard_map/ppermute | solution.py:276
  81.5 17.9 %collective-permute-start.16 = (bf16[2,128,672]{2,1,0:T(8,128)(2,1)S(1)}, bf16[2,128,672]{2,1,0:T(8,128)(2,1)}, u32[]{:S(2)}, u32[]{:S(2)}) collective-permute-start(bf16[2,128,672]{2,1,0:T(8,128)(2,1)S(1)} %get-tuple-element.75), channel_id=1, source_target_pairs={{0,6},{2,4},{4,2},{6,0},{1,7},{3,5},{5,3},{7,1},{8,14},{10,12},{12... | collective-permute-start | bytes 1032200 | tf_op jit(solution)/shard_map/ppermute | solution.py:276
  84.1 1.0 copy-start.2
  85.1 18.7 %all-to-all-start = ((bf16[8,84,660]{2,1,0:T(8,128)(2,1)}), bf16[8,84,660]{2,1,0:T(8,128)(2,1)S(1)}, u32[]{:S(2)}, u32[]{:S(2)}) async-start(bf16[8,84,660]{2,1,0:T(8,128)(2,1)} %copy-done.2), calls=%async_computation | async-start | bytes 2162688 | tf_op jit(solution)/shard_map/all_to_all | solution.py:357
  99.4 1.0 copy-start.8
  104.4 6.6 %collective-permute-start.17 = (bf16[84,660]{1,0:T(8,128)(2,1)S(1)}, bf16[84,660]{1,0:T(8,128)(2,1)S(1)}, u32[]{:S(2)}, u32[]{:S(2)}) collective-permute-start(bf16[84,660]{1,0:T(8,128)(2,1)S(1)} %get-tuple-element.81), channel_id=1, source_target_pairs={{0,128},{128,0},{1,129},{129,1},{2,130},{130,2},{3,131},{131,3},{4... | collective-permute-start | bytes 332648 | tf_op jit(solution)/shard_map/ppermute | solution.py:368

commit v4 on v3

--- a/solution.py
+++ b/solution.py
@@ -20,10 +20,10 @@
 SEQ_AXES = ("zp", "zl", "x_lo", "core")
 F32 = jnp.float32
 BF16 = jnp.bfloat16
-VMEM_LIMIT = 48 * 1024 * 1024
+VMEM_LIMIT = 32 * 1024 * 1024
 SMALL_LIMIT = 16 * 1024 * 1024
 COST = dict(
-    pack=1, join=1, forward=2, core=1, finish=1, backward=3, weight=2, unpack=10, sum_y=0, sum=0
+    pack=1, join=1, forward=2, core=1, finish=1, backward=3, weight=2, unpack_k=10, unpack_v=3, sum_y=0, sum=0
 )
 NT = (((1,), (1,)), ((), ()))
 NN = (((1,), (0,)), ((), ()))
@@ -59,23 +59,19 @@
                     q_ref[...] = q_all[:, cols]
 
 
-def unpack_kernel(place, s0, s1, s2, s3, gk_ref, gv_ref, all_k, all_v, sems):
+def unpack_kernel(which, place, s0, s1, s2, s3, out_ref, rows, sem):
     chip = place[0]
-    slots = (s0, s1, s2, s3)
-    copies = []
-    for n, (rows, out) in enumerate(((all_k, gk_ref), (all_v, gv_ref))):
-        for g in range(GROUPS):
-            cols = slice(g * GROUP_WIDTH, (g + 1) * GROUP_WIDTH)
-            for s in range(GROUPS):
-
-                @pl.when(lax.bitwise_xor(chip, s) == g)
-                def _():
-                    rows[:, cols] = slots[s][n]
-
-        copies.append(pltpu.make_async_copy(rows, out, sems.at[n]))
-        copies[-1].start()
-    for copy in copies:
-        copy.wait()
+    for g in range(GROUPS):
+        cols = slice(g * GROUP_WIDTH, (g + 1) * GROUP_WIDTH)
+        for s, slot in enumerate((s0, s1, s2, s3)):
+
+            @pl.when(lax.bitwise_xor(chip, s) == g)
+            def _():
+                rows[:, cols] = slot[which]
+
+    copy = pltpu.make_async_copy(rows, out_ref, sem)
+    copy.start()
+    copy.wait()
 
 
 def set_mask(place, ws_ref, bias):
@@ -92,13 +88,16 @@
         bias[s * kv_len : (s + 1) * kv_len, :] = jnp.where(visible, 0.0, NEG)
 
 
-def join_kernel(place, m0, m1, m2, m3, theirs_ref, out_ref, pieces, rows):
+def join_kernel(place, m0, m1, t0, t1, out_ref, pieces, rows):
     pair, half = place[1], place[2]
-    rows_each = m0.shape[0]
-    for j, mine in enumerate((m0, m1, m2, m3)):
-        at = lax.bitwise_xor(pair, j)
-        pieces[2 * at + half] = mine[...].astype(F32)
-        pieces[2 * at + 1 - half] = theirs_ref[j].astype(F32)
+    rows_each = m0.shape[1]
+    for j, (mine, theirs) in enumerate(((m0, t0), (m1, t1))):
+        at = 2 * lax.bitwise_xor(pair, 2 * half + j)
+        pieces[at + half] = mine[0].astype(F32)
+        pieces[at + 1 - half] = mine[1].astype(F32)
+        at = 2 * lax.bitwise_xor(pair, 2 * (1 - half) + j)
+        pieces[at + 1 - half] = theirs[0].astype(F32)
+        pieces[at + half] = theirs[1].astype(F32)
     for k in range(PIECES):
         rows[k * rows_each : (k + 1) * rows_each, :] = pieces[k]
     out_ref[...] = rows[...].astype(BF16)
@@ -284,8 +283,16 @@
     return lax.ppermute(x, "core", [(0, 1), (1, 0)])
 
 
-def trade(x, j=0):
-    return lax.ppermute(x, ("zp", "zl", "x_lo"), [(a * GROUPS + b, (b ^ j) * GROUPS + a) for a in range(GROUPS) for b in range(GROUPS)])
+ALL = [(a, b) for a in range(GROUPS) for b in range(GROUPS)]
+
+
+def trade(x):
+    return lax.ppermute(x, ("zp", "zl", "x_lo"), [(a * GROUPS + b, b * GROUPS + a) for a, b in ALL])
+
+
+def spread(x, j):
+    pairs = [((a * GROUPS + b) * 2 + c, ((b ^ j ^ (2 * c)) * GROUPS + a) * 2 + c) for a, b in ALL for c in range(2)]
+    return lax.ppermute(x, SEQ_AXES, pairs)
 
 
 def local(queries, keys, values, out_grad, w_out, window_start):
@@ -315,9 +322,10 @@
     w_out, send = lax.optimization_barrier((w_out, send))
     slots = [send[0]] + [swap_chip(send[s], s) for s in range(1, GROUPS)]
     d_own = lax.dot_general(w_out, cotangent, NN, preferred_element_type=F32).astype(BF16)
-    mine = [trade(d_own, j) for j in range(GROUPS)]
-    theirs = swap_half(jnp.stack(mine))
-    d_group = call("join", join_kernel, 5, sds((GROUP_WIDTH, q_len), BF16), [pieces, features])(place, *mine, theirs)
+    both = jnp.stack([d_own, swap_half(d_own)])
+    mine = [spread(both, j) for j in range(2)]
+    theirs = [swap_half(m) for m in mine]
+    d_group = call("join", join_kernel, 4, sds((GROUP_WIDTH, q_len), BF16), [pieces, features])(place, *mine, *theirs)
 
     keep, half, stats = call(
         "forward",
@@ -333,7 +341,8 @@
         [sds((STATS + 40, q_len), BF16)] * GROUPS,
         [pltpu.VMEM((4, 24, q_len), F32), pltpu.VMEM((GROUPS, STATS + 40, q_len), F32)],
     )(place, keep, stats, swap_half(half), swap_half(stats))
-    parts = [parts[0]] + [swap_pair(parts[j], j) for j in range(1, GROUPS)]
+    far = swap_pair(parts[2], 2)
+    parts = [parts[0], swap_pair(parts[1], 1), far, swap_pair(parts[3], 3)]
     rows = call("finish", finish_kernel, 4, sds((2, rows_each, q_len), BF16), [pltpu.VMEM((2, 24, q_len), F32)])(place, *parts)
     rows, parts = lax.optimization_barrier((rows, parts))
     rows = trade(rows)
@@ -355,16 +364,17 @@
         limit=SMALL_LIMIT,
     )(rows, cotangent)
     gw = lax.all_to_all(gw, "y", 0, 0, tiled=True)
-    grad_k, grad_v = call(
-        "unpack",
-        unpack_kernel,
-        4,
-        [sds((kv_len, width), BF16)] * 2,
-        [whole, whole, pltpu.SemaphoreType.DMA((2,))],
-        out_blocks=[ANY] * 2,
-    )(place, *back)
+
+    def unpack(which, name, back):
+        kernel = functools.partial(unpack_kernel, which)
+        out = sds((kv_len, width), BF16)
+        return call(name, kernel, 4, out, [whole, pltpu.SemaphoreType.DMA], out_blocks=ANY, limit=SMALL_LIMIT)(place, *back)
+
+    grad_k = unpack(0, "unpack_k", back)
     gw, grad_k = lax.optimization_barrier((gw, grad_k))
     keep, half = call("sum_y", sum_y_kernel, 1, [sds((rows_each, part), F32), sds((rows_each, part), BF16)], limit=SMALL_LIMIT)(place, gw)
+    keep, back = lax.optimization_barrier((keep, back))
+    grad_v = unpack(1, "unpack_v", back)
     half = lax.ppermute(half, "x_hi", [(0, 1), (1, 0)])
     grad_weight = call("sum", sum_kernel, 2, sds((rows_each, part), BF16), scalars=0, limit=SMALL_LIMIT)(keep, half)
     return grad_q[None], grad_k[None], grad_v[None], grad_weight

time: 112 us -> 108 us (0.964)
  waiting for transfers between devices: 45.7 us -> 29.5 us
  starting transfers between devices: 41.2 us -> 50.8 us
  Pallas kernels: 20.8 us -> 22.9 us
    ppermute x3 -> x5, starting transfers between devices: 0.68 us -> 16.8 us  [swap_half(): return lax.ppermute(x, 'core', [(0, 1), (1, 0)])]
    ppermute x6, waiting for transfers between devices: 24 us -> 9.74 us  [swap_chip(): return lax.ppermute(x, ('zl', 'x_lo'), [(i, i ^ s) for i in range(GROUPS)])]
    ppermute x5 -> x3, starting transfers between devices: 18.8 us -> 13 us  [the longest x2 6.71 us: spread(): return lax.ppermute(x, SEQ_AXES, pairs)]
    ppermute x1, waiting for transfers between devices: 5.16 us -> 3 us  [local(): half = lax.ppermute(half, 'x_hi', [(0, 1), (1, 0)])]
    pallas_call x2 -> x3, Pallas kernels: 3.56 us -> 5.43 us  [the longest x2 4.8 us: unpack(): call(name, kernel, 4, out, [whole, pltpu.SemaphoreType.DMA], out_blocks=A...]
    ppermute x6, starting transfers between devices: 9.14 us -> 7.63 us  [swap_chip(): return lax.ppermute(x, ('zl', 'x_lo'), [(i, i ^ s) for i in range(GROUPS)])]
    ppermute x3 -> x5, waiting for transfers between devices: 2.86 us -> 2.27 us  [swap_half(): return lax.ppermute(x, 'core', [(0, 1), (1, 0)])]
    unnamed x24 -> x26, local copies, waits for them, and re-layouts: 2.03 us -> 2.26 us
  transfers between devices with their start and end apart: 19 -> 19, of which waited for: 13 -> 11; matrix products, arithmetic and copies ran while one was open for 0% -> 0% of each run, Pallas kernels for 8% -> 10%
where the time goes in v4:
time: 108 us; the launch traced here: 107 us
  starting transfers between devices  50.8 us (47%)
  waiting for transfers between devices  29.5 us (27%)
  Pallas kernels  22.9 us (21%)
  local copies, waits for them, and re-layouts  2.26 us (2%)
    ppermute x5, starting transfers between devices, swap_half(): return lax.ppermute(x, 'core', [(0, 1), (1, 0)])  16.8 us
    ppermute x3, waiting for transfers between devices, swap_pair(): return lax.ppermute(x, 'zp', [(i, i ^ j) for i in range(GROUPS)])  13 us
    ppermute x6, waiting for transfers between devices, swap_chip(): return lax.ppermute(x, ('zl', 'x_lo'), [(i, i ^ s) for i in range(GROUPS)])  9.74 us
    ppermute x6, starting transfers between devices, swap_chip(): return lax.ppermute(x, ('zl', 'x_lo'), [(i, i ^ s) for i in range(GROUPS)])  7.63 us
    ppermute x3, starting transfers between devices, swap_pair(): return lax.ppermute(x, 'zp', [(i, i ^ j) for i in range(GROUPS)])  7.56 us
    ppermute x2, starting transfers between devices, spread(): return lax.ppermute(x, SEQ_AXES, pairs)  6.71 us
    ppermute x1, starting transfers between devices, trade(): lax.ppermute(x, ('zp', 'zl', 'x_lo'), [(a * GROUPS + b, b * GROUPS + a) f...  6.31 us
    pallas_call x2, Pallas kernels, unpack(): call(name, kernel, 4, out, [whole, pltpu.SemaphoreType.DMA], out_blocks=A...  4.8 us
  transfers between devices with their start and end apart: 19, of which 11 were waited for; matrix products, arithmetic and copies ran while one was open for 0% of the time, Pallas kernels for 10%

profile of v4, /device:TPU:6, one launch (start us, length us, event | category | flops | bytes accessed | tf_op | source)
XLA Modules:
  0.0 107.5 jit_solution(4494396312058541132)
XLA Ops:
  0.6 0.0 copy-start
  0.7 0.6 pad_add_fusion.place
  1.3 4.2 %pack.1 = (bf16[2,128,672]{2,1,0:T(8,128)(2,1)}, bf16[2,128,672]{2,1,0:T(8,128)(2,1)}, bf16[2,128,672]{2,1,0:T(8,128)(2,1)}, bf16[2,128,672]{2,1,0:T(8,128)(2,1)}, bf16[256,672]{1,0:T(8,128)(2,1)}) custom-call(s32[4]{0:T(128)} %pad_add_fusion.place, bf16[128,2688]{1,0:T(8,128)(2,1)} %bitcast.27, bf16[128,2688]{1,0:T(8,128)(2,1)} %bitcast.28, ...), custom_call_target="tpu_custom_call" | custom-call | flops 1000000000 | tf_op jit(solution)/shard_map/pack/pallas_call | solution.py:313
  5.4 0.0 copy-start.12
  5.5 0.6 fusion.2
  6.1 0.0 copy-start.4
  6.1 0.0 copy-start.5
  6.1 0.1 collective-permute-start.3
  6.2 0.2 copy-done.12
  6.4 0.7 collective-permute-start
  7.1 2.0 %collective-permute-start.1 = (bf16[2,128,672]{2,1,0:T(8,128)(2,1)S(1)}, bf16[2,128,672]{2,1,0:T(8,128)(2,1)S(1)}, u32[]{:S(2)}, u32[]{:S(2)}) collective-permute-start(bf16[2,128,672]{2,1,0:T(8,128)(2,1)S(1)} %copy-done.11), channel_id=1, source_target_pairs={{0,4},{2,6},{4,0},{6,2},{1,5},{3,7},{5,1},{7,3},{8,12},{10,14},{12... | collective-permute-start | bytes 1032200 | tf_op jit(solution)/shard_map/ppermute | solution.py:275
  9.2 0.7 collective-permute-start.2
  10.0 0.9 collective-permute-start.5
  10.9 5.8 %collective-permute-start.4 = (bf16[2,84,256]{2,1,0:T(8,128)(2,1)S(1)}, bf16[2,84,256]{2,1,0:T(8,128)(2,1)S(1)}, u32[]{:S(2)}, u32[]{:S(2)}) collective-permute-start(bf16[2,84,256]{2,1,0:T(8,128)(2,1)S(1)} %pad_maximum_fusion), channel_id=1, source_target_pairs={{0,0},{1,17},{2,8},{3,25},{4,16},{5,1},{6,24},{7,9},{8,2},{9,19},{... | collective-permute-start | bytes 258056 | tf_op jit(solution)/shard_map/ppermute | solution.py:295
  16.7 0.3 collective-permute-done.5.m1
  16.9 15.3 %collective-permute-start.7 = (bf16[2,84,256]{2,1,0:T(8,128)(2,1)S(1)}, bf16[2,84,256]{2,1,0:T(8,128)(2,1)S(1)}, u32[]{:S(2)}, u32[]{:S(2)}) collective-permute-start(bf16[2,84,256]{2,1,0:T(8,128)(2,1)S(1)} %collective-permute-done.5.m1), channel_id=1, source_target_pairs={{0,1},{1,0},{2,3},{3,2},{4,5},{5,4},{6,7},{7,6},{8,9},{9,8},{10,11... | collective-permute-start | bytes 258056 | tf_op jit(solution)/shard_map/ppermute | solution.py:283
  32.2 0.7 collective-permute-start.6
  32.9 0.2 collective-permute-done.7.t1
  33.1 0.7 collective-permute-done.6.t0
  33.9 0.6 join.1.d_ref
  34.6 4.5 %forward.1 = (f32[12,84,256]{2,1,0:T(8,128)S(1)}, bf16[12,84,256]{2,1,0:T(8,128)(2,1)S(1)}, f32[3,8,256]{2,1,0:T(8,128)S(1)}) custom-call(s32[4]{0:T(128)S(1)} %copy-done.3, s32[1,256]{1,0:T(1,128)S(1)} %bitcast.22, bf16[256,672]{1,0:T(8,128)(2,1)S(1)} %copy-done.6, bf16[2,128,672]{2,1,0:T(8,128)(2,1)S(1)} %copy-done.5, ...), custom_call_target="tpu_custom_call" | custom-call | flops 2000000000 | tf_op jit(solution)/shard_map/forward/pallas_call | solution.py:330
  39.1 0.4 collective-permute-start.8
  39.6 0.3 collective-permute-start.9
  39.8 1.3 %collective-permute-done.9.got_stats_ref = f32[3,8,256]{2,1,0:T(8,128)S(1)} collective-permute-done((f32[3,8,256]{2,1,0:T(8,128)S(1)}, f32[3,8,256]{2,1,0:T(8,128)S(1)}, u32[]{:S(2)}, u32[]{:S(2)}) %collective-permute-start.9) | collective-permute-done | bytes 24608 | tf_op jit(solution)/shard_map/ppermute | solution.py:283
  41.2 1.0 core.1
  42.2 1.5 %collective-permute-start.10 = (bf16[304,256]{1,0:T(8,128)(2,1)S(1)}, bf16[304,256]{1,0:T(8,128)(2,1)S(1)}, u32[]{:S(2)}, u32[]{:S(2)}) collective-permute-start(bf16[304,256]{1,0:T(8,128)(2,1)S(1)} %get-tuple-element.60), channel_id=1, source_target_pairs={{0,8},{8,0},{16,24},{24,16},{1,9},{9,1},{17,25},{25,17},{2,10},{10... | collective-permute-start | bytes 466952 | tf_op jit(solution)/shard_map/ppermute | solution.py:279
  43.6 6.1 %collective-permute-start.11 = (bf16[304,256]{1,0:T(8,128)(2,1)S(1)}, bf16[304,256]{1,0:T(8,128)(2,1)S(1)}, u32[]{:S(2)}, u32[]{:S(2)}) collective-permute-start(bf16[304,256]{1,0:T(8,128)(2,1)S(1)} %get-tuple-element.61), channel_id=1, source_target_pairs={{0,16},{8,24},{16,0},{24,8},{1,17},{9,25},{17,1},{25,9},{2,18},{10... | collective-permute-start | bytes 466952 | tf_op jit(solution)/shard_map/ppermute | solution.py:279
  49.7 11.0 %collective-permute-done.11.p2 = bf16[304,256]{1,0:T(8,128)(2,1)S(1)} collective-permute-done((bf16[304,256]{1,0:T(8,128)(2,1)S(1)}, bf16[304,256]{1,0:T(8,128)(2,1)S(1)}, u32[]{:S(2)}, u32[]{:S(2)}) %collective-permute-start.11) | collective-permute-done | bytes 155680 | tf_op jit(solution)/shard_map/ppermute | solution.py:279
  60.8 2.0 %collective-permute-done.12.p3 = bf16[304,256]{1,0:T(8,128)(2,1)S(1)} collective-permute-done((bf16[304,256]{1,0:T(8,128)(2,1)S(1)}, bf16[304,256]{1,0:T(8,128)(2,1)S(1)}, u32[]{:S(2)}, u32[]{:S(2)}) %collective-permute-start.12) | collective-permute-done | bytes 155680 | tf_op jit(solution)/shard_map/ppermute | solution.py:279
  62.7 0.7 finish.1
  63.5 6.3 %collective-permute-start.13 = (bf16[2,84,256]{2,1,0:T(8,128)(2,1)S(1)}, bf16[2,84,256]{2,1,0:T(8,128)(2,1)S(1)}, u32[]{:S(2)}, u32[]{:S(2)}) collective-permute-start(bf16[2,84,256]{2,1,0:T(8,128)(2,1)S(1)} %finish.1), channel_id=1, source_target_pairs={{0,0},{2,8},{4,16},{6,24},{8,2},{10,10},{12,18},{14,26},{16,4},{18... | collective-permute-start | bytes 258056 | tf_op jit(solution)/shard_map/ppermute | solution.py:290
  69.8 4.0 %backward.1 = (bf16[2,128,672]{2,1,0:T(8,128)(2,1)S(1)}, bf16[2,128,672]{2,1,0:T(8,128)(2,1)}, bf16[2,128,672]{2,1,0:T(8,128)(2,1)}, bf16[2,128,672]{2,1,0:T(8,128)(2,1)}) custom-call(s32[4]{0:T(128)S(1)} %copy-done.3, s32[1,256]{1,0:T(1,128)S(1)} %bitcast.23, bf16[256,672]{1,0:T(8,128)(2,1)S(1)} %copy-done.6, bf16[2,128,672]{2,1,0:T(8,128)(2,1)S(1)} %copy-done.5, ...), custom_call_target="tpu_custom_call" | custom-call | flops 3000000000 | tf_op jit(solution)/shard_map/backward/pallas_call | solution.py:350
  73.8 0.1 collective-permute-done.13.rows_ref
  74.0 2.7 %collective-permute-start.15 = (bf16[2,128,672]{2,1,0:T(8,128)(2,1)}, bf16[2,128,672]{2,1,0:T(8,128)(2,1)}, u32[]{:S(2)}, u32[]{:S(2)}) collective-permute-start(bf16[2,128,672]{2,1,0:T(8,128)(2,1)} %get-tuple-element.77), channel_id=1, source_target_pairs={{0,4},{2,6},{4,0},{6,2},{1,5},{3,7},{5,1},{7,3},{8,12},{10,14},{12... | collective-permute-start | bytes 1032200 | tf_op jit(solution)/shard_map/ppermute | solution.py:275
  76.6 1.5 %collective-permute-start.16 = (bf16[2,128,672]{2,1,0:T(8,128)(2,1)}, bf16[2,128,672]{2,1,0:T(8,128)(2,1)}, u32[]{:S(2)}, u32[]{:S(2)}) collective-permute-start(bf16[2,128,672]{2,1,0:T(8,128)(2,1)} %get-tuple-element.78), channel_id=1, source_target_pairs={{0,6},{2,4},{4,2},{6,0},{1,7},{3,5},{5,3},{7,1},{8,14},{10,12},{12... | collective-permute-start | bytes 1032200 | tf_op jit(solution)/shard_map/ppermute | solution.py:275
  78.1 1.6 %weight.1 = (bf16[8,84,660]{2,1,0:T(8,128)(2,1)S(1)}, bf16[84,256]{1,0:T(8,128)(2,1)}) custom-call(bf16[2,84,256]{2,1,0:T(8,128)(2,1)S(1)} %collective-permute-done.13.rows_ref, bf16[5280,256]{1,0:T(8,128)(2,1)S(1)} %bitcast.21), custom_call_target="tpu_custom_call" | custom-call | flops 2000000000 | tf_op jit(solution)/shard_map/weight/pallas_call | solution.py:357
  79.7 1.0 copy-done.2
  80.7 4.6 %all-to-all-start = ((bf16[8,84,660]{2,1,0:T(8,128)(2,1)}), bf16[8,84,660]{2,1,0:T(8,128)(2,1)S(1)}, u32[]{:S(2)}, u32[]{:S(2)}) async-start(bf16[8,84,660]{2,1,0:T(8,128)(2,1)} %copy-done.2), calls=%async_computation | async-start | bytes 2162688 | tf_op jit(solution)/shard_map/all_to_all | solution.py:366
  85.3 1.7 %collective-permute-done.15.s2 = bf16[2,128,672]{2,1,0:T(8,128)(2,1)} collective-permute-done((bf16[2,128,672]{2,1,0:T(8,128)(2,1)}, bf16[2,128,672]{2,1,0:T(8,128)(2,1)}, u32[]{:S(2)}, u32[]{:S(2)}) %collective-permute-start.15) | collective-permute-done | bytes 344096 | tf_op jit(solution)/shard_map/ppermute | solution.py:275
  87.0 8.0 %collective-permute-done.16.s3 = bf16[2,128,672]{2,1,0:T(8,128)(2,1)} collective-permute-done((bf16[2,128,672]{2,1,0:T(8,128)(2,1)}, bf16[2,128,672]{2,1,0:T(8,128)(2,1)}, u32[]{:S(2)}, u32[]{:S(2)}) %collective-permute-start.16) | collective-permute-done | bytes 344096 | tf_op jit(solution)/shard_map/ppermute | solution.py:275
  95.0 1.0 copy-done.8
  96.0 2.4 %unpack_k.1 = bf16[128,2688]{1,0:T(8,128)(2,1)} custom-call(s32[4]{0:T(128)S(1)} %copy-done.3, bf16[2,128,672]{2,1,0:T(8,128)(2,1)S(1)} %copy-done.8, bf16[2,128,672]{2,1,0:T(8,128)(2,1)S(1)} %collective-permute-done.14.s1, bf16[2,128,672]{2,1,0:T(8,128)(2,1)} %collective-permute-done.15.s2, bf16[2,128,672]{2,1,0:T(8,128)(2,1)} %collective-permute-done.16.s3), custom_call_target="tpu_custom_call" | custom-call | flops 10000000000 | tf_op jit(solution)/shard_map/unpack_k/pallas_call | solution.py:371
  98.4 1.1 %all-to-all-done.x_ref = bf16[8,84,660]{2,1,0:T(8,128)(2,1)S(1)} async-done(((bf16[8,84,660]{2,1,0:T(8,128)(2,1)}), bf16[8,84,660]{2,1,0:T(8,128)(2,1)S(1)}, u32[]{:S(2)}, u32[]{:S(2)}) %all-to-all-start) | async-done | bytes 887072 | tf_op jit(solution)/shard_map/all_to_all | solution.py:366
  99.5 0.7 sum_y.1
  100.2 1.2 %collective-permute-start.17 = (bf16[84,660]{1,0:T(8,128)(2,1)S(1)}, bf16[84,660]{1,0:T(8,128)(2,1)S(1)}, u32[]{:S(2)}, u32[]{:S(2)}) collective-permute-start(bf16[84,660]{1,0:T(8,128)(2,1)S(1)} %get-tuple-element.87), channel_id=1, source_target_pairs={{0,128},{128,0},{1,129},{129,1},{2,130},{130,2},{3,131},{131,3},{4... | collective-permute-start | bytes 332648 | tf_op jit(solution)/shard_map/ppermute | solution.py:378
  101.4 2.4 %unpack_v.1 = bf16[128,2688]{1,0:T(8,128)(2,1)} custom-call(s32[4]{0:T(128)S(1)} %copy-done.3, bf16[2,128,672]{2,1,0:T(8,128)(2,1)S(1)} %copy-done.9, bf16[2,128,672]{2,1,0:T(8,128)(2,1)S(1)} %collective-permute-done.14.s1, bf16[2,128,672]{2,1,0:T(8,128)(2,1)} %collective-permute-done.15.s2, bf16[2,128,672]{2,1,0:T(8,128)(2,1)} %collective-permute-done.16.s3), custom_call_target="tpu_custom_call" | custom-call | flops 3000000000 | tf_op jit(solution)/shard_map/unpack_v/pallas_call | solution.py:371
  103.8 3.0 %collective-permute-done.17.got_ref = bf16[84,660]{1,0:T(8,128)(2,1)S(1)} collective-permute-done((bf16[84,660]{1,0:T(8,128)(2,1)S(1)}, bf16[84,660]{1,0:T(8,128)(2,1)S(1)}, u32[]{:S(2)}, u32[]{:S(2)}) %collective-permute-start.17) | collective-permute-done | bytes 110912 | tf_op jit(solution)/shard_map/ppermute | solution.py:378
  106.8 0.7 sum.1
  (30 shorter events, 0.1 us)
Async XLA Ops:
  0.6 4.9 %copy-start = (bf16[84,5280]{1,0:T(8,128)(2,1)S(1)}, bf16[84,5280]{1,0:T(8,128)(2,1)}, u32[]{:S(2)}) copy-start(bf16[84,5280]{1,0:T(8,128)(2,1)} %param.10) | copy-start | bytes 2661124
  0.7 4.8 %copy-start.1 = (bf16[1,256,5280]{1,2,0:T(8,128)(2,1)S(1)}, bf16[1,256,5280]{1,2,0:T(8,128)(2,1)}, u32[]{:S(2)}) copy-start(bf16[1,256,5280]{1,2,0:T(8,128)(2,1)} %param.9) | copy-start | bytes 8110084
  5.4 1.0 copy-start.12
  5.5 1.7 %copy-start.11 = (bf16[2,128,672]{2,1,0:T(8,128)(2,1)S(1)}, bf16[2,128,672]{2,1,0:T(8,128)(2,1)}, u32[]{:S(2)}) copy-start(bf16[2,128,672]{2,1,0:T(8,128)(2,1)} %get-tuple-element.53) | copy-start | bytes 1032196
  5.5 3.7 %copy-start.10 = (bf16[2,128,672]{2,1,0:T(8,128)(2,1)S(1)}, bf16[2,128,672]{2,1,0:T(8,128)(2,1)}, u32[]{:S(2)}) copy-start(bf16[2,128,672]{2,1,0:T(8,128)(2,1)} %get-tuple-element.54) | copy-start | bytes 1032196
  5.5 28.4 %copy-start.3 = (s32[4]{0:T(128)S(1)}, s32[4]{0:T(128)}, u32[]{:S(2)}) copy-start(s32[4]{0:T(128)} %pad_add_fusion.place) | copy-start | bytes 52
  6.1 28.5 %copy-start.4 = (s32[256]{0:T(256)S(1)}, s32[256]{0:T(256)}, u32[]{:S(2)}) copy-start(s32[256]{0:T(256)} %param.11) | copy-start | bytes 3076
  6.1 28.5 %copy-start.5 = (bf16[2,128,672]{2,1,0:T(8,128)(2,1)S(1)}, bf16[2,128,672]{2,1,0:T(8,128)(2,1)}, u32[]{:S(2)}) copy-start(bf16[2,128,672]{2,1,0:T(8,128)(2,1)} %get-tuple-element.51.s0) | copy-start | bytes 1032196
  6.1 28.5 %copy-start.6 = (bf16[256,672]{1,0:T(8,128)(2,1)S(1)}, bf16[256,672]{1,0:T(8,128)(2,1)}, u32[]{:S(2)}) copy-start(bf16[256,672]{1,0:T(8,128)(2,1)} %get-tuple-element.46.q_ref) | copy-start | bytes 1032196
  6.1 3.8 %collective-permute-start.3 = (bf16[84,256]{1,0:T(8,128)(2,1)S(1)}, bf16[84,256]{1,0:T(8,128)(2,1)S(1)}, u32[]{:S(2)}, u32[]{:S(2)}) collective-permute-start(bf16[84,256]{1,0:T(8,128)(2,1)S(1)} %fusion.2), channel_id=1, source_target_pairs={{0,1},{1,0},{2,3},{3,2},{4,5},{5,4},{6,7},{7,6},{8,9},{9,8},{10,11... | collective-permute-start | bytes 129032 | tf_op jit(solution)/shard_map/ppermute | solution.py:283
  6.4 28.1 %collective-permute-start = (bf16[2,128,672]{2,1,0:T(8,128)(2,1)S(1)}, bf16[2,128,672]{2,1,0:T(8,128)(2,1)S(1)}, u32[]{:S(2)}, u32[]{:S(2)}) collective-permute-start(bf16[2,128,672]{2,1,0:T(8,128)(2,1)S(1)} %copy-done.12), channel_id=1, source_target_pairs={{0,2},{2,0},{4,6},{6,4},{1,3},{3,1},{5,7},{7,5},{8,10},{10,8},{12,... | collective-permute-start | bytes 1032200 | tf_op jit(solution)/shard_map/ppermute | solution.py:275
  7.1 27.4 %collective-permute-start.1 = (bf16[2,128,672]{2,1,0:T(8,128)(2,1)S(1)}, bf16[2,128,672]{2,1,0:T(8,128)(2,1)S(1)}, u32[]{:S(2)}, u32[]{:S(2)}) collective-permute-start(bf16[2,128,672]{2,1,0:T(8,128)(2,1)S(1)} %copy-done.11), channel_id=1, source_target_pairs={{0,4},{2,6},{4,0},{6,2},{1,5},{3,7},{5,1},{7,3},{8,12},{10,14},{12... | collective-permute-start | bytes 1032200 | tf_op jit(solution)/shard_map/ppermute | solution.py:275
  9.2 25.3 %collective-permute-start.2 = (bf16[2,128,672]{2,1,0:T(8,128)(2,1)S(1)}, bf16[2,128,672]{2,1,0:T(8,128)(2,1)S(1)}, u32[]{:S(2)}, u32[]{:S(2)}) collective-permute-start(bf16[2,128,672]{2,1,0:T(8,128)(2,1)S(1)} %copy-done.10), channel_id=1, source_target_pairs={{0,6},{2,4},{4,2},{6,0},{1,7},{3,5},{5,3},{7,1},{8,14},{10,12},{12... | collective-permute-start | bytes 1032200 | tf_op jit(solution)/shard_map/ppermute | solution.py:275
  10.0 7.0 %collective-permute-start.5 = (bf16[2,84,256]{2,1,0:T(8,128)(2,1)S(1)}, bf16[2,84,256]{2,1,0:T(8,128)(2,1)S(1)}, u32[]{:S(2)}, u32[]{:S(2)}) collective-permute-start(bf16[2,84,256]{2,1,0:T(8,128)(2,1)S(1)} %pad_maximum_fusion), channel_id=1, source_target_pairs={{0,8},{1,25},{2,0},{3,17},{4,24},{5,9},{6,16},{7,1},{8,10},{9,27},... | collective-permute-start | bytes 258056 | tf_op jit(solution)/shard_map/ppermute | solution.py:295
  10.9 21.4 %collective-permute-start.4 = (bf16[2,84,256]{2,1,0:T(8,128)(2,1)S(1)}, bf16[2,84,256]{2,1,0:T(8,128)(2,1)S(1)}, u32[]{:S(2)}, u32[]{:S(2)}) collective-permute-start(bf16[2,84,256]{2,1,0:T(8,128)(2,1)S(1)} %pad_maximum_fusion), channel_id=1, source_target_pairs={{0,0},{1,17},{2,8},{3,25},{4,16},{5,1},{6,24},{7,9},{8,2},{9,19},{... | collective-permute-start | bytes 258056 | tf_op jit(solution)/shard_map/ppermute | solution.py:295
  16.9 16.2 %collective-permute-start.7 = (bf16[2,84,256]{2,1,0:T(8,128)(2,1)S(1)}, bf16[2,84,256]{2,1,0:T(8,128)(2,1)S(1)}, u32[]{:S(2)}, u32[]{:S(2)}) collective-permute-start(bf16[2,84,256]{2,1,0:T(8,128)(2,1)S(1)} %collective-permute-done.5.m1), channel_id=1, source_target_pairs={{0,1},{1,0},{2,3},{3,2},{4,5},{5,4},{6,7},{7,6},{8,9},{9,8},{10,11... | collective-permute-start | bytes 258056 | tf_op jit(solution)/shard_map/ppermute | solution.py:283
  32.2 1.7 %collective-permute-start.6 = (bf16[2,84,256]{2,1,0:T(8,128)(2,1)S(1)}, bf16[2,84,256]{2,1,0:T(8,128)(2,1)S(1)}, u32[]{:S(2)}, u32[]{:S(2)}) collective-permute-start(bf16[2,84,256]{2,1,0:T(8,128)(2,1)S(1)} %collective-permute-done.4.m0), channel_id=1, source_target_pairs={{0,1},{1,0},{2,3},{3,2},{4,5},{5,4},{6,7},{7,6},{8,9},{9,8},{10,11... | collective-permute-start | bytes 258056 | tf_op jit(solution)/shard_map/ppermute | solution.py:283
  39.1 2.1 %collective-permute-start.8 = (bf16[12,84,256]{2,1,0:T(8,128)(2,1)S(1)}, bf16[12,84,256]{2,1,0:T(8,128)(2,1)S(1)}, u32[]{:S(2)}, u32[]{:S(2)}) collective-permute-start(bf16[12,84,256]{2,1,0:T(8,128)(2,1)S(1)} %get-tuple-element.58), channel_id=1, source_target_pairs={{0,1},{1,0},{2,3},{3,2},{4,5},{5,4},{6,7},{7,6},{8,9},{9,8},{10,11... | collective-permute-start | bytes 1548296 | tf_op jit(solution)/shard_map/ppermute | solution.py:283
  39.6 1.6 %collective-permute-start.9 = (f32[3,8,256]{2,1,0:T(8,128)S(1)}, f32[3,8,256]{2,1,0:T(8,128)S(1)}, u32[]{:S(2)}, u32[]{:S(2)}) collective-permute-start(f32[3,8,256]{2,1,0:T(8,128)S(1)} %get-tuple-element.57.stats_ref), channel_id=1, source_target_pairs={{0,1},{1,0},{2,3},{3,2},{4,5},{5,4},{6,7},{7,6},{8,9},{9,8},{10,11... | collective-permute-start | bytes 73736 | tf_op jit(solution)/shard_map/ppermute | solution.py:283
  42.2 7.6 %collective-permute-start.10 = (bf16[304,256]{1,0:T(8,128)(2,1)S(1)}, bf16[304,256]{1,0:T(8,128)(2,1)S(1)}, u32[]{:S(2)}, u32[]{:S(2)}) collective-permute-start(bf16[304,256]{1,0:T(8,128)(2,1)S(1)} %get-tuple-element.60), channel_id=1, source_target_pairs={{0,8},{8,0},{16,24},{24,16},{1,9},{9,1},{17,25},{25,17},{2,10},{10... | collective-permute-start | bytes 466952 | tf_op jit(solution)/shard_map/ppermute | solution.py:279
  43.6 17.1 %collective-permute-start.11 = (bf16[304,256]{1,0:T(8,128)(2,1)S(1)}, bf16[304,256]{1,0:T(8,128)(2,1)S(1)}, u32[]{:S(2)}, u32[]{:S(2)}) collective-permute-start(bf16[304,256]{1,0:T(8,128)(2,1)S(1)} %get-tuple-element.61), channel_id=1, source_target_pairs={{0,16},{8,24},{16,0},{24,8},{1,17},{9,25},{17,1},{25,9},{2,18},{10... | collective-permute-start | bytes 466952 | tf_op jit(solution)/shard_map/ppermute | solution.py:279
  49.7 13.0 %collective-permute-start.12 = (bf16[304,256]{1,0:T(8,128)(2,1)S(1)}, bf16[304,256]{1,0:T(8,128)(2,1)S(1)}, u32[]{:S(2)}, u32[]{:S(2)}) collective-permute-start(bf16[304,256]{1,0:T(8,128)(2,1)S(1)} %get-tuple-element.62), channel_id=1, source_target_pairs={{0,24},{8,16},{16,8},{24,0},{1,25},{9,17},{17,9},{25,1},{2,26},{10... | collective-permute-start | bytes 466952 | tf_op jit(solution)/shard_map/ppermute | solution.py:279
  63.5 10.5 %collective-permute-start.13 = (bf16[2,84,256]{2,1,0:T(8,128)(2,1)S(1)}, bf16[2,84,256]{2,1,0:T(8,128)(2,1)S(1)}, u32[]{:S(2)}, u32[]{:S(2)}) collective-permute-start(bf16[2,84,256]{2,1,0:T(8,128)(2,1)S(1)} %finish.1), channel_id=1, source_target_pairs={{0,0},{2,8},{4,16},{6,24},{8,2},{10,10},{12,18},{14,26},{16,4},{18... | collective-permute-start | bytes 258056 | tf_op jit(solution)/shard_map/ppermute | solution.py:290
  73.8 5.9 %copy-start.7 = (bf16[2,128,672]{2,1,0:T(8,128)(2,1)}, bf16[2,128,672]{2,1,0:T(8,128)(2,1)S(1)}, u32[]{:S(2)}) copy-start(bf16[2,128,672]{2,1,0:T(8,128)(2,1)S(1)} %get-tuple-element.82.s0) | copy-start | bytes 1032196
  74.0 11.3 %collective-permute-start.14 = (bf16[2,128,672]{2,1,0:T(8,128)(2,1)}, bf16[2,128,672]{2,1,0:T(8,128)(2,1)S(1)}, u32[]{:S(2)}, u32[]{:S(2)}) collective-permute-start(bf16[2,128,672]{2,1,0:T(8,128)(2,1)} %get-tuple-element.76), channel_id=1, source_target_pairs={{0,2},{2,0},{4,6},{6,4},{1,3},{3,1},{5,7},{7,5},{8,10},{10,8},{12,... | collective-permute-start | bytes 1032200 | tf_op jit(solution)/shard_map/ppermute | solution.py:275
  74.0 13.0 %collective-permute-start.15 = (bf16[2,128,672]{2,1,0:T(8,128)(2,1)}, bf16[2,128,672]{2,1,0:T(8,128)(2,1)}, u32[]{:S(2)}, u32[]{:S(2)}) collective-permute-start(bf16[2,128,672]{2,1,0:T(8,128)(2,1)} %get-tuple-element.77), channel_id=1, source_target_pairs={{0,4},{2,6},{4,0},{6,2},{1,5},{3,7},{5,1},{7,3},{8,12},{10,14},{12... | collective-permute-start | bytes 1032200 | tf_op jit(solution)/shard_map/ppermute | solution.py:275
  76.6 18.4 %collective-permute-start.16 = (bf16[2,128,672]{2,1,0:T(8,128)(2,1)}, bf16[2,128,672]{2,1,0:T(8,128)(2,1)}, u32[]{:S(2)}, u32[]{:S(2)}) collective-permute-start(bf16[2,128,672]{2,1,0:T(8,128)(2,1)} %get-tuple-element.78), channel_id=1, source_target_pairs={{0,6},{2,4},{4,2},{6,0},{1,7},{3,5},{5,3},{7,1},{8,14},{10,12},{12... | collective-permute-start | bytes 1032200 | tf_op jit(solution)/shard_map/ppermute | solution.py:275
  79.7 1.0 copy-start.2
  80.7 20.7 %copy-start.9 = (bf16[2,128,672]{2,1,0:T(8,128)(2,1)S(1)}, bf16[2,128,672]{2,1,0:T(8,128)(2,1)}, u32[]{:S(2)}) copy-start(bf16[2,128,672]{2,1,0:T(8,128)(2,1)} %copy-done.7) | copy-start | bytes 1032196
  80.7 18.8 %all-to-all-start = ((bf16[8,84,660]{2,1,0:T(8,128)(2,1)}), bf16[8,84,660]{2,1,0:T(8,128)(2,1)S(1)}, u32[]{:S(2)}, u32[]{:S(2)}) async-start(bf16[8,84,660]{2,1,0:T(8,128)(2,1)} %copy-done.2), calls=%async_computation | async-start | bytes 2162688 | tf_op jit(solution)/shard_map/all_to_all | solution.py:366
  95.0 1.0 copy-start.8
  100.2 6.6 %collective-permute-start.17 = (bf16[84,660]{1,0:T(8,128)(2,1)S(1)}, bf16[84,660]{1,0:T(8,128)(2,1)S(1)}, u32[]{:S(2)}, u32[]{:S(2)}) collective-permute-start(bf16[84,660]{1,0:T(8,128)(2,1)S(1)} %get-tuple-element.87), channel_id=1, source_target_pairs={{0,128},{128,0},{1,129},{129,1},{2,130},{130,2},{3,131},{131,3},{4... | collective-permute-start | bytes 332648 | tf_op jit(solution)/shard_map/ppermute | solution.py:378

commit v5 on v4

--- a/solution.py
+++ b/solution.py
@@ -23,7 +23,7 @@
 VMEM_LIMIT = 32 * 1024 * 1024
 SMALL_LIMIT = 16 * 1024 * 1024
 COST = dict(
-    pack=1, join=1, forward=2, core=1, finish=1, backward=3, weight=2, unpack_k=10, unpack_v=3, sum_y=0, sum=0
+    pack=1, own=1, join=1, forward=2, core=1, finish=1, backward=3, weight=2, unpack_k=10, unpack_v=3, sum_y=0, sum=0
 )
 NT = (((1,), (1,)), ((), ()))
 NN = (((1,), (0,)), ((), ()))
@@ -34,29 +34,30 @@
     return lax.dot_general(a, b, dims, preferred_element_type=F32)
 
 
-def pack_kernel(place, k_hbm, v_hbm, q_hbm, o0, o1, o2, o3, q_ref, k_all, v_all, q_all, sems):
+def pack_kernel(place, k_hbm, v_hbm, o1, o2, o3, k_all, v_all, sems):
     chip = place[0]
-    copies = [
-        pltpu.make_async_copy(src, dst, sems.at[n]) for n, (src, dst) in enumerate(((k_hbm, k_all), (v_hbm, v_all), (q_hbm, q_all)))
-    ]
+    copies = [pltpu.make_async_copy(src, dst, sems.at[n]) for n, (src, dst) in enumerate(((k_hbm, k_all), (v_hbm, v_all)))]
     for copy in copies:
         copy.start()
-    for n, copy in enumerate(copies):
+    for n, (copy, rows) in enumerate(zip(copies, (k_all, v_all))):
         copy.wait()
         for g in range(GROUPS):
+            for s, out in enumerate((o1, o2, o3), 1):
+
+                @pl.when(lax.bitwise_xor(chip, s) == g)
+                def _():
+                    out[n] = rows[:, g * GROUP_WIDTH : (g + 1) * GROUP_WIDTH]
+
+
+def own_kernel(place, k_ref, v_ref, q_ref, own_ref, q_own_ref):
+    for g in range(GROUPS):
+
+        @pl.when(place[0] == g)
+        def _():
             cols = slice(g * GROUP_WIDTH, (g + 1) * GROUP_WIDTH)
-            for s, out in enumerate((o0, o1, o2, o3)):
-                if n < 2:
-
-                    @pl.when(lax.bitwise_xor(chip, s) == g)
-                    def _():
-                        out[n] = (k_all, v_all)[n][:, cols]
-
-            if n == 2:
-
-                @pl.when(chip == g)
-                def _():
-                    q_ref[...] = q_all[:, cols]
+            own_ref[0] = k_ref[:, cols]
+            own_ref[1] = v_ref[:, cols]
+            q_own_ref[...] = q_ref[:, cols]
 
 
 def unpack_kernel(which, place, s0, s1, s2, s3, out_ref, rows, sem):
@@ -310,17 +311,20 @@
     pieces = pltpu.VMEM((PIECES, rows_each, q_len), F32)
 
     whole = pltpu.VMEM((kv_len, width), BF16)
-    *send, q_own = call(
+    send = call(
         "pack",
         pack_kernel,
-        3,
-        slots4 + [sds((q_len, GROUP_WIDTH), BF16)],
-        [whole, whole, pltpu.VMEM((q_len, width), BF16), pltpu.SemaphoreType.DMA((3,))],
-        in_blocks=[ANY] * 3,
+        2,
+        slots4[1:],
+        [whole, whole, pltpu.SemaphoreType.DMA((2,))],
+        in_blocks=[ANY] * 2,
         limit=60 * 1024 * 1024,
-    )(place, key_rows, value_rows, query)
+    )(place, key_rows, value_rows)
+    own, q_own = call("own", own_kernel, 3, [slots4[0], sds((q_len, GROUP_WIDTH), BF16)], limit=SMALL_LIMIT)(
+        place, key_rows, value_rows, query
+    )
     w_out, send = lax.optimization_barrier((w_out, send))
-    slots = [send[0]] + [swap_chip(send[s], s) for s in range(1, GROUPS)]
+    slots = [own] + [swap_chip(send[s - 1], s) for s in range(1, GROUPS)]
     d_own = lax.dot_general(w_out, cotangent, NN, preferred_element_type=F32).astype(BF16)
     both = jnp.stack([d_own, swap_half(d_own)])
     mine = [spread(both, j) for j in range(2)]

time: 108 us -> 107 us (level)
    pallas_call x1 -> x2, Pallas kernels: 4.18 us -> 4.32 us  [the longest x1 3.48 us: local(): call('pack', pack_kernel, 2, slots4[1:], [whole, whole, pltpu.SemaphoreTy...]
  transfers between devices with their start and end apart: 19 -> 19, of which waited for: 11 -> 10; matrix products, arithmetic and copies ran while one was open for 0% -> 0% of each run, Pallas kernels for 10% -> 11%
where the time goes in v5:
time: 107 us
  starting transfers between devices  50.3 us (47%)
  waiting for transfers between devices  29.3 us (27%)
  Pallas kernels  23 us (21%)
  local copies, waits for them, and re-layouts  2.06 us (2%)
    ppermute x5, starting transfers between devices, swap_half(): return lax.ppermute(x, 'core', [(0, 1), (1, 0)])  16.3 us
    ppermute x3, waiting for transfers between devices, swap_pair(): return lax.ppermute(x, 'zp', [(i, i ^ j) for i in range(GROUPS)])  13 us
    ppermute x6, waiting for transfers between devices, swap_chip(): return lax.ppermute(x, ('zl', 'x_lo'), [(i, i ^ s) for i in range(GROUPS)])  9.73 us
    ppermute x6, starting transfers between devices, swap_chip(): return lax.ppermute(x, ('zl', 'x_lo'), [(i, i ^ s) for i in range(GROUPS)])  7.68 us
    ppermute x3, starting transfers between devices, swap_pair(): return lax.ppermute(x, 'zp', [(i, i ^ j) for i in range(GROUPS)])  7.56 us
    ppermute x2, starting transfers between devices, spread(): return lax.ppermute(x, SEQ_AXES, pairs)  6.71 us
    ppermute x1, starting transfers between devices, trade(): lax.ppermute(x, ('zp', 'zl', 'x_lo'), [(a * GROUPS + b, b * GROUPS + a) f...  6.3 us
    pallas_call x2, Pallas kernels, unpack(): call(name, kernel, 4, out, [whole, pltpu.SemaphoreType.DMA], out_blocks=A...  4.8 us
  transfers between devices with their start and end apart: 19, of which 10 were waited for; matrix products, arithmetic and copies ran while one was open for 0% of the time, Pallas kernels for 11%

profile of v5, /device:TPU:6, one launch (start us, length us, event | category | flops | bytes accessed | tf_op | source)
XLA Modules:
  0.0 106.8 jit_solution(4671383895473123186)
XLA Ops:
  0.6 0.0 copy-start
  0.7 0.7 pad_add_fusion.place
  1.3 3.5 %pack.1 = (bf16[2,128,672]{2,1,0:T(8,128)(2,1)}, bf16[2,128,672]{2,1,0:T(8,128)(2,1)}, bf16[2,128,672]{2,1,0:T(8,128)(2,1)}) custom-call(s32[4]{0:T(128)} %pad_add_fusion.place, bf16[128,2688]{1,0:T(8,128)(2,1)} %bitcast.23, bf16[128,2688]{1,0:T(8,128)(2,1)} %bitcast.25), custom_call_target="tpu_custom_call" | custom-call | flops 1000000000 | tf_op jit(solution)/shard_map/pack/pallas_call | solution.py:314
  4.8 0.0 copy-start.12
  4.9 0.0 copy-start.4
  4.9 0.0 copy-start.5
  4.9 0.0 copy-start.6
  4.9 0.6 fusion.2
  5.5 0.1 collective-permute-start.3
  5.6 1.1 %collective-permute-start = (bf16[2,128,672]{2,1,0:T(8,128)(2,1)}, bf16[2,128,672]{2,1,0:T(8,128)(2,1)S(1)}, u32[]{:S(2)}, u32[]{:S(2)}) collective-permute-start(bf16[2,128,672]{2,1,0:T(8,128)(2,1)} %get-tuple-element.50), channel_id=1, source_target_pairs={{0,2},{2,0},{4,6},{6,4},{1,3},{3,1},{5,7},{7,5},{8,10},{10,8},{12,... | collective-permute-start | bytes 1032200 | tf_op jit(solution)/shard_map/ppermute | solution.py:276
  6.7 1.7 %collective-permute-start.1 = (bf16[2,128,672]{2,1,0:T(8,128)(2,1)S(1)}, bf16[2,128,672]{2,1,0:T(8,128)(2,1)S(1)}, u32[]{:S(2)}, u32[]{:S(2)}) collective-permute-start(bf16[2,128,672]{2,1,0:T(8,128)(2,1)S(1)} %copy-done.12), channel_id=1, source_target_pairs={{0,4},{2,6},{4,0},{6,2},{1,5},{3,7},{5,1},{7,3},{8,12},{10,14},{12... | collective-permute-start | bytes 1032200 | tf_op jit(solution)/shard_map/ppermute | solution.py:276
  8.4 0.8 collective-permute-start.2
  9.2 1.1 %collective-permute-start.5 = (bf16[2,84,256]{2,1,0:T(8,128)(2,1)S(1)}, bf16[2,84,256]{2,1,0:T(8,128)(2,1)S(1)}, u32[]{:S(2)}, u32[]{:S(2)}) collective-permute-start(bf16[2,84,256]{2,1,0:T(8,128)(2,1)S(1)} %pad_maximum_fusion), channel_id=1, source_target_pairs={{0,8},{1,25},{2,0},{3,17},{4,24},{5,9},{6,16},{7,1},{8,10},{9,27},... | collective-permute-start | bytes 258056 | tf_op jit(solution)/shard_map/ppermute | solution.py:296
  10.3 5.6 %collective-permute-start.4 = (bf16[2,84,256]{2,1,0:T(8,128)(2,1)S(1)}, bf16[2,84,256]{2,1,0:T(8,128)(2,1)S(1)}, u32[]{:S(2)}, u32[]{:S(2)}) collective-permute-start(bf16[2,84,256]{2,1,0:T(8,128)(2,1)S(1)} %pad_maximum_fusion), channel_id=1, source_target_pairs={{0,0},{1,17},{2,8},{3,25},{4,16},{5,1},{6,24},{7,9},{8,2},{9,19},{... | collective-permute-start | bytes 258056 | tf_op jit(solution)/shard_map/ppermute | solution.py:296
  15.9 0.9 collective-permute-done.5.m1
  16.8 14.7 %collective-permute-start.7 = (bf16[2,84,256]{2,1,0:T(8,128)(2,1)S(1)}, bf16[2,84,256]{2,1,0:T(8,128)(2,1)S(1)}, u32[]{:S(2)}, u32[]{:S(2)}) collective-permute-start(bf16[2,84,256]{2,1,0:T(8,128)(2,1)S(1)} %collective-permute-done.5.m1), channel_id=1, source_target_pairs={{0,1},{1,0},{2,3},{3,2},{4,5},{5,4},{6,7},{7,6},{8,9},{9,8},{10,11... | collective-permute-start | bytes 258056 | tf_op jit(solution)/shard_map/ppermute | solution.py:284
  31.5 0.8 collective-permute-start.6
  32.3 0.8 own.1
  33.2 0.1 collective-permute-done.6.t0
  33.3 0.6 join.1.d_ref
  34.0 4.5 %forward.1 = (f32[12,84,256]{2,1,0:T(8,128)S(1)}, bf16[12,84,256]{2,1,0:T(8,128)(2,1)S(1)}, f32[3,8,256]{2,1,0:T(8,128)S(1)}) custom-call(s32[4]{0:T(128)S(1)} %copy-done.3, s32[1,256]{1,0:T(1,128)S(1)} %bitcast.27, bf16[256,672]{1,0:T(8,128)(2,1)S(1)} %get-tuple-element.45.q_ref, bf16[2,128,672]{2,1,0:T(8,128)(2,1)S(1)} %get-tuple-element.46.s0, ...), custom_call_target="tpu_custom_call" | custom-call | flops 2000000000 | tf_op jit(solution)/shard_map/forward/pallas_call | solution.py:334
  38.5 0.4 collective-permute-start.8
  38.9 0.3 collective-permute-start.9
  39.2 1.3 %collective-permute-done.9.got_stats_ref = f32[3,8,256]{2,1,0:T(8,128)S(1)} collective-permute-done((f32[3,8,256]{2,1,0:T(8,128)S(1)}, f32[3,8,256]{2,1,0:T(8,128)S(1)}, u32[]{:S(2)}, u32[]{:S(2)}) %collective-permute-start.9) | collective-permute-done | bytes 24608 | tf_op jit(solution)/shard_map/ppermute | solution.py:284
  40.5 1.0 core.1
  41.5 1.5 %collective-permute-start.10 = (bf16[304,256]{1,0:T(8,128)(2,1)S(1)}, bf16[304,256]{1,0:T(8,128)(2,1)S(1)}, u32[]{:S(2)}, u32[]{:S(2)}) collective-permute-start(bf16[304,256]{1,0:T(8,128)(2,1)S(1)} %get-tuple-element.58), channel_id=1, source_target_pairs={{0,8},{8,0},{16,24},{24,16},{1,9},{9,1},{17,25},{25,17},{2,10},{10... | collective-permute-start | bytes 466952 | tf_op jit(solution)/shard_map/ppermute | solution.py:280
  43.0 6.1 %collective-permute-start.11 = (bf16[304,256]{1,0:T(8,128)(2,1)S(1)}, bf16[304,256]{1,0:T(8,128)(2,1)S(1)}, u32[]{:S(2)}, u32[]{:S(2)}) collective-permute-start(bf16[304,256]{1,0:T(8,128)(2,1)S(1)} %get-tuple-element.59), channel_id=1, source_target_pairs={{0,16},{8,24},{16,0},{24,8},{1,17},{9,25},{17,1},{25,9},{2,18},{10... | collective-permute-start | bytes 466952 | tf_op jit(solution)/shard_map/ppermute | solution.py:280
  49.1 11.0 %collective-permute-done.11.p2 = bf16[304,256]{1,0:T(8,128)(2,1)S(1)} collective-permute-done((bf16[304,256]{1,0:T(8,128)(2,1)S(1)}, bf16[304,256]{1,0:T(8,128)(2,1)S(1)}, u32[]{:S(2)}, u32[]{:S(2)}) %collective-permute-start.11) | collective-permute-done | bytes 155680 | tf_op jit(solution)/shard_map/ppermute | solution.py:280
  60.1 2.0 %collective-permute-done.12.p3 = bf16[304,256]{1,0:T(8,128)(2,1)S(1)} collective-permute-done((bf16[304,256]{1,0:T(8,128)(2,1)S(1)}, bf16[304,256]{1,0:T(8,128)(2,1)S(1)}, u32[]{:S(2)}, u32[]{:S(2)}) %collective-permute-start.12) | collective-permute-done | bytes 155680 | tf_op jit(solution)/shard_map/ppermute | solution.py:280
  62.1 0.7 finish.1
  62.8 6.3 %collective-permute-start.13 = (bf16[2,84,256]{2,1,0:T(8,128)(2,1)S(1)}, bf16[2,84,256]{2,1,0:T(8,128)(2,1)S(1)}, u32[]{:S(2)}, u32[]{:S(2)}) collective-permute-start(bf16[2,84,256]{2,1,0:T(8,128)(2,1)S(1)} %finish.1), channel_id=1, source_target_pairs={{0,0},{2,8},{4,16},{6,24},{8,2},{10,10},{12,18},{14,26},{16,4},{18... | collective-permute-start | bytes 258056 | tf_op jit(solution)/shard_map/ppermute | solution.py:291
  69.2 4.1 %backward.1 = (bf16[2,128,672]{2,1,0:T(8,128)(2,1)S(1)}, bf16[2,128,672]{2,1,0:T(8,128)(2,1)}, bf16[2,128,672]{2,1,0:T(8,128)(2,1)}, bf16[2,128,672]{2,1,0:T(8,128)(2,1)}) custom-call(s32[4]{0:T(128)S(1)} %copy-done.3, s32[1,256]{1,0:T(1,128)S(1)} %bitcast.28, bf16[256,672]{1,0:T(8,128)(2,1)S(1)} %get-tuple-element.45.q_ref, ...), custom_call_target="tpu_custom_call" | custom-call | flops 3000000000 | tf_op jit(solution)/shard_map/backward/pallas_call | solution.py:354
  73.2 0.1 collective-permute-done.13.rows_ref
  73.4 2.6 %collective-permute-start.15 = (bf16[2,128,672]{2,1,0:T(8,128)(2,1)}, bf16[2,128,672]{2,1,0:T(8,128)(2,1)}, u32[]{:S(2)}, u32[]{:S(2)}) collective-permute-start(bf16[2,128,672]{2,1,0:T(8,128)(2,1)} %get-tuple-element.75), channel_id=1, source_target_pairs={{0,4},{2,6},{4,0},{6,2},{1,5},{3,7},{5,1},{7,3},{8,12},{10,14},{12... | collective-permute-start | bytes 1032200 | tf_op jit(solution)/shard_map/ppermute | solution.py:276
  76.0 1.5 %collective-permute-start.16 = (bf16[2,128,672]{2,1,0:T(8,128)(2,1)}, bf16[2,128,672]{2,1,0:T(8,128)(2,1)}, u32[]{:S(2)}, u32[]{:S(2)}) collective-permute-start(bf16[2,128,672]{2,1,0:T(8,128)(2,1)} %get-tuple-element.76), channel_id=1, source_target_pairs={{0,6},{2,4},{4,2},{6,0},{1,7},{3,5},{5,3},{7,1},{8,14},{10,12},{12... | collective-permute-start | bytes 1032200 | tf_op jit(solution)/shard_map/ppermute | solution.py:276
  77.5 1.6 %weight.1 = (bf16[8,84,660]{2,1,0:T(8,128)(2,1)S(1)}, bf16[84,256]{1,0:T(8,128)(2,1)}) custom-call(bf16[2,84,256]{2,1,0:T(8,128)(2,1)S(1)} %collective-permute-done.13.rows_ref, bf16[5280,256]{1,0:T(8,128)(2,1)S(1)} %bitcast.21), custom_call_target="tpu_custom_call" | custom-call | flops 2000000000 | tf_op jit(solution)/shard_map/weight/pallas_call | solution.py:361
  79.1 1.0 copy-done.2
  80.1 4.6 %all-to-all-start = ((bf16[8,84,660]{2,1,0:T(8,128)(2,1)}), bf16[8,84,660]{2,1,0:T(8,128)(2,1)S(1)}, u32[]{:S(2)}, u32[]{:S(2)}) async-start(bf16[8,84,660]{2,1,0:T(8,128)(2,1)} %copy-done.2), calls=%async_computation | async-start | bytes 2162688 | tf_op jit(solution)/shard_map/all_to_all | solution.py:370
  84.6 1.7 %collective-permute-done.15.s2 = bf16[2,128,672]{2,1,0:T(8,128)(2,1)} collective-permute-done((bf16[2,128,672]{2,1,0:T(8,128)(2,1)}, bf16[2,128,672]{2,1,0:T(8,128)(2,1)}, u32[]{:S(2)}, u32[]{:S(2)}) %collective-permute-start.15) | collective-permute-done | bytes 344096 | tf_op jit(solution)/shard_map/ppermute | solution.py:276
  86.3 8.0 %collective-permute-done.16.s3 = bf16[2,128,672]{2,1,0:T(8,128)(2,1)} collective-permute-done((bf16[2,128,672]{2,1,0:T(8,128)(2,1)}, bf16[2,128,672]{2,1,0:T(8,128)(2,1)}, u32[]{:S(2)}, u32[]{:S(2)}) %collective-permute-start.16) | collective-permute-done | bytes 344096 | tf_op jit(solution)/shard_map/ppermute | solution.py:276
  94.4 1.0 copy-done.9
  95.4 2.4 %unpack_k.1 = bf16[128,2688]{1,0:T(8,128)(2,1)} custom-call(s32[4]{0:T(128)S(1)} %copy-done.3, bf16[2,128,672]{2,1,0:T(8,128)(2,1)S(1)} %copy-done.9, bf16[2,128,672]{2,1,0:T(8,128)(2,1)S(1)} %collective-permute-done.14.s1, bf16[2,128,672]{2,1,0:T(8,128)(2,1)} %collective-permute-done.15.s2, bf16[2,128,672]{2,1,0:T(8,128)(2,1)} %collective-permute-done.16.s3), custom_call_target="tpu_custom_call" | custom-call | flops 10000000000 | tf_op jit(solution)/shard_map/unpack_k/pallas_call | solution.py:375
  97.8 1.1 %all-to-all-done.x_ref = bf16[8,84,660]{2,1,0:T(8,128)(2,1)S(1)} async-done(((bf16[8,84,660]{2,1,0:T(8,128)(2,1)}), bf16[8,84,660]{2,1,0:T(8,128)(2,1)S(1)}, u32[]{:S(2)}, u32[]{:S(2)}) %all-to-all-start) | async-done | bytes 887072 | tf_op jit(solution)/shard_map/all_to_all | solution.py:370
  98.9 0.7 sum_y.1
  99.5 1.2 %collective-permute-start.17 = (bf16[84,660]{1,0:T(8,128)(2,1)S(1)}, bf16[84,660]{1,0:T(8,128)(2,1)S(1)}, u32[]{:S(2)}, u32[]{:S(2)}) collective-permute-start(bf16[84,660]{1,0:T(8,128)(2,1)S(1)} %get-tuple-element.85), channel_id=1, source_target_pairs={{0,128},{128,0},{1,129},{129,1},{2,130},{130,2},{3,131},{131,3},{4... | collective-permute-start | bytes 332648 | tf_op jit(solution)/shard_map/ppermute | solution.py:382
  100.8 2.4 %unpack_v.1 = bf16[128,2688]{1,0:T(8,128)(2,1)} custom-call(s32[4]{0:T(128)S(1)} %copy-done.3, bf16[2,128,672]{2,1,0:T(8,128)(2,1)S(1)} %copy-done.10, bf16[2,128,672]{2,1,0:T(8,128)(2,1)S(1)} %collective-permute-done.14.s1, bf16[2,128,672]{2,1,0:T(8,128)(2,1)} %collective-permute-done.15.s2, bf16[2,128,672]{2,1,0:T(8,128)(2,1)} %collective-permute-done.16.s3), custom_call_target="tpu_custom_call" | custom-call | flops 3000000000 | tf_op jit(solution)/shard_map/unpack_v/pallas_call | solution.py:375
  103.2 3.0 %collective-permute-done.17.got_ref = bf16[84,660]{1,0:T(8,128)(2,1)S(1)} collective-permute-done((bf16[84,660]{1,0:T(8,128)(2,1)S(1)}, bf16[84,660]{1,0:T(8,128)(2,1)S(1)}, u32[]{:S(2)}, u32[]{:S(2)}) %collective-permute-start.17) | collective-permute-done | bytes 110912 | tf_op jit(solution)/shard_map/ppermute | solution.py:382
  106.2 0.7 sum.1
  (31 shorter events, 0.1 us)
Async XLA Ops:
  0.6 4.3 %copy-start = (bf16[84,5280]{1,0:T(8,128)(2,1)S(1)}, bf16[84,5280]{1,0:T(8,128)(2,1)}, u32[]{:S(2)}) copy-start(bf16[84,5280]{1,0:T(8,128)(2,1)} %param.10) | copy-start | bytes 2661124
  0.7 4.3 %copy-start.1 = (bf16[1,256,5280]{1,2,0:T(8,128)(2,1)S(1)}, bf16[1,256,5280]{1,2,0:T(8,128)(2,1)}, u32[]{:S(2)}) copy-start(bf16[1,256,5280]{1,2,0:T(8,128)(2,1)} %param.9) | copy-start | bytes 8110084
  4.8 1.9 %copy-start.12 = (bf16[2,128,672]{2,1,0:T(8,128)(2,1)S(1)}, bf16[2,128,672]{2,1,0:T(8,128)(2,1)}, u32[]{:S(2)}) copy-start(bf16[2,128,672]{2,1,0:T(8,128)(2,1)} %get-tuple-element.51) | copy-start | bytes 1032196
  4.8 3.6 %copy-start.11 = (bf16[2,128,672]{2,1,0:T(8,128)(2,1)S(1)}, bf16[2,128,672]{2,1,0:T(8,128)(2,1)}, u32[]{:S(2)}) copy-start(bf16[2,128,672]{2,1,0:T(8,128)(2,1)} %get-tuple-element.52) | copy-start | bytes 1032196
  4.8 27.5 %copy-start.3 = (s32[4]{0:T(128)S(1)}, s32[4]{0:T(128)}, u32[]{:S(2)}) copy-start(s32[4]{0:T(128)} %pad_add_fusion.place) | copy-start | bytes 52
  4.9 27.5 %copy-start.4 = (bf16[1,256,2688]{2,1,0:T(8,128)(2,1)S(1)}, bf16[1,256,2688]{2,1,0:T(8,128)(2,1)}, u32[]{:S(2)}) copy-start(bf16[1,256,2688]{2,1,0:T(8,128)(2,1)} %param.6) | copy-start | bytes 4128772
  4.9 27.5 %copy-start.5 = (bf16[1,128,2688]{2,1,0:T(8,128)(2,1)S(1)}, bf16[1,128,2688]{2,1,0:T(8,128)(2,1)}, u32[]{:S(2)}) copy-start(bf16[1,128,2688]{2,1,0:T(8,128)(2,1)} %param.7) | copy-start | bytes 2064388
  4.9 27.5 %copy-start.6 = (bf16[1,128,2688]{2,1,0:T(8,128)(2,1)S(1)}, bf16[1,128,2688]{2,1,0:T(8,128)(2,1)}, u32[]{:S(2)}) copy-start(bf16[1,128,2688]{2,1,0:T(8,128)(2,1)} %param.8) | copy-start | bytes 2064388
  5.5 3.7 %collective-permute-start.3 = (bf16[84,256]{1,0:T(8,128)(2,1)S(1)}, bf16[84,256]{1,0:T(8,128)(2,1)S(1)}, u32[]{:S(2)}, u32[]{:S(2)}) collective-permute-start(bf16[84,256]{1,0:T(8,128)(2,1)S(1)} %fusion.2), channel_id=1, source_target_pairs={{0,1},{1,0},{2,3},{3,2},{4,5},{5,4},{6,7},{7,6},{8,9},{9,8},{10,11... | collective-permute-start | bytes 129032 | tf_op jit(solution)/shard_map/ppermute | solution.py:284
  5.6 28.3 %collective-permute-start = (bf16[2,128,672]{2,1,0:T(8,128)(2,1)}, bf16[2,128,672]{2,1,0:T(8,128)(2,1)S(1)}, u32[]{:S(2)}, u32[]{:S(2)}) collective-permute-start(bf16[2,128,672]{2,1,0:T(8,128)(2,1)} %get-tuple-element.50), channel_id=1, source_target_pairs={{0,2},{2,0},{4,6},{6,4},{1,3},{3,1},{5,7},{7,5},{8,10},{10,8},{12,... | collective-permute-start | bytes 1032200 | tf_op jit(solution)/shard_map/ppermute | solution.py:276
  6.7 27.2 %collective-permute-start.1 = (bf16[2,128,672]{2,1,0:T(8,128)(2,1)S(1)}, bf16[2,128,672]{2,1,0:T(8,128)(2,1)S(1)}, u32[]{:S(2)}, u32[]{:S(2)}) collective-permute-start(bf16[2,128,672]{2,1,0:T(8,128)(2,1)S(1)} %copy-done.12), channel_id=1, source_target_pairs={{0,4},{2,6},{4,0},{6,2},{1,5},{3,7},{5,1},{7,3},{8,12},{10,14},{12... | collective-permute-start | bytes 1032200 | tf_op jit(solution)/shard_map/ppermute | solution.py:276
  8.4 25.5 %collective-permute-start.2 = (bf16[2,128,672]{2,1,0:T(8,128)(2,1)S(1)}, bf16[2,128,672]{2,1,0:T(8,128)(2,1)S(1)}, u32[]{:S(2)}, u32[]{:S(2)}) collective-permute-start(bf16[2,128,672]{2,1,0:T(8,128)(2,1)S(1)} %copy-done.11), channel_id=1, source_target_pairs={{0,6},{2,4},{4,2},{6,0},{1,7},{3,5},{5,3},{7,1},{8,14},{10,12},{12... | collective-permute-start | bytes 1032200 | tf_op jit(solution)/shard_map/ppermute | solution.py:276
  9.2 7.6 %collective-permute-start.5 = (bf16[2,84,256]{2,1,0:T(8,128)(2,1)S(1)}, bf16[2,84,256]{2,1,0:T(8,128)(2,1)S(1)}, u32[]{:S(2)}, u32[]{:S(2)}) collective-permute-start(bf16[2,84,256]{2,1,0:T(8,128)(2,1)S(1)} %pad_maximum_fusion), channel_id=1, source_target_pairs={{0,8},{1,25},{2,0},{3,17},{4,24},{5,9},{6,16},{7,1},{8,10},{9,27},... | collective-permute-start | bytes 258056 | tf_op jit(solution)/shard_map/ppermute | solution.py:296
  10.3 21.2 %collective-permute-start.4 = (bf16[2,84,256]{2,1,0:T(8,128)(2,1)S(1)}, bf16[2,84,256]{2,1,0:T(8,128)(2,1)S(1)}, u32[]{:S(2)}, u32[]{:S(2)}) collective-permute-start(bf16[2,84,256]{2,1,0:T(8,128)(2,1)S(1)} %pad_maximum_fusion), channel_id=1, source_target_pairs={{0,0},{1,17},{2,8},{3,25},{4,16},{5,1},{6,24},{7,9},{8,2},{9,19},{... | collective-permute-start | bytes 258056 | tf_op jit(solution)/shard_map/ppermute | solution.py:296
  16.8 16.4 %collective-permute-start.7 = (bf16[2,84,256]{2,1,0:T(8,128)(2,1)S(1)}, bf16[2,84,256]{2,1,0:T(8,128)(2,1)S(1)}, u32[]{:S(2)}, u32[]{:S(2)}) collective-permute-start(bf16[2,84,256]{2,1,0:T(8,128)(2,1)S(1)} %collective-permute-done.5.m1), channel_id=1, source_target_pairs={{0,1},{1,0},{2,3},{3,2},{4,5},{5,4},{6,7},{7,6},{8,9},{9,8},{10,11... | collective-permute-start | bytes 258056 | tf_op jit(solution)/shard_map/ppermute | solution.py:284
  31.5 1.7 %collective-permute-start.6 = (bf16[2,84,256]{2,1,0:T(8,128)(2,1)S(1)}, bf16[2,84,256]{2,1,0:T(8,128)(2,1)S(1)}, u32[]{:S(2)}, u32[]{:S(2)}) collective-permute-start(bf16[2,84,256]{2,1,0:T(8,128)(2,1)S(1)} %collective-permute-done.4.m0), channel_id=1, source_target_pairs={{0,1},{1,0},{2,3},{3,2},{4,5},{5,4},{6,7},{7,6},{8,9},{9,8},{10,11... | collective-permute-start | bytes 258056 | tf_op jit(solution)/shard_map/ppermute | solution.py:284
  33.2 0.8 copy-start.7
  38.5 2.1 %collective-permute-start.8 = (bf16[12,84,256]{2,1,0:T(8,128)(2,1)S(1)}, bf16[12,84,256]{2,1,0:T(8,128)(2,1)S(1)}, u32[]{:S(2)}, u32[]{:S(2)}) collective-permute-start(bf16[12,84,256]{2,1,0:T(8,128)(2,1)S(1)} %get-tuple-element.56), channel_id=1, source_target_pairs={{0,1},{1,0},{2,3},{3,2},{4,5},{5,4},{6,7},{7,6},{8,9},{9,8},{10,11... | collective-permute-start | bytes 1548296 | tf_op jit(solution)/shard_map/ppermute | solution.py:284
  38.9 1.6 %collective-permute-start.9 = (f32[3,8,256]{2,1,0:T(8,128)S(1)}, f32[3,8,256]{2,1,0:T(8,128)S(1)}, u32[]{:S(2)}, u32[]{:S(2)}) collective-permute-start(f32[3,8,256]{2,1,0:T(8,128)S(1)} %get-tuple-element.55.stats_ref), channel_id=1, source_target_pairs={{0,1},{1,0},{2,3},{3,2},{4,5},{5,4},{6,7},{7,6},{8,9},{9,8},{10,11... | collective-permute-start | bytes 73736 | tf_op jit(solution)/shard_map/ppermute | solution.py:284
  41.5 7.6 %collective-permute-start.10 = (bf16[304,256]{1,0:T(8,128)(2,1)S(1)}, bf16[304,256]{1,0:T(8,128)(2,1)S(1)}, u32[]{:S(2)}, u32[]{:S(2)}) collective-permute-start(bf16[304,256]{1,0:T(8,128)(2,1)S(1)} %get-tuple-element.58), channel_id=1, source_target_pairs={{0,8},{8,0},{16,24},{24,16},{1,9},{9,1},{17,25},{25,17},{2,10},{10... | collective-permute-start | bytes 466952 | tf_op jit(solution)/shard_map/ppermute | solution.py:280
  43.0 17.1 %collective-permute-start.11 = (bf16[304,256]{1,0:T(8,128)(2,1)S(1)}, bf16[304,256]{1,0:T(8,128)(2,1)S(1)}, u32[]{:S(2)}, u32[]{:S(2)}) collective-permute-start(bf16[304,256]{1,0:T(8,128)(2,1)S(1)} %get-tuple-element.59), channel_id=1, source_target_pairs={{0,16},{8,24},{16,0},{24,8},{1,17},{9,25},{17,1},{25,9},{2,18},{10... | collective-permute-start | bytes 466952 | tf_op jit(solution)/shard_map/ppermute | solution.py:280
  49.1 13.0 %collective-permute-start.12 = (bf16[304,256]{1,0:T(8,128)(2,1)S(1)}, bf16[304,256]{1,0:T(8,128)(2,1)S(1)}, u32[]{:S(2)}, u32[]{:S(2)}) collective-permute-start(bf16[304,256]{1,0:T(8,128)(2,1)S(1)} %get-tuple-element.60), channel_id=1, source_target_pairs={{0,24},{8,16},{16,8},{24,0},{1,25},{9,17},{17,9},{25,1},{2,26},{10... | collective-permute-start | bytes 466952 | tf_op jit(solution)/shard_map/ppermute | solution.py:280
  62.8 10.5 %collective-permute-start.13 = (bf16[2,84,256]{2,1,0:T(8,128)(2,1)S(1)}, bf16[2,84,256]{2,1,0:T(8,128)(2,1)S(1)}, u32[]{:S(2)}, u32[]{:S(2)}) collective-permute-start(bf16[2,84,256]{2,1,0:T(8,128)(2,1)S(1)} %finish.1), channel_id=1, source_target_pairs={{0,0},{2,8},{4,16},{6,24},{8,2},{10,10},{12,18},{14,26},{16,4},{18... | collective-permute-start | bytes 258056 | tf_op jit(solution)/shard_map/ppermute | solution.py:291
  73.2 5.8 %copy-start.8 = (bf16[2,128,672]{2,1,0:T(8,128)(2,1)}, bf16[2,128,672]{2,1,0:T(8,128)(2,1)S(1)}, u32[]{:S(2)}) copy-start(bf16[2,128,672]{2,1,0:T(8,128)(2,1)S(1)} %get-tuple-element.80.s0) | copy-start | bytes 1032196
  73.4 11.3 %collective-permute-start.14 = (bf16[2,128,672]{2,1,0:T(8,128)(2,1)}, bf16[2,128,672]{2,1,0:T(8,128)(2,1)S(1)}, u32[]{:S(2)}, u32[]{:S(2)}) collective-permute-start(bf16[2,128,672]{2,1,0:T(8,128)(2,1)} %get-tuple-element.74), channel_id=1, source_target_pairs={{0,2},{2,0},{4,6},{6,4},{1,3},{3,1},{5,7},{7,5},{8,10},{10,8},{12,... | collective-permute-start | bytes 1032200 | tf_op jit(solution)/shard_map/ppermute | solution.py:276
  73.4 13.0 %collective-permute-start.15 = (bf16[2,128,672]{2,1,0:T(8,128)(2,1)}, bf16[2,128,672]{2,1,0:T(8,128)(2,1)}, u32[]{:S(2)}, u32[]{:S(2)}) collective-permute-start(bf16[2,128,672]{2,1,0:T(8,128)(2,1)} %get-tuple-element.75), channel_id=1, source_target_pairs={{0,4},{2,6},{4,0},{6,2},{1,5},{3,7},{5,1},{7,3},{8,12},{10,14},{12... | collective-permute-start | bytes 1032200 | tf_op jit(solution)/shard_map/ppermute | solution.py:276
  76.0 18.4 %collective-permute-start.16 = (bf16[2,128,672]{2,1,0:T(8,128)(2,1)}, bf16[2,128,672]{2,1,0:T(8,128)(2,1)}, u32[]{:S(2)}, u32[]{:S(2)}) collective-permute-start(bf16[2,128,672]{2,1,0:T(8,128)(2,1)} %get-tuple-element.76), channel_id=1, source_target_pairs={{0,6},{2,4},{4,2},{6,0},{1,7},{3,5},{5,3},{7,1},{8,14},{10,12},{12... | collective-permute-start | bytes 1032200 | tf_op jit(solution)/shard_map/ppermute | solution.py:276
  79.1 1.0 copy-start.2
  80.1 20.7 %copy-start.10 = (bf16[2,128,672]{2,1,0:T(8,128)(2,1)S(1)}, bf16[2,128,672]{2,1,0:T(8,128)(2,1)}, u32[]{:S(2)}) copy-start(bf16[2,128,672]{2,1,0:T(8,128)(2,1)} %copy-done.8) | copy-start | bytes 1032196
  80.1 18.8 %all-to-all-start = ((bf16[8,84,660]{2,1,0:T(8,128)(2,1)}), bf16[8,84,660]{2,1,0:T(8,128)(2,1)S(1)}, u32[]{:S(2)}, u32[]{:S(2)}) async-start(bf16[8,84,660]{2,1,0:T(8,128)(2,1)} %copy-done.2), calls=%async_computation | async-start | bytes 2162688 | tf_op jit(solution)/shard_map/all_to_all | solution.py:370
  94.4 1.0 copy-start.9
  99.5 6.6 %collective-permute-start.17 = (bf16[84,660]{1,0:T(8,128)(2,1)S(1)}, bf16[84,660]{1,0:T(8,128)(2,1)S(1)}, u32[]{:S(2)}, u32[]{:S(2)}) collective-permute-start(bf16[84,660]{1,0:T(8,128)(2,1)S(1)} %get-tuple-element.85), channel_id=1, source_target_pairs={{0,128},{128,0},{1,129},{129,1},{2,130},{130,2},{3,131},{131,3},{4... | collective-permute-start | bytes 332648 | tf_op jit(solution)/shard_map/ppermute | solution.py:382

commit v6 on v5

--- a/solution.py
+++ b/solution.py
@@ -34,8 +34,8 @@
     return lax.dot_general(a, b, dims, preferred_element_type=F32)
 
 
-def pack_kernel(place, k_hbm, v_hbm, o1, o2, o3, k_all, v_all, sems):
-    chip = place[0]
+def pack_kernel(k_hbm, v_hbm, o1, o2, o3, k_all, v_all, sems):
+    chip = 2 * lax.axis_index("zl") + lax.axis_index("x_lo")
     copies = [pltpu.make_async_copy(src, dst, sems.at[n]) for n, (src, dst) in enumerate(((k_hbm, k_all), (v_hbm, v_all)))]
     for copy in copies:
         copy.start()
@@ -60,17 +60,21 @@
             q_own_ref[...] = q_ref[:, cols]
 
 
-def unpack_kernel(which, place, s0, s1, s2, s3, out_ref, rows, sem):
+def unpack_kernel(which, place, s0, s1, s2, s3, out_ref, parts, rows, sems):
     chip = place[0]
-    for g in range(GROUPS):
-        cols = slice(g * GROUP_WIDTH, (g + 1) * GROUP_WIDTH)
-        for s, slot in enumerate((s0, s1, s2, s3)):
+    slots = (s0, s1, s2, s3)
+    copies = [pltpu.make_async_copy(slot.at[which], parts.at[s], sems.at[s]) for s, slot in enumerate(slots)]
+    for copy in copies:
+        copy.start()
+    for s, copy in enumerate(copies):
+        copy.wait()
+        for g in range(GROUPS):
 
             @pl.when(lax.bitwise_xor(chip, s) == g)
             def _():
-                rows[:, cols] = slot[which]
-
-    copy = pltpu.make_async_copy(rows, out_ref, sem)
+                rows[:, g * GROUP_WIDTH : (g + 1) * GROUP_WIDTH] = parts[s]
+
+    copy = pltpu.make_async_copy(rows, out_ref, sems.at[GROUPS])
     copy.start()
     copy.wait()
 
@@ -318,8 +322,9 @@
         slots4[1:],
         [whole, whole, pltpu.SemaphoreType.DMA((2,))],
         in_blocks=[ANY] * 2,
+        scalars=0,
         limit=60 * 1024 * 1024,
-    )(place, key_rows, value_rows)
+    )(key_rows, value_rows)
     own, q_own = call("own", own_kernel, 3, [slots4[0], sds((q_len, GROUP_WIDTH), BF16)], limit=SMALL_LIMIT)(
         place, key_rows, value_rows, query
     )
@@ -372,7 +377,8 @@
     def unpack(which, name, back):
         kernel = functools.partial(unpack_kernel, which)
         out = sds((kv_len, width), BF16)
-        return call(name, kernel, 4, out, [whole, pltpu.SemaphoreType.DMA], out_blocks=ANY, limit=SMALL_LIMIT)(place, *back)
+        scratch = [pltpu.VMEM((GROUPS, kv_len, GROUP_WIDTH), BF16), whole, pltpu.SemaphoreType.DMA((GROUPS + 1,))]
+        return call(name, kernel, 4, out, scratch, in_blocks=[ANY] * 4, out_blocks=ANY, limit=SMALL_LIMIT)(place, *back)
 
     grad_k = unpack(0, "unpack_k", back)
     gw, grad_k = lax.optimization_barrier((gw, grad_k))

time: 107 us -> 110 us (1.028)
  local copies, waits for them, and re-layouts: 2.06 us -> 5.56 us
  waiting for transfers between devices: 29.3 us -> 27.3 us
  Pallas kernels: 23 us -> 24.4 us
    unnamed x26 -> x22, local copies, waits for them, and re-layouts: 2.06 us -> 5.56 us
    ppermute x1, waiting for transfers between devices: 2.99 us -> 1.16 us  [local(): half = lax.ppermute(half, 'x_hi', [(0, 1), (1, 0)])]
    pallas_call x2, Pallas kernels: 4.8 us -> 6.47 us  [unpack(): call(name, kernel, 4, out, scratch, in_blocks=[ANY] * 4, out_blocks=ANY,...]
  transfers between devices with their start and end apart: 19 -> 19, of which waited for: 10 -> 8; matrix products, arithmetic and copies ran while one was open for 0% -> 0% of each run, Pallas kernels for 11% -> 13%
where the time goes in v6:
time: 110 us; the launch traced here: 109 us
  starting transfers between devices  50.2 us (46%)
  waiting for transfers between devices  27.3 us (25%)
  Pallas kernels  24.4 us (22%)
  local copies, waits for them, and re-layouts  5.56 us (5%)
    ppermute x5, starting transfers between devices, swap_half(): return lax.ppermute(x, 'core', [(0, 1), (1, 0)])  16.4 us
    ppermute x3, waiting for transfers between devices, swap_pair(): return lax.ppermute(x, 'zp', [(i, i ^ j) for i in range(GROUPS)])  13 us
    ppermute x6, waiting for transfers between devices, swap_chip(): return lax.ppermute(x, ('zl', 'x_lo'), [(i, i ^ s) for i in range(GROUPS)])  10.4 us
    ppermute x6, starting transfers between devices, swap_chip(): return lax.ppermute(x, ('zl', 'x_lo'), [(i, i ^ s) for i in range(GROUPS)])  7.78 us
    ppermute x3, starting transfers between devices, swap_pair(): return lax.ppermute(x, 'zp', [(i, i ^ j) for i in range(GROUPS)])  7.55 us
    ppermute x2, starting transfers between devices, spread(): return lax.ppermute(x, SEQ_AXES, pairs)  6.7 us
    pallas_call x2, Pallas kernels, unpack(): call(name, kernel, 4, out, scratch, in_blocks=[ANY] * 4, out_blocks=ANY,...  6.47 us
    ppermute x1, starting transfers between devices, trade(): lax.ppermute(x, ('zp', 'zl', 'x_lo'), [(a * GROUPS + b, b * GROUPS + a) f...  6.15 us
  transfers between devices with their start and end apart: 19, of which 8 were waited for; matrix products, arithmetic and copies ran while one was open for 0% of the time, Pallas kernels for 13%

profile of v6, /device:TPU:6, one launch (start us, length us, event | category | flops | bytes accessed | tf_op | source)
XLA Modules:
  0.0 109.1 jit_solution(3744039467659887644)
XLA Ops:
  0.6 0.0 copy-start
  0.6 0.0 copy-start.1
  0.7 2.8 %pack.1 = (bf16[2,128,672]{2,1,0:T(8,128)(2,1)}, bf16[2,128,672]{2,1,0:T(8,128)(2,1)}, bf16[2,128,672]{2,1,0:T(8,128)(2,1)}) custom-call(bf16[128,2688]{1,0:T(8,128)(2,1)} %bitcast.23, bf16[128,2688]{1,0:T(8,128)(2,1)} %bitcast.25), custom_call_target="tpu_custom_call" | custom-call | flops 1000000000 | tf_op jit(solution)/shard_map/pack/pallas_call | solution.py:318
  3.5 0.6 fusion.2
  4.1 0.1 collective-permute-start.3
  4.2 1.1 %collective-permute-start = (bf16[2,128,672]{2,1,0:T(8,128)(2,1)}, bf16[2,128,672]{2,1,0:T(8,128)(2,1)S(1)}, u32[]{:S(2)}, u32[]{:S(2)}) collective-permute-start(bf16[2,128,672]{2,1,0:T(8,128)(2,1)} %get-tuple-element.50), channel_id=1, source_target_pairs={{0,2},{2,0},{4,6},{6,4},{1,3},{3,1},{5,7},{7,5},{8,10},{10,8},{12,... | collective-permute-start | bytes 1032200 | tf_op jit(solution)/shard_map/ppermute | solution.py:280
  5.3 1.7 %collective-permute-start.1 = (bf16[2,128,672]{2,1,0:T(8,128)(2,1)}, bf16[2,128,672]{2,1,0:T(8,128)(2,1)S(1)}, u32[]{:S(2)}, u32[]{:S(2)}) collective-permute-start(bf16[2,128,672]{2,1,0:T(8,128)(2,1)} %get-tuple-element.51), channel_id=1, source_target_pairs={{0,4},{2,6},{4,0},{6,2},{1,5},{3,7},{5,1},{7,3},{8,12},{10,14},{12... | collective-permute-start | bytes 1032200 | tf_op jit(solution)/shard_map/ppermute | solution.py:280
  7.0 0.8 collective-permute-start.2
  7.8 1.1 collective-permute-start.5
  8.9 5.6 %collective-permute-start.4 = (bf16[2,84,256]{2,1,0:T(8,128)(2,1)S(1)}, bf16[2,84,256]{2,1,0:T(8,128)(2,1)S(1)}, u32[]{:S(2)}, u32[]{:S(2)}) collective-permute-start(bf16[2,84,256]{2,1,0:T(8,128)(2,1)S(1)} %pad_maximum_fusion), channel_id=1, source_target_pairs={{0,0},{1,17},{2,8},{3,25},{4,16},{5,1},{6,24},{7,9},{8,2},{9,19},{... | collective-permute-start | bytes 258056 | tf_op jit(solution)/shard_map/ppermute | solution.py:300
  14.5 0.1 pad_add_fusion.place
  14.6 0.8 collective-permute-done.5.m1
  15.5 14.8 %collective-permute-start.7 = (bf16[2,84,256]{2,1,0:T(8,128)(2,1)S(1)}, bf16[2,84,256]{2,1,0:T(8,128)(2,1)S(1)}, u32[]{:S(2)}, u32[]{:S(2)}) collective-permute-start(bf16[2,84,256]{2,1,0:T(8,128)(2,1)S(1)} %collective-permute-done.5.m1), channel_id=1, source_target_pairs={{0,1},{1,0},{2,3},{3,2},{4,5},{5,4},{6,7},{7,6},{8,9},{9,8},{10,11... | collective-permute-start | bytes 258056 | tf_op jit(solution)/shard_map/ppermute | solution.py:288
  30.2 0.9 collective-permute-start.6
  31.2 1.3 %copy-done.3 = bf16[1,256,2688]{2,1,0:T(8,128)(2,1)S(1)} copy-done((bf16[1,256,2688]{2,1,0:T(8,128)(2,1)S(1)}, bf16[1,256,2688]{2,1,0:T(8,128)(2,1)}, u32[]{:S(2)}) %copy-start.3) | copy-done | bytes 1376280
  32.5 1.1 %copy-done.4 = bf16[1,128,2688]{2,1,0:T(8,128)(2,1)S(1)} copy-done((bf16[1,128,2688]{2,1,0:T(8,128)(2,1)S(1)}, bf16[1,128,2688]{2,1,0:T(8,128)(2,1)}, u32[]{:S(2)}) %copy-start.4) | copy-done | bytes 688152
  33.6 1.1 %copy-done.5 = bf16[1,128,2688]{2,1,0:T(8,128)(2,1)S(1)} copy-done((bf16[1,128,2688]{2,1,0:T(8,128)(2,1)S(1)}, bf16[1,128,2688]{2,1,0:T(8,128)(2,1)}, u32[]{:S(2)}) %copy-start.5) | copy-done | bytes 688152
  34.7 0.8 own.1
  35.5 0.0 copy-start.6
  35.6 0.6 join.1.d_ref
  36.3 4.6 %forward.1 = (f32[12,84,256]{2,1,0:T(8,128)S(1)}, bf16[12,84,256]{2,1,0:T(8,128)(2,1)S(1)}, f32[3,8,256]{2,1,0:T(8,128)S(1)}) custom-call(s32[4]{0:T(128)S(1)} %pad_add_fusion.place, s32[1,256]{1,0:T(1,128)S(1)} %bitcast.27, bf16[256,672]{1,0:T(8,128)(2,1)S(1)} %get-tuple-element.45.q_ref, bf16[2,128,672]{2,1,0:T(8,128)(2,1)S(1)} %get-tuple-element.46.s0, ...), custom_call_target="tpu_custom_call" | custom-call | flops 2000000000 | tf_op jit(solution)/shard_map/forward/pallas_call | solution.py:339
  40.9 0.1 collective-permute-start.8
  41.0 0.5 collective-permute-start.9
  41.5 1.5 %collective-permute-done.9.got_stats_ref = f32[3,8,256]{2,1,0:T(8,128)S(1)} collective-permute-done((f32[3,8,256]{2,1,0:T(8,128)S(1)}, f32[3,8,256]{2,1,0:T(8,128)S(1)}, u32[]{:S(2)}, u32[]{:S(2)}) %collective-permute-start.9) | collective-permute-done | bytes 24608 | tf_op jit(solution)/shard_map/ppermute | solution.py:288
  42.9 1.0 core.1
  43.9 1.5 %collective-permute-start.10 = (bf16[304,256]{1,0:T(8,128)(2,1)S(1)}, bf16[304,256]{1,0:T(8,128)(2,1)S(1)}, u32[]{:S(2)}, u32[]{:S(2)}) collective-permute-start(bf16[304,256]{1,0:T(8,128)(2,1)S(1)} %get-tuple-element.58), channel_id=1, source_target_pairs={{0,8},{8,0},{16,24},{24,16},{1,9},{9,1},{17,25},{25,17},{2,10},{10... | collective-permute-start | bytes 466952 | tf_op jit(solution)/shard_map/ppermute | solution.py:284
  45.4 6.1 %collective-permute-start.11 = (bf16[304,256]{1,0:T(8,128)(2,1)S(1)}, bf16[304,256]{1,0:T(8,128)(2,1)S(1)}, u32[]{:S(2)}, u32[]{:S(2)}) collective-permute-start(bf16[304,256]{1,0:T(8,128)(2,1)S(1)} %get-tuple-element.59), channel_id=1, source_target_pairs={{0,16},{8,24},{16,0},{24,8},{1,17},{9,25},{17,1},{25,9},{2,18},{10... | collective-permute-start | bytes 466952 | tf_op jit(solution)/shard_map/ppermute | solution.py:284
  51.5 10.8 %collective-permute-done.11.p2 = bf16[304,256]{1,0:T(8,128)(2,1)S(1)} collective-permute-done((bf16[304,256]{1,0:T(8,128)(2,1)S(1)}, bf16[304,256]{1,0:T(8,128)(2,1)S(1)}, u32[]{:S(2)}, u32[]{:S(2)}) %collective-permute-start.11) | collective-permute-done | bytes 155680 | tf_op jit(solution)/shard_map/ppermute | solution.py:284
  62.3 2.2 %collective-permute-done.12.p3 = bf16[304,256]{1,0:T(8,128)(2,1)S(1)} collective-permute-done((bf16[304,256]{1,0:T(8,128)(2,1)S(1)}, bf16[304,256]{1,0:T(8,128)(2,1)S(1)}, u32[]{:S(2)}, u32[]{:S(2)}) %collective-permute-start.12) | collective-permute-done | bytes 155680 | tf_op jit(solution)/shard_map/ppermute | solution.py:284
  64.5 0.7 finish.1
  65.2 0.0 copy-start.2
  65.2 6.1 %collective-permute-start.13 = (bf16[2,84,256]{2,1,0:T(8,128)(2,1)S(1)}, bf16[2,84,256]{2,1,0:T(8,128)(2,1)S(1)}, u32[]{:S(2)}, u32[]{:S(2)}) collective-permute-start(bf16[2,84,256]{2,1,0:T(8,128)(2,1)S(1)} %finish.1), channel_id=1, source_target_pairs={{0,0},{2,8},{4,16},{6,24},{8,2},{10,10},{12,18},{14,26},{16,4},{18... | collective-permute-start | bytes 258056 | tf_op jit(solution)/shard_map/ppermute | solution.py:295
  71.4 3.9 %backward.1 = (bf16[2,128,672]{2,1,0:T(8,128)(2,1)S(1)}, bf16[2,128,672]{2,1,0:T(8,128)(2,1)}, bf16[2,128,672]{2,1,0:T(8,128)(2,1)}, bf16[2,128,672]{2,1,0:T(8,128)(2,1)S(1)}) custom-call(s32[4]{0:T(128)S(1)} %pad_add_fusion.place, s32[1,256]{1,0:T(1,128)S(1)} %bitcast.28, bf16[256,672]{1,0:T(8,128)(2,1)S(1)} %get-tuple-element.45.q_ref, ...), custom_call_target="tpu_custom_call" | custom-call | flops 3000000000 | tf_op jit(solution)/shard_map/backward/pallas_call | solution.py:359
  75.3 0.4 collective-permute-done.13.rows_ref
  75.7 2.7 %collective-permute-start.15 = (bf16[2,128,672]{2,1,0:T(8,128)(2,1)}, bf16[2,128,672]{2,1,0:T(8,128)(2,1)S(1)}, u32[]{:S(2)}, u32[]{:S(2)}) collective-permute-start(bf16[2,128,672]{2,1,0:T(8,128)(2,1)} %get-tuple-element.75), channel_id=1, source_target_pairs={{0,4},{2,6},{4,0},{6,2},{1,5},{3,7},{5,1},{7,3},{8,12},{10,14},{12... | collective-permute-start | bytes 1032200 | tf_op jit(solution)/shard_map/ppermute | solution.py:280
  78.5 1.5 %collective-permute-start.16 = (bf16[2,128,672]{2,1,0:T(8,128)(2,1)S(1)}, bf16[2,128,672]{2,1,0:T(8,128)(2,1)}, u32[]{:S(2)}, u32[]{:S(2)}) collective-permute-start(bf16[2,128,672]{2,1,0:T(8,128)(2,1)S(1)} %get-tuple-element.76), channel_id=1, source_target_pairs={{0,6},{2,4},{4,2},{6,0},{1,7},{3,5},{5,3},{7,1},{8,14},{10,12},{12... | collective-permute-start | bytes 1032200 | tf_op jit(solution)/shard_map/ppermute | solution.py:280
  79.9 2.0 %weight.1 = (bf16[8,84,660]{2,1,0:T(8,128)(2,1)}, bf16[84,256]{1,0:T(8,128)(2,1)}) custom-call(bf16[2,84,256]{2,1,0:T(8,128)(2,1)S(1)} %collective-permute-done.13.rows_ref, bf16[5280,256]{1,0:T(8,128)(2,1)S(1)} %bitcast.21), custom_call_target="tpu_custom_call" | custom-call | flops 2000000000 | tf_op jit(solution)/shard_map/weight/pallas_call | solution.py:366
  82.0 4.5 %all-to-all-start = ((bf16[8,84,660]{2,1,0:T(8,128)(2,1)}), bf16[8,84,660]{2,1,0:T(8,128)(2,1)S(1)}, u32[]{:S(2)}, u32[]{:S(2)}) async-start(bf16[8,84,660]{2,1,0:T(8,128)(2,1)} %get-tuple-element.72), calls=%async_computation | async-start | bytes 2162688 | tf_op jit(solution)/shard_map/all_to_all | solution.py:375
  86.4 2.3 %collective-permute-done.15.s2 = bf16[2,128,672]{2,1,0:T(8,128)(2,1)S(1)} collective-permute-done((bf16[2,128,672]{2,1,0:T(8,128)(2,1)}, bf16[2,128,672]{2,1,0:T(8,128)(2,1)S(1)}, u32[]{:S(2)}, u32[]{:S(2)}) %collective-permute-start.15) | collective-permute-done | bytes 344096 | tf_op jit(solution)/shard_map/ppermute | solution.py:280
  88.7 8.1 %collective-permute-done.16.s3 = bf16[2,128,672]{2,1,0:T(8,128)(2,1)} collective-permute-done((bf16[2,128,672]{2,1,0:T(8,128)(2,1)S(1)}, bf16[2,128,672]{2,1,0:T(8,128)(2,1)}, u32[]{:S(2)}, u32[]{:S(2)}) %collective-permute-start.16) | collective-permute-done | bytes 344096 | tf_op jit(solution)/shard_map/ppermute | solution.py:280
  96.8 1.0 copy-done.8
  97.8 3.2 %unpack_k.1 = bf16[128,2688]{1,0:T(8,128)(2,1)} custom-call(s32[4]{0:T(128)S(1)} %pad_add_fusion.place, bf16[2,128,672]{2,1,0:T(8,128)(2,1)S(1)} %copy-done.8, bf16[2,128,672]{2,1,0:T(8,128)(2,1)S(1)} %collective-permute-done.14.s1, bf16[2,128,672]{2,1,0:T(8,128)(2,1)S(1)} %collective-permute-done.15.s2, bf16[2,128,672]{2,1,0:T(8,128)(2,1)} %collective-permute-done.16.s3), custom_call_target="tpu_custom_call" | custom-call | flops 10000000000 | tf_op jit(solution)/shard_map/unpack_k/pallas_call | solution.py:381
  101.1 0.7 sum_y.1
  101.8 1.2 %collective-permute-start.17 = (bf16[84,660]{1,0:T(8,128)(2,1)S(1)}, bf16[84,660]{1,0:T(8,128)(2,1)S(1)}, u32[]{:S(2)}, u32[]{:S(2)}) collective-permute-start(bf16[84,660]{1,0:T(8,128)(2,1)S(1)} %get-tuple-element.85), channel_id=1, source_target_pairs={{0,128},{128,0},{1,129},{129,1},{2,130},{130,2},{3,131},{131,3},{4... | collective-permute-start | bytes 332648 | tf_op jit(solution)/shard_map/ppermute | solution.py:388
  103.0 1.0 copy-done.9
  104.0 3.2 %unpack_v.1 = bf16[128,2688]{1,0:T(8,128)(2,1)} custom-call(s32[4]{0:T(128)S(1)} %pad_add_fusion.place, bf16[2,128,672]{2,1,0:T(8,128)(2,1)S(1)} %copy-done.9, bf16[2,128,672]{2,1,0:T(8,128)(2,1)S(1)} %collective-permute-done.14.s1, bf16[2,128,672]{2,1,0:T(8,128)(2,1)S(1)} %collective-permute-done.15.s2, bf16[2,128,672]{2,1,0:T(8,128)(2,1)} %collective-permute-done.16.s3), custom_call_target="tpu_custom_call" | custom-call | flops 3000000000 | tf_op jit(solution)/shard_map/unpack_v/pallas_call | solution.py:381
  107.2 1.2 %collective-permute-done.17.got_ref = bf16[84,660]{1,0:T(8,128)(2,1)S(1)} collective-permute-done((bf16[84,660]{1,0:T(8,128)(2,1)S(1)}, bf16[84,660]{1,0:T(8,128)(2,1)S(1)}, u32[]{:S(2)}, u32[]{:S(2)}) %collective-permute-start.17) | collective-permute-done | bytes 110912 | tf_op jit(solution)/shard_map/ppermute | solution.py:388
  108.4 0.7 sum.1
  (27 shorter events, 0.1 us)
Async XLA Ops:
  0.6 2.9 %copy-start = (bf16[84,5280]{1,0:T(8,128)(2,1)S(1)}, bf16[84,5280]{1,0:T(8,128)(2,1)}, u32[]{:S(2)}) copy-start(bf16[84,5280]{1,0:T(8,128)(2,1)} %param.10) | copy-start | bytes 2661124
  0.6 2.9 %copy-start.1 = (bf16[1,256,5280]{1,2,0:T(8,128)(2,1)S(1)}, bf16[1,256,5280]{1,2,0:T(8,128)(2,1)}, u32[]{:S(2)}) copy-start(bf16[1,256,5280]{1,2,0:T(8,128)(2,1)} %param.9) | copy-start | bytes 8110084
  3.5 3.5 %copy-start.10 = (bf16[2,128,672]{2,1,0:T(8,128)(2,1)S(1)}, bf16[2,128,672]{2,1,0:T(8,128)(2,1)}, u32[]{:S(2)}) copy-start(bf16[2,128,672]{2,1,0:T(8,128)(2,1)} %get-tuple-element.52) | copy-start | bytes 1032196
  4.1 3.7 %collective-permute-start.3 = (bf16[84,256]{1,0:T(8,128)(2,1)S(1)}, bf16[84,256]{1,0:T(8,128)(2,1)S(1)}, u32[]{:S(2)}, u32[]{:S(2)}) collective-permute-start(bf16[84,256]{1,0:T(8,128)(2,1)S(1)} %fusion.2), channel_id=1, source_target_pairs={{0,1},{1,0},{2,3},{3,2},{4,5},{5,4},{6,7},{7,6},{8,9},{9,8},{10,11... | collective-permute-start | bytes 129032 | tf_op jit(solution)/shard_map/ppermute | solution.py:288
  4.2 32.0 %collective-permute-start = (bf16[2,128,672]{2,1,0:T(8,128)(2,1)}, bf16[2,128,672]{2,1,0:T(8,128)(2,1)S(1)}, u32[]{:S(2)}, u32[]{:S(2)}) collective-permute-start(bf16[2,128,672]{2,1,0:T(8,128)(2,1)} %get-tuple-element.50), channel_id=1, source_target_pairs={{0,2},{2,0},{4,6},{6,4},{1,3},{3,1},{5,7},{7,5},{8,10},{10,8},{12,... | collective-permute-start | bytes 1032200 | tf_op jit(solution)/shard_map/ppermute | solution.py:280
  5.3 30.9 %collective-permute-start.1 = (bf16[2,128,672]{2,1,0:T(8,128)(2,1)}, bf16[2,128,672]{2,1,0:T(8,128)(2,1)S(1)}, u32[]{:S(2)}, u32[]{:S(2)}) collective-permute-start(bf16[2,128,672]{2,1,0:T(8,128)(2,1)} %get-tuple-element.51), channel_id=1, source_target_pairs={{0,4},{2,6},{4,0},{6,2},{1,5},{3,7},{5,1},{7,3},{8,12},{10,14},{12... | collective-permute-start | bytes 1032200 | tf_op jit(solution)/shard_map/ppermute | solution.py:280
  7.0 29.2 %collective-permute-start.2 = (bf16[2,128,672]{2,1,0:T(8,128)(2,1)S(1)}, bf16[2,128,672]{2,1,0:T(8,128)(2,1)S(1)}, u32[]{:S(2)}, u32[]{:S(2)}) collective-permute-start(bf16[2,128,672]{2,1,0:T(8,128)(2,1)S(1)} %copy-done.10), channel_id=1, source_target_pairs={{0,6},{2,4},{4,2},{6,0},{1,7},{3,5},{5,3},{7,1},{8,14},{10,12},{12... | collective-permute-start | bytes 1032200 | tf_op jit(solution)/shard_map/ppermute | solution.py:280
  7.8 7.6 %collective-permute-start.5 = (bf16[2,84,256]{2,1,0:T(8,128)(2,1)S(1)}, bf16[2,84,256]{2,1,0:T(8,128)(2,1)S(1)}, u32[]{:S(2)}, u32[]{:S(2)}) collective-permute-start(bf16[2,84,256]{2,1,0:T(8,128)(2,1)S(1)} %pad_maximum_fusion), channel_id=1, source_target_pairs={{0,8},{1,25},{2,0},{3,17},{4,24},{5,9},{6,16},{7,1},{8,10},{9,27},... | collective-permute-start | bytes 258056 | tf_op jit(solution)/shard_map/ppermute | solution.py:300
  8.9 21.3 %collective-permute-start.4 = (bf16[2,84,256]{2,1,0:T(8,128)(2,1)S(1)}, bf16[2,84,256]{2,1,0:T(8,128)(2,1)S(1)}, u32[]{:S(2)}, u32[]{:S(2)}) collective-permute-start(bf16[2,84,256]{2,1,0:T(8,128)(2,1)S(1)} %pad_maximum_fusion), channel_id=1, source_target_pairs={{0,0},{1,17},{2,8},{3,25},{4,16},{5,1},{6,24},{7,9},{8,2},{9,19},{... | collective-permute-start | bytes 258056 | tf_op jit(solution)/shard_map/ppermute | solution.py:300
  15.5 20.1 %collective-permute-start.7 = (bf16[2,84,256]{2,1,0:T(8,128)(2,1)S(1)}, bf16[2,84,256]{2,1,0:T(8,128)(2,1)S(1)}, u32[]{:S(2)}, u32[]{:S(2)}) collective-permute-start(bf16[2,84,256]{2,1,0:T(8,128)(2,1)S(1)} %collective-permute-done.5.m1), channel_id=1, source_target_pairs={{0,1},{1,0},{2,3},{3,2},{4,5},{5,4},{6,7},{7,6},{8,9},{9,8},{10,11... | collective-permute-start | bytes 258056 | tf_op jit(solution)/shard_map/ppermute | solution.py:288
  30.2 5.3 %collective-permute-start.6 = (bf16[2,84,256]{2,1,0:T(8,128)(2,1)S(1)}, bf16[2,84,256]{2,1,0:T(8,128)(2,1)S(1)}, u32[]{:S(2)}, u32[]{:S(2)}) collective-permute-start(bf16[2,84,256]{2,1,0:T(8,128)(2,1)S(1)} %collective-permute-done.4.m0), channel_id=1, source_target_pairs={{0,1},{1,0},{2,3},{3,2},{4,5},{5,4},{6,7},{7,6},{8,9},{9,8},{10,11... | collective-permute-start | bytes 258056 | tf_op jit(solution)/shard_map/ppermute | solution.py:288
  31.2 1.3 %copy-start.3 = (bf16[1,256,2688]{2,1,0:T(8,128)(2,1)S(1)}, bf16[1,256,2688]{2,1,0:T(8,128)(2,1)}, u32[]{:S(2)}) copy-start(bf16[1,256,2688]{2,1,0:T(8,128)(2,1)} %param.6) | copy-start | bytes 4128772
  32.5 1.1 %copy-start.4 = (bf16[1,128,2688]{2,1,0:T(8,128)(2,1)S(1)}, bf16[1,128,2688]{2,1,0:T(8,128)(2,1)}, u32[]{:S(2)}) copy-start(bf16[1,128,2688]{2,1,0:T(8,128)(2,1)} %param.7) | copy-start | bytes 2064388
  33.6 1.1 %copy-start.5 = (bf16[1,128,2688]{2,1,0:T(8,128)(2,1)S(1)}, bf16[1,128,2688]{2,1,0:T(8,128)(2,1)}, u32[]{:S(2)}) copy-start(bf16[1,128,2688]{2,1,0:T(8,128)(2,1)} %param.8) | copy-start | bytes 2064388
  35.5 0.7 copy-start.6
  40.9 2.1 %collective-permute-start.8 = (bf16[12,84,256]{2,1,0:T(8,128)(2,1)S(1)}, bf16[12,84,256]{2,1,0:T(8,128)(2,1)S(1)}, u32[]{:S(2)}, u32[]{:S(2)}) collective-permute-start(bf16[12,84,256]{2,1,0:T(8,128)(2,1)S(1)} %get-tuple-element.56), channel_id=1, source_target_pairs={{0,1},{1,0},{2,3},{3,2},{4,5},{5,4},{6,7},{7,6},{8,9},{9,8},{10,11... | collective-permute-start | bytes 1548296 | tf_op jit(solution)/shard_map/ppermute | solution.py:288
  41.0 2.0 %collective-permute-start.9 = (f32[3,8,256]{2,1,0:T(8,128)S(1)}, f32[3,8,256]{2,1,0:T(8,128)S(1)}, u32[]{:S(2)}, u32[]{:S(2)}) collective-permute-start(f32[3,8,256]{2,1,0:T(8,128)S(1)} %get-tuple-element.55.stats_ref), channel_id=1, source_target_pairs={{0,1},{1,0},{2,3},{3,2},{4,5},{5,4},{6,7},{7,6},{8,9},{9,8},{10,11... | collective-permute-start | bytes 73736 | tf_op jit(solution)/shard_map/ppermute | solution.py:288
  43.9 7.6 %collective-permute-start.10 = (bf16[304,256]{1,0:T(8,128)(2,1)S(1)}, bf16[304,256]{1,0:T(8,128)(2,1)S(1)}, u32[]{:S(2)}, u32[]{:S(2)}) collective-permute-start(bf16[304,256]{1,0:T(8,128)(2,1)S(1)} %get-tuple-element.58), channel_id=1, source_target_pairs={{0,8},{8,0},{16,24},{24,16},{1,9},{9,1},{17,25},{25,17},{2,10},{10... | collective-permute-start | bytes 466952 | tf_op jit(solution)/shard_map/ppermute | solution.py:284
  45.4 16.9 %collective-permute-start.11 = (bf16[304,256]{1,0:T(8,128)(2,1)S(1)}, bf16[304,256]{1,0:T(8,128)(2,1)S(1)}, u32[]{:S(2)}, u32[]{:S(2)}) collective-permute-start(bf16[304,256]{1,0:T(8,128)(2,1)S(1)} %get-tuple-element.59), channel_id=1, source_target_pairs={{0,16},{8,24},{16,0},{24,8},{1,17},{9,25},{17,1},{25,9},{2,18},{10... | collective-permute-start | bytes 466952 | tf_op jit(solution)/shard_map/ppermute | solution.py:284
  51.5 13.0 %collective-permute-start.12 = (bf16[304,256]{1,0:T(8,128)(2,1)S(1)}, bf16[304,256]{1,0:T(8,128)(2,1)S(1)}, u32[]{:S(2)}, u32[]{:S(2)}) collective-permute-start(bf16[304,256]{1,0:T(8,128)(2,1)S(1)} %get-tuple-element.60), channel_id=1, source_target_pairs={{0,24},{8,16},{16,8},{24,0},{1,25},{9,17},{17,9},{25,1},{2,26},{10... | collective-permute-start | bytes 466952 | tf_op jit(solution)/shard_map/ppermute | solution.py:284
  65.2 14.7 %copy-start.2 = (bf16[1,256,5280]{1,2,0:T(8,128)(2,1)S(1)}, bf16[1,256,5280]{1,2,0:T(8,128)(2,1)}, u32[]{:S(2)}) copy-start(bf16[1,256,5280]{1,2,0:T(8,128)(2,1)} %param.9) | copy-start | bytes 8110084
  65.2 10.5 %collective-permute-start.13 = (bf16[2,84,256]{2,1,0:T(8,128)(2,1)S(1)}, bf16[2,84,256]{2,1,0:T(8,128)(2,1)S(1)}, u32[]{:S(2)}, u32[]{:S(2)}) collective-permute-start(bf16[2,84,256]{2,1,0:T(8,128)(2,1)S(1)} %finish.1), channel_id=1, source_target_pairs={{0,0},{2,8},{4,16},{6,24},{8,2},{10,10},{12,18},{14,26},{16,4},{18... | collective-permute-start | bytes 258056 | tf_op jit(solution)/shard_map/ppermute | solution.py:295
  75.3 6.6 %copy-start.7 = (bf16[2,128,672]{2,1,0:T(8,128)(2,1)}, bf16[2,128,672]{2,1,0:T(8,128)(2,1)S(1)}, u32[]{:S(2)}) copy-start(bf16[2,128,672]{2,1,0:T(8,128)(2,1)S(1)} %get-tuple-element.80.s0) | copy-start | bytes 1032196
  75.7 10.7 %collective-permute-start.14 = (bf16[2,128,672]{2,1,0:T(8,128)(2,1)}, bf16[2,128,672]{2,1,0:T(8,128)(2,1)S(1)}, u32[]{:S(2)}, u32[]{:S(2)}) collective-permute-start(bf16[2,128,672]{2,1,0:T(8,128)(2,1)} %get-tuple-element.74), channel_id=1, source_target_pairs={{0,2},{2,0},{4,6},{6,4},{1,3},{3,1},{5,7},{7,5},{8,10},{10,8},{12,... | collective-permute-start | bytes 1032200 | tf_op jit(solution)/shard_map/ppermute | solution.py:280
  75.7 13.0 %collective-permute-start.15 = (bf16[2,128,672]{2,1,0:T(8,128)(2,1)}, bf16[2,128,672]{2,1,0:T(8,128)(2,1)S(1)}, u32[]{:S(2)}, u32[]{:S(2)}) collective-permute-start(bf16[2,128,672]{2,1,0:T(8,128)(2,1)} %get-tuple-element.75), channel_id=1, source_target_pairs={{0,4},{2,6},{4,0},{6,2},{1,5},{3,7},{5,1},{7,3},{8,12},{10,14},{12... | collective-permute-start | bytes 1032200 | tf_op jit(solution)/shard_map/ppermute | solution.py:280
  78.5 18.4 %collective-permute-start.16 = (bf16[2,128,672]{2,1,0:T(8,128)(2,1)S(1)}, bf16[2,128,672]{2,1,0:T(8,128)(2,1)}, u32[]{:S(2)}, u32[]{:S(2)}) collective-permute-start(bf16[2,128,672]{2,1,0:T(8,128)(2,1)S(1)} %get-tuple-element.76), channel_id=1, source_target_pairs={{0,6},{2,4},{4,2},{6,0},{1,7},{3,5},{5,3},{7,1},{8,14},{10,12},{12... | collective-permute-start | bytes 1032200 | tf_op jit(solution)/shard_map/ppermute | solution.py:280
  82.0 19.1 %all-to-all-start = ((bf16[8,84,660]{2,1,0:T(8,128)(2,1)}), bf16[8,84,660]{2,1,0:T(8,128)(2,1)S(1)}, u32[]{:S(2)}, u32[]{:S(2)}) async-start(bf16[8,84,660]{2,1,0:T(8,128)(2,1)} %get-tuple-element.72), calls=%async_computation | async-start | bytes 2162688 | tf_op jit(solution)/shard_map/all_to_all | solution.py:375
  96.8 1.0 copy-start.8
  101.8 6.6 %collective-permute-start.17 = (bf16[84,660]{1,0:T(8,128)(2,1)S(1)}, bf16[84,660]{1,0:T(8,128)(2,1)S(1)}, u32[]{:S(2)}, u32[]{:S(2)}) collective-permute-start(bf16[84,660]{1,0:T(8,128)(2,1)S(1)} %get-tuple-element.85), channel_id=1, source_target_pairs={{0,128},{128,0},{1,129},{129,1},{2,130},{130,2},{3,131},{131,3},{4... | collective-permute-start | bytes 332648 | tf_op jit(solution)/shard_map/ppermute | solution.py:388
  103.0 1.0 copy-start.9
